TPU v7x, 32 devices: a whole 2x2x4 slice. The times are simulated.
32 devices in a mesh: dp: 2 (over x), expert: 16 (over z, y, core).
Axes of the slice: x: 2, y: 2, z: 4, core: 2. Of those that a mesh axis runs over, the one named last changes fastest.
Arguments:
- tokens: bfloat16 [4096, 2048], P(('dp', 'expert')), may hold values from -6 to 6
- out_grad: bfloat16 [4096, 2048], P(('dp', 'expert')), may hold values from -3 to 3
- expert_ids: int32 [4096, 1], P(('dp', 'expert')), may hold values from 0 to 15, as said below
- gates: float32 [4096, 1], P(('dp', 'expert')), may hold values from 0.1 to 1
- w_gate: bfloat16 [16, 2048, 384], P('expert', 'dp'), may hold values from -0.125 to 0.125
- w_up: bfloat16 [16, 2048, 384], P('expert', 'dp'), may hold values from -0.125 to 0.125
- w_down: bfloat16 [16, 384, 2048], P('expert', None, 'dp'), may hold values from -0.3125 to 0.3125
Outputs:
- input_grad: bfloat16 [4096, 2048], P(('dp', 'expert'))
- gate_grad: bfloat16 [16, 2048, 384], P('expert', 'dp')
- up_grad: bfloat16 [16, 2048, 384], P('expert', 'dp')
- down_grad: bfloat16 [16, 384, 2048], P('expert')
Inputs may be any that keep to these rules, and one draw needn't show every extreme that they name: `expert_ids`: among the rows of one device no expert is named more than 24 times; 1 expert, the same ones for every device, are named exactly 24 times by every device.
All inputs are finite; a program needn't handle non-finite values.
Results may differ from a plain program's by a relative error of at most 0.013.
Values may be sent and summed in bfloat16 or wider, within the bound.
No kernel may reach another device: no remote copies, remote signals or barrier semaphores. Data moves between devices by JAX's collectives and lax.ppermute only.
A program may use at most 64 MiB of HBM per device.

v0:
```python
import jax
import jax.numpy as jnp
from jax import lax
from jax.sharding import PartitionSpec as P


def on_device(tokens, out_grad, expert_ids, gates, w_gate, w_up, w_down):
    expert_count = lax.axis_size("expert")
    tok_rows = tokens.shape[0]
    model_width = tokens.shape[1]
    per_token = expert_ids.shape[1]
    hidden = w_gate.shape[2]
    entries = tok_rows * per_token
    slot_depth = 3 * entries // expert_count
    slot_count = expert_count * slot_depth
    flat_ids = expert_ids.reshape(entries)
    onehot = (flat_ids[:, None] == jnp.arange(expert_count, dtype=jnp.int32)[None, :]).astype(
        jnp.int32
    )
    before = jnp.cumsum(onehot, axis=0) - onehot
    ranking = jnp.sum(before * onehot, axis=1)
    slot_of_entry = flat_ids * slot_depth + ranking
    source = (
        jnp.full((slot_count,), entries, jnp.int32)
        .at[slot_of_entry]
        .set(jnp.arange(entries, dtype=jnp.int32))
    )
    entry_scaled = (
        (gates[:, :, None] * out_grad.astype(jnp.float32)[:, None, :])
        .astype(jnp.bfloat16)
        .reshape(entries, model_width)
    )
    grad_table = jnp.concatenate([entry_scaled, jnp.zeros((1, model_width), jnp.bfloat16)], axis=0)
    input_table = jnp.concatenate([tokens, jnp.zeros((1, model_width), tokens.dtype)], axis=0)
    send_grads = grad_table[source].reshape(expert_count, slot_depth, model_width)
    send_inputs = input_table[source // per_token].reshape(expert_count, slot_depth, model_width)
    recv_inputs, recv_grads = (
        lax.all_to_all(send_inputs, "expert", split_axis=0, concat_axis=0, tiled=True),
        lax.all_to_all(send_grads, "expert", split_axis=0, concat_axis=0, tiled=True),
    )
    rows_in = recv_inputs.reshape(slot_count, model_width)
    grads_in = recv_grads.reshape(slot_count, model_width)
    local_joined = jnp.concatenate([w_gate[0], w_up[0]], axis=1)
    full_joined, full_down = (
        lax.all_gather(local_joined, "dp", axis=0, tiled=True),
        lax.all_gather(w_down[0], "dp", axis=1, tiled=True),
    )
    preact = jnp.dot(rows_in, full_joined, preferred_element_type=jnp.float32)
    hidden_grad = lax.dot_general(
        grads_in, full_down, (((1,), (1,)), ((), ())), preferred_element_type=jnp.float32
    )
    gate_pre = preact[:, :hidden]
    up_pre = preact[:, hidden:]
    sigmoid = jax.nn.sigmoid(gate_pre)
    silu_value = gate_pre * sigmoid
    activated = (silu_value * up_pre).astype(jnp.bfloat16)
    gate_side = (hidden_grad * up_pre * sigmoid * (1.0 + gate_pre * (1.0 - sigmoid))).astype(
        jnp.bfloat16
    )
    up_side = (hidden_grad * silu_value).astype(jnp.bfloat16)
    both_sides = jnp.concatenate([gate_side, up_side], axis=1)
    slot_grad = lax.dot_general(
        both_sides, full_joined, (((1,), (1,)), ((), ())), preferred_element_type=jnp.float32
    )
    slot_grad = slot_grad.astype(jnp.bfloat16).reshape(expert_count, slot_depth, model_width)
    returned = lax.all_to_all(slot_grad, "expert", split_axis=0, concat_axis=0, tiled=True).reshape(
        slot_count, model_width
    )
    picked = returned[slot_of_entry].astype(jnp.float32).reshape(tok_rows, per_token, model_width)
    input_grad = jnp.sum(picked, axis=1).astype(jnp.bfloat16)
    down_part = lax.dot_general(
        activated, grads_in, (((0,), (0,)), ((), ())), preferred_element_type=jnp.float32
    )
    down_grad = lax.psum(down_part.astype(jnp.bfloat16), "dp")[None]
    joined_grad = lax.psum_scatter(
        lax.dot_general(
            rows_in, both_sides, (((0,), (0,)), ((), ())), preferred_element_type=jnp.float32
        ).astype(jnp.bfloat16),
        "dp",
        scatter_dimension=0,
        tiled=True,
    )
    gate_grad = joined_grad[:, :hidden][None]
    up_grad = joined_grad[:, hidden:][None]
    return (input_grad, gate_grad, up_grad, down_grad)


def solution(mesh):
    in_specs = (
        P(("dp", "expert"), None),
        P(("dp", "expert"), None),
        P(("dp", "expert"), None),
        P(("dp", "expert"), None),
        P("expert", "dp", None),
        P("expert", "dp", None),
        P("expert", None, "dp"),
    )
    out_specs = (
        P(("dp", "expert"), None),
        P("expert", "dp", None),
        P("expert", "dp", None),
        P("expert", None, None),
    )
    return jax.shard_map(
        on_device, mesh=mesh, in_specs=in_specs, out_specs=out_specs, check_vma=False
    )
```

profile of v0, /device:TPU:13, one launch (start us, length us, event | category | flops | bytes accessed | tf_op | source)
XLA Modules:
  0.0 211.9 jit_solution(15679344374222478198)
XLA Ops:
  7.2 0.7 fusion.5
  7.9 0.2 reduce_window_sum.11
  8.1 0.8 select_reduce_fusion
  8.9 0.7 fusion.8
  9.6 1.0 scatter_custom_fusion
  10.6 1.1 concatenate.13
  11.7 3.1 %gather_fusion.1 = bf16[384,2048]{1,0:T(8,128)(2,1)} fusion(bf16[129,2048]{1,0:T(8,128)(2,1)S(1)} %concatenate.13, s32[1024]{0:T(1024)S(1)} %pad_clamp_fusion.1), kind=kCustom, calls=%fused_computation.1 | custom fusion | bytes 3147264 | tf_op jit(solution)/shard_map/gather | solution.py:36
  14.8 0.0 copy-start
  14.8 0.0 copy-start.1
  14.8 6.7 %all-to-all-start.1 = ((bf16[16,24,2048]{2,1,0:T(8,128)(2,1)}), bf16[16,24,2048]{2,1,0:T(8,128)(2,1)S(1)}, u32[]{:S(2)}, u32[]{:S(2)}) async-start(bf16[16,24,2048]{2,1,0:T(8,128)(2,1)} %bitcast.7), calls=%async_computation.1 | async-start | bytes 3145728 | tf_op jit(solution)/shard_map/all_to_all | solution.py:38
  21.5 0.0 all-gather.4.cloned.1.call-start
  21.5 0.0 copy-done
  21.6 0.0 copy-done.1
  21.6 1.3 pad_maximum_fusion
  22.8 0.0 copy-start.2
  22.8 0.0 copy-start.3
  22.8 0.0 all-gather.4.cloned.1.call-update
  22.9 1.0 copy-done.2
  23.9 0.0 copy-done.3
  23.9 0.2 multiply_convert_fusion
  24.1 3.1 %gather_fusion = bf16[384,2048]{1,0:T(8,128)(2,1)} fusion(bf16[129,2048]{1,0:T(8,128)(2,1)S(1)} %concatenate.12, s32[1024]{0:T(1024)S(1)} %pad_clamp_fusion.1), kind=kCustom, calls=%fused_computation | custom fusion | bytes 3147264 | tf_op jit(solution)/shard_map/gather | solution.py:35
  27.2 30.9 %all-to-all-done.1 = bf16[16,24,2048]{2,1,0:T(8,128)(2,1)S(1)} async-done(((bf16[16,24,2048]{2,1,0:T(8,128)(2,1)}), bf16[16,24,2048]{2,1,0:T(8,128)(2,1)S(1)}, u32[]{:S(2)}, u32[]{:S(2)}) %all-to-all-start.1) | async-done | bytes 1572896 | tf_op jit(solution)/shard_map/all_to_all | solution.py:38
  58.1 4.5 %all-to-all-start = ((bf16[16,24,2048]{2,1,0:T(8,128)(2,1)}), bf16[16,24,2048]{2,1,0:T(8,128)(2,1)}, u32[]{:S(2)}, u32[]{:S(2)}) async-start(bf16[16,24,2048]{2,1,0:T(8,128)(2,1)} %bitcast.4), calls=%async_computation | async-start | bytes 3145728 | tf_op jit(solution)/shard_map/all_to_all | solution.py:39
  62.6 0.0 all-gather.6.cloned.1.call-start
  62.6 0.7 all-gather.6.cloned.1.call-update
  63.3 0.0 reduce-scatter.2.cloned.1.call-start
  63.4 6.6 %all-gather.4.cloned.1.call-done = bf16[2048,768]{1,0:T(8,128)(2,1)} async-done(((bf16[1024,768]{1,0:T(8,128)(2,1)}), bf16[2048,768]{1,0:T(8,128)(2,1)}) %all-gather.4.cloned.1.call-update) | async-done | bytes 3145744 | tf_op jit(solution)/shard_map/all_gather | solution.py:45
  70.0 3.7 %fusion.12 = f32[384,768]{0,1:T(8,128)S(1)} fusion(bf16[384,2048]{1,0:T(8,128)(2,1)S(1)} %bitcast.34, bf16[2048,768]{1,0:T(8,128)(2,1)} %all-gather.4.cloned.1.call-done), kind=kOutput, calls=%fused_computation.34 | convolution fusion | flops 1207959552 | bytes 5898240 | tf_op jit(solution)/shard_map/dot_general | solution.py:48
  73.7 0.0 copy-start.5
  73.7 25.1 %all-gather.6.cloned.1.call-done = bf16[1,384,2048]{2,1,0:T(8,128)(2,1)} async-done(((bf16[1,384,1024]{2,1,0:T(8,128)(2,1)}), bf16[1,384,2048]{2,1,0:T(8,128)(2,1)}) %all-gather.6.cloned.1.call-update) | async-done | bytes 1572880 | tf_op jit(solution)/shard_map/all_gather | solution.py:46
  98.8 0.2 all-to-all-done
  99.0 3.0 %multiply_convert_fusion.3 = (bf16[384,384]{0,1:T(8,128)(2,1)S(1)}, bf16[384,384]{0,1:T(8,128)(2,1)S(1)}) fusion(f32[384,768]{0,1:T(8,128)S(1)} %fusion.12, bf16[384,2048]{1,0:T(8,128)(2,1)} %bitcast.5, bf16[1,384,2048]{2,1,0:T(8,128)(2,1)} %all-gather.6.cloned.1.call-done), kind=kOutput, calls=%fused_computation.17 | convolution fusion | flops 605896704 | bytes 4915200 | tf_op jit(solution)/shard_map/dot_general | solution.py:49
  102.0 0.0 copy-done.5
  102.0 0.0 copy-start.7
  102.0 3.5 %convolution_convert_fusion = bf16[2048,768]{1,0:T(8,128)(2,1)} fusion(bf16[384,2048]{1,0:T(8,128)(2,1)S(1)} %bitcast.35, bf16[384,384]{0,1:T(8,128)(2,1)S(1)} %get-tuple-element.5, bf16[384,384]{0,1:T(8,128)(2,1)S(1)} %get-tuple-element.4), kind=kOutput, calls=%fused_computation.4 | convolution fusion | flops 1210712064 | bytes 5308416 | tf_op jit(solution)/shard_map/dot_general | solution.py:76
  105.5 0.0 copy-done.7
  105.5 0.0 copy-start.4
  105.5 0.0 reduce-scatter.2.cloned.1.call-update
  105.5 1.9 copy-done.4
  107.4 3.6 %convolution_convert_fusion.2 = bf16[384,2048]{1,0:T(8,128)(2,1)} fusion(bf16[2048,768]{1,0:T(8,128)(2,1)S(1)} %copy-done.4, bf16[384,384]{0,1:T(8,128)(2,1)} %copy-done.7, bf16[384,384]{0,1:T(8,128)(2,1)S(1)} %get-tuple-element.4), kind=kOutput, calls=%fused_computation.6 | convolution fusion | flops 1209925632 | bytes 5308416 | tf_op jit(solution)/shard_map/dot_general | solution.py:62
  111.0 0.0 copy-start.6
  111.0 6.3 %all-to-all-start.2 = ((bf16[16,24,2048]{2,1,0:T(8,128)(2,1)}), bf16[16,24,2048]{2,1,0:T(8,128)(2,1)S(1)}, u32[]{:S(2)}, u32[]{:S(2)}) async-start(bf16[16,24,2048]{2,1,0:T(8,128)(2,1)} %bitcast.11), calls=%async_computation.2 | async-start | bytes 3145728 | tf_op jit(solution)/shard_map/all_to_all | solution.py:66
  117.3 0.0 all-reduce.4.cloned.1.call-start
  117.3 0.0 copy-done.6
  117.3 3.6 %fusion = bf16[1,384,2048]{2,1,0:T(8,128)(2,1)} fusion(bf16[384,2048]{1,0:T(8,128)(2,1)} %bitcast.5, f32[384,768]{0,1:T(8,128)S(1)} %copy-done.6), kind=kOutput, calls=%fused_computation.7 | convolution fusion | flops 605650944 | bytes 4325376 | tf_op jit(solution)/shard_map/dot_general | solution.py:71
  120.9 0.0 all-reduce.4.cloned.1.call-update
  121.0 32.5 %all-to-all-done.2 = bf16[16,24,2048]{2,1,0:T(8,128)(2,1)S(1)} async-done(((bf16[16,24,2048]{2,1,0:T(8,128)(2,1)}), bf16[16,24,2048]{2,1,0:T(8,128)(2,1)S(1)}, u32[]{:S(2)}, u32[]{:S(2)}) %all-to-all-start.2) | async-done | bytes 1572896 | tf_op jit(solution)/shard_map/all_to_all | solution.py:66
  153.5 1.7 gather_fusion.2
  155.2 0.0 reduce-scatter.2.cloned.1.call-done
  155.2 2.7 %slice_bitcast_fusion = (bf16[1,1024,384]{2,1,0:T(8,128)(2,1)}, bf16[1,1024,384]{2,1,0:T(8,128)(2,1)}) fusion(bf16[1024,768]{1,0:T(8,128)(2,1)} %reduce-scatter.2.cloned.1.call-done), kind=kLoop, calls=%fused_computation.12 | loop fusion | bytes 3145728 | tf_op jit(solution)/shard_map/broadcast_in_dim | solution.py:84
  157.8 44.8 %all-reduce.4.cloned.1.call-done = bf16[1,384,2048]{2,1,0:T(8,128)(2,1)} async-done(((bf16[1,384,2048]{2,1,0:T(8,128)(2,1)}), bf16[1,384,2048]{2,1,0:T(8,128)(2,1)}) %all-reduce.4.cloned.1.call-update) | async-done | bytes 1572880 | tf_op jit(solution)/shard_map/psum | solution.py:74
  202.6 2.7 %copy.15 = bf16[1,384,2048]{2,1,0:T(8,128)(2,1)} copy(bf16[1,384,2048]{2,1,0:T(8,128)(2,1)} %all-reduce.4.cloned.1.call-done) | data formatting | bytes 3145728
  (5 shorter events, 0.1 us)
Async XLA Ops:
  14.8 6.7 %copy-start = (bf16[1,1024,384]{2,1,0:T(8,128)(2,1)S(1)}, bf16[1,1024,384]{2,1,0:T(8,128)(2,1)}, u32[]{:S(2)}) copy-start(bf16[1,1024,384]{2,1,0:T(8,128)(2,1)} %param.12) | copy-start | bytes 2359300
  14.8 6.7 %copy-start.1 = (bf16[1,1024,384]{2,1,0:T(8,128)(2,1)S(1)}, bf16[1,1024,384]{2,1,0:T(8,128)(2,1)}, u32[]{:S(2)}) copy-start(bf16[1,1024,384]{2,1,0:T(8,128)(2,1)} %param.11) | copy-start | bytes 2359300
  14.8 43.3 %all-to-all-start.1 = ((bf16[16,24,2048]{2,1,0:T(8,128)(2,1)}), bf16[16,24,2048]{2,1,0:T(8,128)(2,1)S(1)}, u32[]{:S(2)}, u32[]{:S(2)}) async-start(bf16[16,24,2048]{2,1,0:T(8,128)(2,1)} %bitcast.7), calls=%async_computation.1 | async-start | bytes 3145728 | tf_op jit(solution)/shard_map/all_to_all | solution.py:38
  21.5 48.5 %all-gather.4.cloned.1.call-start = ((), (), s32[]{:S(2)}) async-start(), calls=%async_computation.4 | async-start | bytes 4718592 | tf_op jit(solution)/shard_map/all_gather | solution.py:45
  22.8 1.0 copy-start.2
  22.8 1.0 copy-start.3
  58.1 40.9 %all-to-all-start = ((bf16[16,24,2048]{2,1,0:T(8,128)(2,1)}), bf16[16,24,2048]{2,1,0:T(8,128)(2,1)}, u32[]{:S(2)}, u32[]{:S(2)}) async-start(bf16[16,24,2048]{2,1,0:T(8,128)(2,1)} %bitcast.4), calls=%async_computation | async-start | bytes 3145728 | tf_op jit(solution)/shard_map/all_to_all | solution.py:39
  62.6 36.2 %all-gather.6.cloned.1.call-start = ((), (), s32[]{:S(2)}) async-start(), calls=%async_computation.7 | async-start | bytes 2359296 | tf_op jit(solution)/shard_map/all_gather | solution.py:46
  63.3 91.8 %reduce-scatter.2.cloned.1.call-start = ((), (), s32[]{:S(2)}) async-start(), calls=%async_computation.5 | async-start | bytes 4718592 | tf_op jit(solution)/shard_map/reduce_scatter | solution.py:75
  73.7 28.2 %copy-start.5 = (f32[384,768]{0,1:T(8,128)}, f32[384,768]{0,1:T(8,128)S(1)}, u32[]{:S(2)}) copy-start(f32[384,768]{0,1:T(8,128)S(1)} %fusion.12) | copy-start | bytes 3538948
  102.0 3.5 %copy-start.7 = (bf16[384,384]{0,1:T(8,128)(2,1)}, bf16[384,384]{0,1:T(8,128)(2,1)S(1)}, u32[]{:S(2)}) copy-start(bf16[384,384]{0,1:T(8,128)(2,1)S(1)} %get-tuple-element.5) | copy-start | bytes 884740
  105.5 1.9 copy-start.4
  111.0 6.4 %copy-start.6 = (f32[384,768]{0,1:T(8,128)S(1)}, f32[384,768]{0,1:T(8,128)}, u32[]{:S(2)}) copy-start(f32[384,768]{0,1:T(8,128)} %copy-done.5) | copy-start | bytes 3538948
  111.0 42.5 %all-to-all-start.2 = ((bf16[16,24,2048]{2,1,0:T(8,128)(2,1)}), bf16[16,24,2048]{2,1,0:T(8,128)(2,1)S(1)}, u32[]{:S(2)}, u32[]{:S(2)}) async-start(bf16[16,24,2048]{2,1,0:T(8,128)(2,1)} %bitcast.11), calls=%async_computation.2 | async-start | bytes 3145728 | tf_op jit(solution)/shard_map/all_to_all | solution.py:66
  117.3 85.4 %all-reduce.4.cloned.1.call-start = ((), (), s32[]{:S(2)}) async-start(), calls=%async_computation.6 | async-start | bytes 3145728 | tf_op jit(solution)/shard_map/psum | solution.py:74
Sparse Core Ops, SparseCore 0:
  24.5 45.4 all-gather.3
  71.5 27.1 all-gather.5
  105.7 43.1 reduce-scatter.1
  151.1 51.4 all-reduce.3
where the time goes:
time: 214 us; the launch traced here: 212 us
  waiting for transfers between devices  141 us (66%)
  local copies, waits for them, and re-layouts  18.4 us (9%)
  starting transfers between devices  17.7 us (8%)
  matrix products  17.4 us (8%)
  between operations  13.9 us (6%)
  other arithmetic  3.84 us (2%)
    psum x1, waiting for transfers between devices, on_device(): down_grad = lax.psum(down_part.astype(jnp.bfloat16), 'dp')[None]  44.8 us
    all_to_all x1, waiting for transfers between devices, on_device(): lax.all_to_all(slot_grad, 'expert', split_axis=0, concat_axis=0, tiled=True)  32.5 us
    all_to_all x1, waiting for transfers between devices, on_device(): lax.all_to_all(send_inputs, 'expert', split_axis=0, concat_axis=0, tiled=...  30.9 us
    all_gather x1, waiting for transfers between devices, on_device(): lax.all_gather(w_down[0], 'dp', axis=1, tiled=True)  25.1 us
    all_to_all x1, starting transfers between devices, on_device(): lax.all_to_all(send_inputs, 'expert', split_axis=0, concat_axis=0, tiled=...  6.69 us
    all_gather x1, waiting for transfers between devices, on_device(): lax.all_gather(local_joined, 'dp', axis=0, tiled=True)  6.61 us
    all_to_all x1, starting transfers between devices, on_device(): lax.all_to_all(slot_grad, 'expert', split_axis=0, concat_axis=0, tiled=True)  6.32 us
    unnamed x17, local copies, waits for them, and re-layouts  5.63 us
  transfers between devices with their start and end apart: 7, of which 6 were waited for; matrix products, arithmetic and copies ran while one was open for 9% of the time, Pallas kernels for 0%

commit v1 on v0

v1 whole, which is shorter than its diff:
```python
import jax
import jax.numpy as jnp
from jax import lax
from jax.sharding import PartitionSpec as P

BF16 = jnp.bfloat16
F32 = jnp.float32
BOTH = ("dp", "expert")


def dot(a, b, contract):
    return lax.dot_general(a, b, ((contract[:1], contract[1:]), ((), ())), preferred_element_type=F32)


def sum_over_dp(partial):
    n_dp = lax.axis_size("dp")
    if n_dp == 1:
        return partial
    if n_dp == 2:
        return partial + lax.ppermute(partial.astype(BF16), "dp", [(0, 1), (1, 0)]).astype(F32)
    return lax.psum(partial, "dp")


def gather_columns(half):
    n_dp = lax.axis_size("dp")
    if n_dp != 2:
        return lax.all_gather(half, "dp", axis=1, tiled=True)
    other = lax.ppermute(half, "dp", [(0, 1), (1, 0)])
    first = lax.axis_index("dp") == 0
    return jnp.concatenate([jnp.where(first, half, other), jnp.where(first, other, half)], axis=1)


def on_device(tokens, out_grad, expert_ids, gates, w_gate, w_up, w_down):
    n_dp = lax.axis_size("dp")
    experts = lax.axis_size("expert")
    tok_rows, width = tokens.shape
    per_token = expert_ids.shape[1]
    hidden = w_gate.shape[2]
    entries = tok_rows * per_token
    depth = 3 * entries // experts
    slots = experts * depth
    cols = width // n_dp
    rows = experts * depth

    flat_ids = expert_ids.reshape(entries)
    onehot = (flat_ids[:, None] == jnp.arange(experts, dtype=jnp.int32)[None, :]).astype(F32)
    earlier = (
        jnp.arange(entries, dtype=jnp.int32)[None, :] < jnp.arange(entries, dtype=jnp.int32)[:, None]
    ).astype(F32)
    before = dot(earlier, onehot, (1, 0))
    ranking = jnp.sum(before * onehot, axis=1).astype(jnp.int32)
    slot_of_entry = flat_ids * depth + ranking
    place = (jnp.arange(slots, dtype=jnp.int32)[:, None] == slot_of_entry[None, :]).astype(BF16)

    def dispatch(table):
        table = jnp.repeat(table, per_token, axis=0) if table.shape[0] != entries else table
        halves = table.reshape(entries, n_dp, cols)
        sent = jnp.stack(
            [dot(place, halves[:, part], (1, 0)).astype(BF16) for part in range(n_dp)]
        ).reshape(n_dp * experts, depth, cols)
        got = lax.all_to_all(sent, BOTH, split_axis=0, concat_axis=0, tiled=True)
        return got.reshape(n_dp * rows, cols)

    scaled = (
        (gates[:, :, None] * out_grad.astype(F32)[:, None, :]).astype(BF16).reshape(entries, width)
    )
    rows_in = dispatch(tokens)
    grads_in = dispatch(scaled)

    joined = jnp.concatenate([w_gate[0], w_up[0]], axis=1)
    preact = sum_over_dp(dot(rows_in, joined, (1, 0)))
    hidden_grad = sum_over_dp(dot(grads_in, w_down[0], (1, 1)))

    gate_pre = preact[:, :hidden]
    up_pre = preact[:, hidden:]
    sigmoid = jax.nn.sigmoid(gate_pre)
    silu_value = gate_pre * sigmoid
    activated = (silu_value * up_pre).astype(BF16)
    gate_side = (hidden_grad * up_pre * sigmoid * (1.0 + gate_pre * (1.0 - sigmoid))).astype(BF16)
    up_side = (hidden_grad * silu_value).astype(BF16)
    sides = jnp.concatenate([gate_side, up_side], axis=1)

    slot_grad = dot(sides, joined, (1, 1)).astype(BF16).reshape(n_dp * experts, depth, cols)
    returned = lax.all_to_all(slot_grad, BOTH, split_axis=0, concat_axis=0, tiled=True).reshape(
        n_dp, slots, cols
    )

    def over_groups(left, right):
        total = 0.0
        for group in range(n_dp):
            part = slice(group * rows, (group + 1) * rows)
            total = total + dot(left[part], right[part], (0, 0)).astype(BF16).astype(F32)
        return total.astype(BF16)

    down_grad = gather_columns(over_groups(activated, grads_in))[None]
    joined_grad = over_groups(rows_in, sides)

    picked = jnp.concatenate(
        [dot(place, returned[part], (0, 0)) for part in range(n_dp)], axis=1
    )
    input_grad = jnp.sum(picked.reshape(tok_rows, per_token, width), axis=1).astype(BF16)
    return (input_grad, joined_grad[:, :hidden][None], joined_grad[:, hidden:][None], down_grad)


def solution(mesh):
    rows = P(BOTH, None)
    in_specs = (
        rows,
        rows,
        rows,
        rows,
        P("expert", "dp", None),
        P("expert", "dp", None),
        P("expert", None, "dp"),
    )
    out_specs = (
        rows,
        P("expert", "dp", None),
        P("expert", "dp", None),
        P("expert", None, None),
    )
    return jax.shard_map(
        on_device, mesh=mesh, in_specs=in_specs, out_specs=out_specs, check_vma=False
    )
```

time: 214 us -> 164 us (0.77)
  waiting for transfers between devices: 141 us -> 110 us
  between operations: 13.9 us -> 0.87 us
  local copies, waits for them, and re-layouts: 18.4 us -> 7.75 us
  starting transfers between devices: 17.7 us -> 20.6 us
  matrix products: 17.4 us -> 14.5 us
  other arithmetic: 3.84 us -> 6.52 us
    ppermute x0 -> x3, waiting for transfers between devices: none -> 48.4 us  [the longest x1 28.4 us: gather_columns(): other = lax.ppermute(half, 'dp', [(0, 1), (1, 0)])]
    psum x1 -> x0, waiting for transfers between devices: 44.8 us -> none  [on_device(): down_grad = lax.psum(down_part.astype(jnp.bfloat16), 'dp')[None]]
    all_gather x2 -> x0, waiting for transfers between devices: 31.7 us -> none  [the longest x1 25.1 us: on_device(): lax.all_gather(w_down[0], 'dp', axis=1, tiled=True)]
    gather x3 -> x0, local copies, waits for them, and re-layouts: 7.97 us -> none  [the longest x1 3.13 us: on_device(): input_table[source // per_token]]
    dot_general x5 -> x14, matrix products: 17.4 us -> 14.5 us  [dot(): lax.dot_general(a, b, ((contract[:1], contract[1:]), ((), ())), preferred...]
    ppermute x0 -> x3, starting transfers between devices: none -> 2.81 us  [the longest x2 1.56 us: sum_over_dp(): lax.ppermute(partial.astype(BF16), 'dp', [(0, 1), (1, 0)]).astype(F32)]
    another operation x1 -> x2, other arithmetic: 0.17 us -> 2.57 us  [dispatch(): jnp.stack([dot(place, halves[:, part], (1, 0)).astype(BF16) for part in r...]
    unnamed x17 -> x24, local copies, waits for them, and re-layouts: 5.63 us -> 4.69 us
  transfers between devices with their start and end apart: 7 -> 6, of which waited for: 6 -> 5; matrix products, arithmetic and copies ran while one was open for 9% -> 9% of each run, Pallas kernels for 0% -> 0%
where the time goes in v1:
time: 164 us; the launch traced here: 161 us
  waiting for transfers between devices  110 us (67%)
  starting transfers between devices  20.6 us (13%)
  matrix products  14.5 us (9%)
  local copies, waits for them, and re-layouts  7.75 us (5%)
  other arithmetic  6.52 us (4%)
    all_to_all x2, waiting for transfers between devices, dispatch(): got = lax.all_to_all(sent, BOTH, split_axis=0, concat_axis=0, tiled=True)  62.1 us
    ppermute x1, waiting for transfers between devices, gather_columns(): other = lax.ppermute(half, 'dp', [(0, 1), (1, 0)])  28.4 us
    ppermute x2, waiting for transfers between devices, sum_over_dp(): lax.ppermute(partial.astype(BF16), 'dp', [(0, 1), (1, 0)]).astype(F32)  20 us
    dot_general x14, matrix products, dot(): lax.dot_general(a, b, ((contract[:1], contract[1:]), ((), ())), preferred...  14.5 us
    all_to_all x2, starting transfers between devices, dispatch(): got = lax.all_to_all(sent, BOTH, split_axis=0, concat_axis=0, tiled=True)  12.3 us
    all_to_all x1, starting transfers between devices, on_device(): lax.all_to_all(slot_grad, BOTH, split_axis=0, concat_axis=0, tiled=True)  5.51 us
    unnamed x24, local copies, waits for them, and re-layouts  4.69 us
  transfers between devices with their start and end apart: 6, of which 5 were waited for; matrix products, arithmetic and copies ran while one was open for 9% of the time, Pallas kernels for 0%

profile of v1, /device:TPU:13, one launch (start us, length us, event | category | flops | bytes accessed | tf_op | source)
XLA Modules:
  0.0 160.7 jit_solution(14764527090781471530)
XLA Ops:
  0.6 0.0 copy-start
  0.6 0.9 fusion.5
  1.5 0.7 convert_add_fusion.2
  2.2 1.3 copy.14
  3.5 0.4 fusion.2
  3.9 0.4 fusion.3
  4.3 1.3 pad_maximum_fusion.1
  5.6 0.0 copy-start.6
  5.6 0.0 copy-start.7
  5.6 6.3 %all-to-all-start.1 = ((bf16[32,24,1024]{2,1,0:T(8,128)(2,1)}), bf16[32,24,1024]{2,1,0:T(8,128)(2,1)S(1)}, u32[]{:S(2)}, u32[]{:S(2)}) async-start(bf16[32,24,1024]{2,1,0:T(8,128)(2,1)} %bitcast.64), calls=%async_computation.1 | async-start | bytes 3145728 | tf_op jit(solution)/shard_map/all_to_all | solution.py:61
  11.9 0.0 copy-done.6
  11.9 0.3 copy.11
  12.2 0.0 copy-done.7
  12.2 0.1 multiply_convert_fusion.3
  12.3 0.4 fusion
  12.7 0.4 fusion.1
  13.1 1.3 pad_maximum_fusion
  14.4 32.8 %all-to-all-done.1 = bf16[32,24,1024]{2,1,0:T(8,128)(2,1)S(1)} async-done(((bf16[32,24,1024]{2,1,0:T(8,128)(2,1)}), bf16[32,24,1024]{2,1,0:T(8,128)(2,1)S(1)}, u32[]{:S(2)}, u32[]{:S(2)}) %all-to-all-start.1) | async-done | bytes 1572896 | tf_op jit(solution)/shard_map/all_to_all | solution.py:61
  47.2 0.0 copy-start.1
  47.2 0.0 copy-start.8
  47.2 1.1 copy-done.1
  48.3 6.0 %all-to-all-start = ((bf16[32,24,1024]{2,1,0:T(8,128)(2,1)}), bf16[32,24,1024]{2,1,0:T(8,128)(2,1)S(1)}, u32[]{:S(2)}, u32[]{:S(2)}) async-start(bf16[32,24,1024]{2,1,0:T(8,128)(2,1)} %bitcast.63), calls=%async_computation | async-start | bytes 3145728 | tf_op jit(solution)/shard_map/all_to_all | solution.py:61
  54.3 0.0 copy-done.8
  54.3 4.9 %fusion.29 = (bf16[768,768]{0,1:T(8,128)(2,1)}, f32[768,768]{0,1:T(8,128)}) fusion(bf16[768,1024]{1,0:T(8,128)(2,1)} %bitcast.62, bf16[1024,384]{1,0:T(8,128)(2,1)S(1)} %bitcast.77, bf16[1024,384]{1,0:T(8,128)(2,1)} %bitcast.79), kind=kOutput, calls=%fused_computation.70 | convolution fusion | flops 1211695104 | bytes 6684672 | tf_op jit(solution)/shard_map/dot_general | solution.py:12
  59.2 1.2 collective-permute-start.1
  60.4 29.3 %all-to-all-done = bf16[32,24,1024]{2,1,0:T(8,128)(2,1)S(1)} async-done(((bf16[32,24,1024]{2,1,0:T(8,128)(2,1)}), bf16[32,24,1024]{2,1,0:T(8,128)(2,1)S(1)}, u32[]{:S(2)}, u32[]{:S(2)}) %all-to-all-start) | async-done | bytes 1572896 | tf_op jit(solution)/shard_map/all_to_all | solution.py:61
  89.6 0.0 copy-done
  89.7 0.0 copy-start.3
  89.7 0.8 fusion.30
  90.5 0.4 collective-permute-start
  90.8 7.7 %collective-permute-done.1 = bf16[768,768]{0,1:T(8,128)(2,1)S(1)} collective-permute-done((bf16[768,768]{0,1:T(8,128)(2,1)}, bf16[768,768]{0,1:T(8,128)(2,1)S(1)}, u32[]{:S(2)}, u32[]{:S(2)}) %collective-permute-start.1) | collective-permute-done | bytes 1179680 | tf_op jit(solution)/shard_map/ppermute | solution.py:20
  98.5 0.0 copy-done.3
  98.5 0.3 convert_add_fusion
  98.8 12.3 %collective-permute-done = bf16[768,384]{0,1:T(8,128)(2,1)S(1)} collective-permute-done((bf16[768,384]{0,1:T(8,128)(2,1)S(1)}, bf16[768,384]{0,1:T(8,128)(2,1)S(1)}, u32[]{:S(2)}, u32[]{:S(2)}) %collective-permute-start) | collective-permute-done | bytes 589856 | tf_op jit(solution)/shard_map/ppermute | solution.py:20
  111.2 0.0 copy-start.9
  111.2 0.0 copy-start.10
  111.2 0.7 multiply_convert_fusion.2
  111.9 0.0 copy-start.4
  111.9 0.4 copy-done.9
  112.3 0.2 copy-done.10
  112.5 2.6 %convolution_convert_fusion.2 = bf16[768,1024]{1,0:T(8,128)(2,1)} fusion(bf16[768,384]{0,1:T(8,128)(2,1)S(1)} %get-tuple-element.5, bf16[768,384]{0,1:T(8,128)(2,1)S(1)} %get-tuple-element.4, bf16[1024,384]{1,0:T(8,128)(2,1)S(1)} %bitcast.78, bf16[1024,384]{1,0:T(8,128)(2,1)S(1)} %bitcast.80), kind=kOutput, calls=%fused_computation.4 | convolution fusion | flops 1214251008 | bytes 4325376 | tf_op jit(solution)/shard_map/dot_general | solution.py:12
  115.1 0.0 copy-done.4
  115.1 5.5 %all-to-all-start.2 = ((bf16[32,24,1024]{2,1,0:T(8,128)(2,1)}), bf16[32,24,1024]{2,1,0:T(8,128)(2,1)}, u32[]{:S(2)}, u32[]{:S(2)}) async-start(bf16[32,24,1024]{2,1,0:T(8,128)(2,1)} %bitcast.73), calls=%async_computation.2 | async-start | bytes 3145728 | tf_op jit(solution)/shard_map/all_to_all | solution.py:84
  120.6 0.0 copy-start.2
  120.7 0.1 fusion.26
  120.8 1.3 copy-done.2
  122.1 0.1 fusion.27
  122.2 0.6 convolution_convert_fusion.7
  122.8 0.0 copy-start.5
  122.8 0.6 add_convert_fusion.1
  123.4 1.2 collective-permute-start.2
  124.6 0.0 copy-done.5
  124.6 1.0 convolution_convert_fusion
  125.7 1.0 add_convert_fusion
  126.7 1.3 slice_bitcast_fusion
  128.0 28.4 %collective-permute-done.2 = bf16[384,1024]{1,0:T(8,128)(2,1)S(1)} collective-permute-done((bf16[384,1024]{1,0:T(8,128)(2,1)S(1)}, bf16[384,1024]{1,0:T(8,128)(2,1)S(1)}, u32[]{:S(2)}, u32[]{:S(2)}) %collective-permute-start.2) | collective-permute-done | bytes 786464 | tf_op jit(solution)/shard_map/ppermute | solution.py:28
  156.3 0.1 broadcast_select_fusion.1
  156.5 1.2 maximum_bitcast_fusion
  157.7 0.0 all-to-all-done.2
  157.7 1.5 fusion.28
  159.2 0.4 convolution_convert_fusion.10
  159.6 0.3 convolution_convert_fusion.9
  159.9 0.8 pad_maximum_fusion.7
Async XLA Ops:
  0.6 89.0 %copy-start = (bf16[1,384,1024]{2,1,0:T(8,128)(2,1)S(1)}, bf16[1,384,1024]{2,1,0:T(8,128)(2,1)}, u32[]{:S(2)}) copy-start(bf16[1,384,1024]{2,1,0:T(8,128)(2,1)} %param.13) | copy-start | bytes 2359300
  5.6 6.3 %copy-start.6 = (bf16[128,2048]{1,0:T(8,128)(2,1)S(1)}, bf16[128,2048]{1,0:T(8,128)(2,1)}, u32[]{:S(2)}) copy-start(bf16[128,2048]{1,0:T(8,128)(2,1)} %param.8) | copy-start | bytes 1572868
  5.6 6.6 %copy-start.7 = (f32[128,1]{0,1:T(1,128)S(1)}, f32[128,1]{0,1:T(1,128)}, u32[]{:S(2)}) copy-start(f32[128,1]{0,1:T(1,128)} %param.10) | copy-start | bytes 1540
  5.6 41.6 %all-to-all-start.1 = ((bf16[32,24,1024]{2,1,0:T(8,128)(2,1)}), bf16[32,24,1024]{2,1,0:T(8,128)(2,1)S(1)}, u32[]{:S(2)}, u32[]{:S(2)}) async-start(bf16[32,24,1024]{2,1,0:T(8,128)(2,1)} %bitcast.64), calls=%async_computation.1 | async-start | bytes 3145728 | tf_op jit(solution)/shard_map/all_to_all | solution.py:61
  47.2 1.1 copy-start.1
  47.2 7.2 %copy-start.8 = (bf16[1,1024,384]{2,1,0:T(8,128)(2,1)S(1)}, bf16[1,1024,384]{2,1,0:T(8,128)(2,1)}, u32[]{:S(2)}) copy-start(bf16[1,1024,384]{2,1,0:T(8,128)(2,1)} %param.12) | copy-start | bytes 2359300
  48.3 41.3 %all-to-all-start = ((bf16[32,24,1024]{2,1,0:T(8,128)(2,1)}), bf16[32,24,1024]{2,1,0:T(8,128)(2,1)S(1)}, u32[]{:S(2)}, u32[]{:S(2)}) async-start(bf16[32,24,1024]{2,1,0:T(8,128)(2,1)} %bitcast.63), calls=%async_computation | async-start | bytes 3145728 | tf_op jit(solution)/shard_map/all_to_all | solution.py:61
  59.2 39.3 %collective-permute-start.1 = (bf16[768,768]{0,1:T(8,128)(2,1)}, bf16[768,768]{0,1:T(8,128)(2,1)S(1)}, u32[]{:S(2)}, u32[]{:S(2)}) collective-permute-start(bf16[768,768]{0,1:T(8,128)(2,1)} %get-tuple-element.17), channel_id=1, source_target_pairs={{0,16},{16,0},{1,17},{17,1},{2,18},{18,2},{3,19},{19,3},{4,20},{20... | collective-permute-start | bytes 3538952 | tf_op jit(solution)/shard_map/ppermute | solution.py:20
  89.7 8.9 %copy-start.3 = (f32[768,768]{0,1:T(8,128)S(1)}, f32[768,768]{0,1:T(8,128)}, u32[]{:S(2)}) copy-start(f32[768,768]{0,1:T(8,128)} %get-tuple-element.18) | copy-start | bytes 7077892
  90.5 20.7 %collective-permute-start = (bf16[768,384]{0,1:T(8,128)(2,1)S(1)}, bf16[768,384]{0,1:T(8,128)(2,1)S(1)}, u32[]{:S(2)}, u32[]{:S(2)}) collective-permute-start(bf16[768,384]{0,1:T(8,128)(2,1)S(1)} %get-tuple-element.19), channel_id=1, source_target_pairs={{0,16},{16,0},{1,17},{17,1},{2,18},{18,2},{3,19},{19,3},{4,20},{20... | collective-permute-start | bytes 1769480 | tf_op jit(solution)/shard_map/ppermute | solution.py:20
  111.2 1.1 copy-start.9
  111.2 1.4 copy-start.10
  111.9 3.3 %copy-start.4 = (bf16[768,384]{0,1:T(8,128)(2,1)}, bf16[768,384]{0,1:T(8,128)(2,1)S(1)}, u32[]{:S(2)}) copy-start(bf16[768,384]{0,1:T(8,128)(2,1)S(1)} %get-tuple-element.5) | copy-start | bytes 1769476
  115.1 42.6 %all-to-all-start.2 = ((bf16[32,24,1024]{2,1,0:T(8,128)(2,1)}), bf16[32,24,1024]{2,1,0:T(8,128)(2,1)}, u32[]{:S(2)}, u32[]{:S(2)}) async-start(bf16[32,24,1024]{2,1,0:T(8,128)(2,1)} %bitcast.73), calls=%async_computation.2 | async-start | bytes 3145728 | tf_op jit(solution)/shard_map/all_to_all | solution.py:84
  120.6 1.4 copy-start.2
  122.8 1.8 %copy-start.5 = (bf16[768,384]{0,1:T(8,128)(2,1)S(1)}, bf16[768,384]{0,1:T(8,128)(2,1)}, u32[]{:S(2)}) copy-start(bf16[768,384]{0,1:T(8,128)(2,1)} %copy-done.4) | copy-start | bytes 1769476
  123.4 33.0 %collective-permute-start.2 = (bf16[384,1024]{1,0:T(8,128)(2,1)S(1)}, bf16[384,1024]{1,0:T(8,128)(2,1)S(1)}, u32[]{:S(2)}, u32[]{:S(2)}) collective-permute-start(bf16[384,1024]{1,0:T(8,128)(2,1)S(1)} %add_convert_fusion.1), channel_id=1, source_target_pairs={{0,16},{16,0},{1,17},{17,1},{2,18},{18,2},{3,19},{19,3},{4,20},{20... | collective-permute-start | bytes 2359304 | tf_op jit(solution)/shard_map/ppermute | solution.py:28

commit v2 on v1

v2 whole, which is shorter than its diff:
```python
import functools

import jax
import jax.numpy as jnp
from jax import lax
from jax.experimental import pallas as pl
from jax.experimental.pallas import tpu as pltpu
from jax.sharding import PartitionSpec as P

BF16 = jnp.bfloat16
F32 = jnp.float32
BOTH = ("dp", "expert")
LATE_FLOPS = 100_000_000_000


def dot(a, b, contract):
    return lax.dot_general(a, b, ((contract[:1], contract[1:]), ((), ())), preferred_element_type=F32)


def swap(x):
    return lax.ppermute(x, "dp", [(0, 1), (1, 0)])


def exchange(x, axes):
    return lax.all_to_all(x, axes, split_axis=0, concat_axis=0, tiled=True)


def place_matrix(expert_ids, experts, depth):
    entries = expert_ids.size
    flat_ids = expert_ids.reshape(entries)
    order = jnp.arange(entries, dtype=jnp.int32)
    onehot = (flat_ids[:, None] == jnp.arange(experts, dtype=jnp.int32)[None, :]).astype(BF16)
    earlier = (order[None, :] < order[:, None]).astype(BF16)
    before = dot(earlier, onehot, (1, 0))
    ranking = jnp.sum(before * onehot.astype(F32), axis=1).astype(jnp.int32)
    slot_of_entry = flat_ids * depth + ranking
    return (
        jnp.arange(experts * depth, dtype=jnp.int32)[:, None] == slot_of_entry[None, :]
    ).astype(BF16)


def sides_of(gate_pre, up_pre, hidden_grad):
    sigmoid = jax.nn.sigmoid(gate_pre)
    silu_value = gate_pre * sigmoid
    activated = (silu_value * up_pre).astype(BF16)
    gate_side = (hidden_grad * up_pre * sigmoid * (1.0 + gate_pre * (1.0 - sigmoid))).astype(BF16)
    up_side = (hidden_grad * silu_value).astype(BF16)
    return activated, jnp.concatenate([gate_side, up_side], axis=1)


def sum_parts(first, second):
    return (first.astype(BF16).astype(F32) + second.astype(BF16).astype(F32)).astype(BF16)


def scaled_rows(out_grad, gates):
    return (
        (gates[:, :, None] * out_grad.astype(F32)[:, None, :])
        .astype(BF16)
        .reshape(gates.size, out_grad.shape[1])
    )


def token_rows(tokens, per_token):
    return jnp.repeat(tokens, per_token, axis=0) if per_token > 1 else tokens


def sum_choices(picked, per_token):
    if per_token > 1:
        picked = jnp.sum(picked.reshape(-1, per_token, picked.shape[1]).astype(F32), axis=1)
    return picked.astype(BF16)


MIB = 1 << 20
IN_HBM = pl.BlockSpec(memory_space=pltpu.HBM)


def shape(*dims, dtype=BF16):
    return jax.ShapeDtypeStruct(dims, dtype)


def call(kernel, out_shapes, scratch, copies, flops, *operands):
    moved = sum(x.size * x.dtype.itemsize for x in operands)
    moved += sum(x.size * x.dtype.itemsize for x in out_shapes)
    return pl.pallas_call(
        kernel,
        out_shape=list(out_shapes),
        in_specs=[IN_HBM] * len(operands),
        out_specs=[IN_HBM] * len(out_shapes),
        scratch_shapes=[pltpu.VMEM(x.shape, x.dtype) for x in scratch]
        + [pltpu.SemaphoreType.DMA((copies,))],
        compiler_params=pltpu.CompilerParams(vmem_limit_bytes=60 * MIB),
        cost_estimate=pl.CostEstimate(flops=flops, bytes_accessed=moved, transcendentals=0),
    )(*operands)


class Mover:
    def __init__(self, semaphores):
        self.semaphores, self.count = semaphores, 0

    def start(self, source, target):
        copy = pltpu.make_async_copy(source, target, self.semaphores.at[self.count])
        self.count += 1
        copy.start()
        return copy


def wait(*copies):
    for copy in copies:
        copy.wait()


def half_at(index, half):
    return pl.ds(pl.multiple_of(index * half, half), half)


def kernel_place(
    experts, depth, ids_hbm, gates_hbm, grad_hbm, place_hbm, send_hbm, ids, gates, grad, place_at, send, sems
):
    entries = ids.shape[1]
    slots = experts * depth
    half = grad.shape[1] // 2
    move = Mover(sems)
    small = move.start(ids_hbm, ids), move.start(gates_hbm, gates)
    loads = [
        move.start(grad_hbm.at[:, pl.ds(part * half, half)], grad.at[:, pl.ds(part * half, half)])
        for part in range(2)
    ]
    wait(*small)
    onehot = (lax.broadcasted_iota(jnp.int32, (experts, entries), 0) == ids[...]).astype(F32)
    earlier = (
        lax.broadcasted_iota(jnp.int32, (entries, entries), 0)
        < lax.broadcasted_iota(jnp.int32, (entries, entries), 1)
    ).astype(BF16)
    before = dot(onehot.astype(BF16), earlier, (1, 0))
    ranking = jnp.sum(before * onehot, axis=0, keepdims=True).astype(jnp.int32)
    slot = ids[...] * depth + ranking
    place = (lax.broadcasted_iota(jnp.int32, (slots, entries), 0) == slot).astype(F32).astype(BF16)
    place_at[...] = place
    stores = [move.start(place_at, place_hbm)]
    weight = jnp.broadcast_to(gates[...], (entries, entries)).T[:, :1]
    for part in range(2):
        wait(loads[part])
        scaled = (weight * grad[:, part * half : (part + 1) * half].astype(F32)).astype(BF16)
        rows = pl.ds(part * slots, slots)
        send[rows] = dot(place, scaled, (1, 0)).astype(BF16)
        stores.append(move.start(send.at[rows], send_hbm.at[rows]))
    wait(*stores)


def kernel_core(
    rows_hbm, gate_hbm, up_hbm, other_gate_hbm, other_up_hbm, partial_hbm, remote_hbm,
    pre_hbm, act_hbm, sides_hbm, slot_hbm,
    rows, joined, partial, remote, pre_at, act, sides, slot, sems,
):
    slots, width = rows.shape
    half = width // 2
    hidden = act.shape[1]
    mine = pl.ds(pl.multiple_of(lax.axis_index("dp") * slots, slots), slots)
    move = Mover(sems)
    first = [move.start(rows_hbm.at[:, pl.ds(0, half)], rows.at[:, pl.ds(0, half)])]
    first += [
        move.start(source, joined.at[pl.ds(0, half), pl.ds(at, hidden)])
        for at, source in ((0, gate_hbm), (hidden, up_hbm))
    ]
    second = [move.start(rows_hbm.at[:, pl.ds(half, half)], rows.at[:, pl.ds(half, half)])]
    second += [
        move.start(source, joined.at[pl.ds(half, half), pl.ds(at, hidden)])
        for at, source in ((0, other_gate_hbm), (hidden, other_up_hbm))
    ]
    third = [move.start(partial_hbm.at[mine], partial), move.start(remote_hbm.at[mine], remote)]
    wait(*first)
    pre = dot(rows[:, :half], joined[:half], (1, 0))
    wait(*second)
    pre = pre + dot(rows[:, half:], joined[half:], (1, 0))
    pre_at[...] = pre.astype(BF16)
    stores = [move.start(pre_at, pre_hbm)]
    wait(*third)
    hidden_grad = partial[...] + remote[...].astype(F32)
    activated, both = sides_of(pre[:, :hidden], pre[:, hidden:], hidden_grad)
    act[...] = activated
    sides[...] = both
    stores += [move.start(act, act_hbm), move.start(sides, sides_hbm)]
    for part in range(2):
        columns = pl.ds(part * half, half)
        slot[:, part * half : (part + 1) * half] = dot(
            both, joined[part * half : (part + 1) * half], (1, 1)
        ).astype(BF16)
        stores.append(move.start(slot.at[:, columns], slot_hbm.at[:, columns]))
    wait(*stores)


def kernel_down(
    pre_hbm, partial_hbm, remote_hbm, act_hbm, grads_hbm,
    down_hbm, sides_hbm,
    pre, partial, remote, act, grads, down, sides, sems,
):
    slots, hidden = act.shape
    me = lax.axis_index("dp")
    mine = pl.ds(pl.multiple_of(me * slots, slots), slots)
    theirs = pl.ds(pl.multiple_of((1 - me) * slots, slots), slots)
    move = Mover(sems)
    first = [
        move.start(source, target)
        for source, target in (
            (pre_hbm, pre),
            (partial_hbm.at[theirs], partial),
            (remote_hbm.at[theirs], remote),
        )
    ]
    second = [
        move.start(source, target)
        for source, target in (
            (act_hbm, act),
            (grads_hbm.at[mine], grads.at[pl.ds(0, slots)]),
            (grads_hbm.at[theirs], grads.at[pl.ds(slots, slots)]),
        )
    ]
    wait(*first)
    hidden_grad = partial[...] + remote[...].astype(F32)
    act_other, sides_other = sides_of(
        pre[:, :hidden].astype(F32), pre[:, hidden:].astype(F32), hidden_grad
    )
    sides[...] = sides_other
    stores = [move.start(sides, sides_hbm)]
    wait(*second)
    down[...] = sum_parts(
        dot(act[...], grads[:slots], (0, 0)), dot(act_other, grads[slots:], (0, 0))
    )
    stores.append(move.start(down, down_hbm))
    wait(*stores)


def kernel_joined(
    rows_hbm, other_rows_hbm, sides_hbm, other_sides_hbm,
    gate_hbm, up_hbm,
    rows, other_rows, sides, other_sides, joined, sems,
):
    half = rows.shape[1]
    hidden = sides.shape[1] // 2
    move = Mover(sems)
    loads = [
        move.start(source, target)
        for source, target in (
            (rows_hbm.at[:, pl.ds(0, half)], rows),
            (sides_hbm, sides),
            (other_rows_hbm, other_rows),
            (other_sides_hbm, other_sides),
        )
    ]
    wait(*loads)
    stores = []
    for at, target in ((0, gate_hbm), (hidden, up_hbm)):
        columns = slice(at, at + hidden)
        joined[:, columns] = sum_parts(
            dot(rows[...], sides[:, columns], (0, 0)),
            dot(other_rows[...], other_sides[:, columns], (0, 0)),
        )
        stores.append(move.start(joined.at[:, pl.ds(at, hidden)], target))
    wait(*stores)


def kernel_final(
    place_hbm, returned_hbm, own_hbm, other_hbm, input_hbm, down_hbm, place, returned, out, down, sems
):
    half = out.shape[1] // 2
    me = lax.axis_index("dp")
    move = Mover(sems)
    loads = [move.start(place_hbm, place)] + [
        move.start(
            returned_hbm.at[:, pl.ds(part * half, half)], returned.at[:, pl.ds(part * half, half)]
        )
        for part in range(2)
    ]
    at = half_at(me, half), half_at(1 - me, half)
    down_loads = [
        move.start(source, down.at[part]) for part, source in enumerate((own_hbm, other_hbm))
    ]
    wait(*loads[:2])
    stores = []
    for part in range(2):
        columns = slice(part * half, (part + 1) * half)
        out[:, columns] = dot(place[...], returned[:, columns], (0, 0)).astype(BF16)
        stores.append(
            move.start(out.at[:, pl.ds(part * half, half)], input_hbm.at[:, at[part]])
        )
        wait(down_loads[part])
        stores.append(move.start(down.at[part], down_hbm.at[:, at[part]]))
        if part == 0:
            wait(loads[2])
    wait(*stores)


def on_pair(tokens, out_grad, expert_ids, gates, w_gate, w_up, w_down):
    experts = lax.axis_size("expert")
    width = tokens.shape[1]
    per_token = expert_ids.shape[1]
    hidden = w_gate.shape[2]
    entries = expert_ids.size
    depth = 3 * entries // experts
    slots = experts * depth
    half = width // 2
    first = lax.axis_index("dp") == 0

    grad_rows = token_rows(out_grad, per_token)
    place, send_grads = call(
        functools.partial(kernel_place, experts, depth),
        (shape(slots, entries), shape(2 * slots, half)),
        (
            shape(1, entries, dtype=jnp.int32),
            shape(1, entries, dtype=F32),
            shape(entries, width),
            shape(slots, entries),
            shape(2 * slots, half),
        ),
        7,
        2 * slots * entries * width,
        expert_ids.reshape(1, entries),
        gates.reshape(1, entries),
        grad_rows,
    )
    recv_grads = exchange(send_grads.reshape(2 * experts, depth, half), BOTH)
    other_gate = swap(w_gate[0])
    inputs = token_rows(tokens, per_token)
    low, high = inputs[:, :half], inputs[:, half:]
    inputs = jnp.concatenate([jnp.where(first, low, high), jnp.where(first, high, low)], axis=1)
    send_inputs = dot(place, inputs, (1, 0)).astype(BF16)
    recv_grads, other_gate, send_inputs = lax.optimization_barrier(
        (recv_grads, other_gate, send_inputs)
    )
    rows_in = exchange(send_inputs.reshape(experts, depth, width), "expert").reshape(slots, width)
    other_up = swap(w_up[0])

    grads_in = recv_grads.reshape(2 * slots, half)
    partial = dot(grads_in, w_down[0], (1, 1))
    remote = swap(partial.astype(BF16))

    other_rows = swap(rows_in[:, half:])
    pre, act, sides, slot_grad = call(
        kernel_core,
        (
            shape(slots, 2 * hidden),
            shape(slots, hidden),
            shape(slots, 2 * hidden),
            shape(slots, width),
        ),
        (
            shape(slots, width),
            shape(width, 2 * hidden),
            shape(slots, hidden, dtype=F32),
            shape(slots, hidden),
            shape(slots, 2 * hidden),
            shape(slots, hidden),
            shape(slots, 2 * hidden),
            shape(slots, width),
        ),
        13,
        8 * slots * hidden * width,
        rows_in,
        w_gate[0],
        w_up[0],
        other_gate,
        other_up,
        partial,
        remote,
    )
    other_pre = swap(pre)
    returned = exchange(slot_grad.reshape(experts, depth, width), "expert").reshape(slots, width)

    own_down, other_sides = call(
        kernel_down,
        (shape(hidden, half), shape(slots, 2 * hidden)),
        (
            shape(slots, 2 * hidden),
            shape(slots, hidden, dtype=F32),
            shape(slots, hidden),
            shape(slots, hidden),
            shape(2 * slots, half),
            shape(hidden, half),
            shape(slots, 2 * hidden),
        ),
        8,
        LATE_FLOPS,
        other_pre,
        partial,
        remote,
        act,
        grads_in,
    )
    other_down = swap(own_down)
    gate_grad, up_grad = call(
        kernel_joined,
        (shape(half, hidden), shape(half, hidden)),
        (
            shape(slots, half),
            shape(slots, half),
            shape(slots, 2 * hidden),
            shape(slots, 2 * hidden),
            shape(half, 2 * hidden),
        ),
        6,
        LATE_FLOPS,
        rows_in,
        other_rows,
        sides,
        other_sides,
    )
    picked, down_grad = call(
        kernel_final,
        (shape(entries, width), shape(hidden, width)),
        (
            shape(slots, entries),
            shape(slots, width),
            shape(entries, width),
            shape(2, hidden, half),
        ),
        9,
        2 * slots * entries * width,
        place,
        returned,
        own_down,
        other_down,
    )
    return (sum_choices(picked, per_token), gate_grad[None], up_grad[None], down_grad[None])


def on_device(tokens, out_grad, expert_ids, gates, w_gate, w_up, w_down):
    if lax.axis_size("dp") == 2:
        return on_pair(tokens, out_grad, expert_ids, gates, w_gate, w_up, w_down)
    experts = lax.axis_size("expert")
    width = tokens.shape[1]
    per_token = expert_ids.shape[1]
    hidden = w_gate.shape[2]
    depth = 3 * expert_ids.size // experts
    slots = experts * depth

    joined = lax.all_gather(
        jnp.concatenate([w_gate[0], w_up[0]], axis=1), "dp", axis=0, tiled=True
    )
    down = lax.all_gather(w_down[0], "dp", axis=1, tiled=True)
    place = place_matrix(expert_ids, experts, depth)

    def dispatch(table):
        sent = dot(place, table, (1, 0)).astype(BF16).reshape(experts, depth, width)
        return exchange(sent, "expert").reshape(slots, width)

    rows_in = dispatch(token_rows(tokens, per_token))
    grads_in = dispatch(scaled_rows(out_grad, gates))
    preact = dot(rows_in, joined, (1, 0))
    activated, sides = sides_of(
        preact[:, :hidden], preact[:, hidden:], dot(grads_in, down, (1, 1))
    )
    slot_grad = dot(sides, joined, (1, 1)).astype(BF16)
    returned = exchange(slot_grad.reshape(experts, depth, width), "expert").reshape(slots, width)
    down_grad = lax.psum(dot(activated, grads_in, (0, 0)).astype(BF16), "dp")
    joined_grad = lax.psum_scatter(
        dot(rows_in, sides, (0, 0)).astype(BF16), "dp", scatter_dimension=0, tiled=True
    )
    input_grad = sum_choices(dot(place, returned, (0, 0)), per_token)
    return (
        input_grad,
        joined_grad[:, :hidden][None],
        joined_grad[:, hidden:][None],
        down_grad[None],
    )


def solution(mesh):
    rows = P(BOTH, None)
    in_specs = (
        rows,
        rows,
        rows,
        rows,
        P("expert", "dp", None),
        P("expert", "dp", None),
        P("expert", None, "dp"),
    )
    out_specs = (
        rows,
        P("expert", "dp", None),
        P("expert", "dp", None),
        P("expert", None, None),
    )
    return jax.shard_map(
        on_device, mesh=mesh, in_specs=in_specs, out_specs=out_specs, check_vma=False
    )
```

time: 164 us -> 150 us (0.915); the launches traced: 161 us -> 149 us
  Pallas kernels: 0 us -> 21.3 us
  waiting for transfers between devices: 110 us -> 94.2 us
  matrix products: 14.5 us -> 3.76 us
  other arithmetic: 6.52 us -> 0.04 us
  starting transfers between devices: 20.6 us -> 24.2 us
  local copies, waits for them, and re-layouts: 7.75 us -> 4.69 us
    all_to_all x3, waiting for transfers between devices: 62.1 us -> 4.83 us  [exchange(): return lax.all_to_all(x, axes, split_axis=0, concat_axis=0, tiled=True)]
    ppermute x3 -> x6, waiting for transfers between devices: 48.4 us -> 89.4 us  [swap(): return lax.ppermute(x, 'dp', [(0, 1), (1, 0)])]
    pallas_call x0 -> x5, Pallas kernels: none -> 21.3 us  [call(): pl.pallas_call(kernel, out_shape=list(out_shapes), in_specs=[IN_HBM] * le...]
    dot_general x14 -> x2, matrix products: 14.5 us -> 3.76 us  [dot(): lax.dot_general(a, b, ((contract[:1], contract[1:]), ((), ())), preferred...]
    another operation x2 -> x0, other arithmetic: 2.57 us -> none  [dispatch(): jnp.stack([dot(place, halves[:, part], (1, 0)).astype(BF16) for part in r...]
    ppermute x3 -> x6, starting transfers between devices: 2.81 us -> 4.92 us  [swap(): return lax.ppermute(x, 'dp', [(0, 1), (1, 0)])]
    unnamed x24 -> x20, local copies, waits for them, and re-layouts: 4.69 us -> 3.51 us
  transfers between devices with their start and end apart: 6 -> 9, of which waited for: 5 -> 7; matrix products, arithmetic and copies ran while one was open for 9% -> 3% of each run, Pallas kernels for 0% -> 6%
where the time goes in v2:
time: 150 us; the launch traced here: 149 us
  waiting for transfers between devices  94.2 us (63%)
  starting transfers between devices  24.2 us (16%)
  Pallas kernels  21.3 us (14%)
  local copies, waits for them, and re-layouts  4.69 us (3%)
  matrix products  3.76 us (3%)
    ppermute x6, waiting for transfers between devices, swap(): return lax.ppermute(x, 'dp', [(0, 1), (1, 0)])  89.4 us
    pallas_call x5, Pallas kernels, call(): pl.pallas_call(kernel, out_shape=list(out_shapes), in_specs=[IN_HBM] * le...  21.3 us
    all_to_all x3, starting transfers between devices, exchange(): return lax.all_to_all(x, axes, split_axis=0, concat_axis=0, tiled=True)  19.3 us
    ppermute x6, starting transfers between devices, swap(): return lax.ppermute(x, 'dp', [(0, 1), (1, 0)])  4.92 us
    all_to_all x3, waiting for transfers between devices, exchange(): return lax.all_to_all(x, axes, split_axis=0, concat_axis=0, tiled=True)  4.83 us
    dot_general x2, matrix products, dot(): lax.dot_general(a, b, ((contract[:1], contract[1:]), ((), ())), preferred...  3.76 us
    unnamed x20, local copies, waits for them, and re-layouts  3.51 us
  transfers between devices with their start and end apart: 9, of which 7 were waited for; matrix products, arithmetic and copies ran while one was open for 3% of the time, Pallas kernels for 6%

profile of v2, /device:TPU:13, one launch (start us, length us, event | category | flops | bytes accessed | tf_op | source)
XLA Modules:
  0.0 148.9 jit_solution(8928860466865132411)
XLA Ops:
  0.6 0.0 copy-start
  0.6 2.8 %shard_map.102 = (bf16[384,128]{1,0:T(8,128)(2,1)}, bf16[768,1024]{1,0:T(8,128)(2,1)}) custom-call(s32[1,128]{1,0:T(1,128)} %bitcast.28, f32[1,128]{1,0:T(1,128)} %bitcast.29, bf16[128,2048]{1,0:T(8,128)(2,1)} %grad_hbm.1), custom_call_target="tpu_custom_call" | custom-call | flops 201326592 | bytes 2196480 | tf_op jit(solution)/shard_map/pallas_call | solution.py:84
  3.4 0.0 copy-start.3
  3.4 0.0 copy-start.4
  3.5 6.3 %all-to-all-start = ((bf16[32,24,1024]{2,1,0:T(8,128)(2,1)}), bf16[32,24,1024]{2,1,0:T(8,128)(2,1)S(1)}, u32[]{:S(2)}, u32[]{:S(2)}) async-start(bf16[32,24,1024]{2,1,0:T(8,128)(2,1)} %bitcast.22), calls=%async_computation | async-start | bytes 3145728 | tf_op jit(solution)/shard_map/all_to_all | solution.py:25
  9.8 1.2 collective-permute-start
  11.0 0.0 copy-done.3
  11.1 0.0 copy-done.4
  11.1 1.7 %convolution_convert_fusion = bf16[384,2048]{1,0:T(8,128)(2,1)} fusion(bf16[384,128]{1,0:T(8,128)(2,1)S(1)} %copy-done.4, bf16[128,1024]{1,0:T(8,128)(2,1)S(1)} %get-tuple-element.35, bf16[128,1024]{1,0:T(8,128)(2,1)S(1)} %get-tuple-element.34), kind=kOutput, calls=%fused_computation | convolution fusion | flops 203161600 | bytes 2195456 | tf_op jit(solution)/shard_map/dot_general | solution.py:17
  12.8 32.8 %collective-permute-done.other_gate_hbm = bf16[1024,384]{1,0:T(8,128)(2,1)} collective-permute-done((bf16[1024,384]{1,0:T(8,128)(2,1)}, bf16[1024,384]{1,0:T(8,128)(2,1)}, u32[]{:S(2)}, u32[]{:S(2)}) %collective-permute-start) | collective-permute-done | bytes 786464 | tf_op jit(solution)/shard_map/ppermute | solution.py:21
  45.6 0.0 all-to-all-done
  45.6 0.0 copy-start.1
  45.6 0.0 copy-start.5
  45.6 7.6 %all-to-all-start.1 = ((bf16[16,24,2048]{2,1,0:T(8,128)(2,1)}), bf16[16,24,2048]{2,1,0:T(8,128)(2,1)}, u32[]{:S(2)}, u32[]{:S(2)}) async-start(bf16[16,24,2048]{2,1,0:T(8,128)(2,1)} %bitcast.4), calls=%async_computation.1 | async-start | bytes 3145728 | tf_op jit(solution)/shard_map/all_to_all | solution.py:25
  53.2 0.0 copy-done.5
  53.2 0.5 collective-permute-start.1
  53.8 0.0 copy-done.1
  53.8 0.0 copy-done
  53.8 2.1 %fusion.6 = (bf16[768,384]{1,0:T(8,128)(2,1)S(1)}, f32[768,384]{1,0:T(8,128)}) fusion(bf16[768,1024]{1,0:T(8,128)(2,1)S(1)} %bitcast.20, bf16[1,384,1024]{2,1,0:T(8,128)(2,1)S(1)} %copy-done), kind=kOutput, calls=%fused_computation.9 | convolution fusion | flops 604274688 | bytes 4128768 | tf_op jit(solution)/shard_map/dot_general | solution.py:17
  55.8 1.0 collective-permute-start.2
  56.8 15.2 %collective-permute-done.1.other_up_hbm = bf16[1024,384]{1,0:T(8,128)(2,1)S(1)} collective-permute-done((bf16[1024,384]{1,0:T(8,128)(2,1)S(1)}, bf16[1024,384]{1,0:T(8,128)(2,1)S(1)}, u32[]{:S(2)}, u32[]{:S(2)}) %collective-permute-start.1) | collective-permute-done | bytes 786464 | tf_op jit(solution)/shard_map/ppermute | solution.py:21
  72.1 0.0 copy-start.7
  72.1 0.9 copy-done.7
  72.9 11.8 %collective-permute-done.2.remote_hbm = bf16[768,384]{1,0:T(8,128)(2,1)S(1)} collective-permute-done((bf16[768,384]{1,0:T(8,128)(2,1)S(1)}, bf16[768,384]{1,0:T(8,128)(2,1)S(1)}, u32[]{:S(2)}, u32[]{:S(2)}) %collective-permute-start.2) | collective-permute-done | bytes 589856 | tf_op jit(solution)/shard_map/ppermute | solution.py:21
  84.7 0.0 copy-start.8
  84.7 4.8 %all-to-all-done.1 = bf16[16,24,2048]{2,1,0:T(8,128)(2,1)} async-done(((bf16[16,24,2048]{2,1,0:T(8,128)(2,1)}), bf16[16,24,2048]{2,1,0:T(8,128)(2,1)}, u32[]{:S(2)}, u32[]{:S(2)}) %all-to-all-start.1) | async-done | bytes 1572896 | tf_op jit(solution)/shard_map/all_to_all | solution.py:25
  89.5 0.0 copy-done.8
  89.5 6.8 %shard_map.103 = (bf16[384,768]{1,0:T(8,128)(2,1)}, bf16[384,384]{1,0:T(8,128)(2,1)}, bf16[384,768]{1,0:T(8,128)(2,1)}, bf16[384,2048]{1,0:T(8,128)(2,1)}) custom-call(bf16[384,2048]{1,0:T(8,128)(2,1)} %bitcast.5.rows_hbm, bf16[1024,384]{1,0:T(8,128)(2,1)} %bitcast.25, bf16[1024,384]{1,0:T(8,128)(2,1)} %bitcast.26, ...), custom_call_target="tpu_custom_call" | custom-call | flops 2415919104 | bytes 9535488 | tf_op jit(solution)/shard_map/pallas_call | solution.py:84
  96.3 0.5 collective-permute-start.3
  96.8 1.2 slice.12
  98.0 1.1 collective-permute-start.5
  99.1 5.4 %all-to-all-start.2 = ((bf16[16,24,2048]{2,1,0:T(8,128)(2,1)}), bf16[16,24,2048]{2,1,0:T(8,128)(2,1)}, u32[]{:S(2)}, u32[]{:S(2)}) async-start(bf16[16,24,2048]{2,1,0:T(8,128)(2,1)} %bitcast.9), calls=%async_computation.2 | async-start | bytes 3145728 | tf_op jit(solution)/shard_map/all_to_all | solution.py:25
  104.5 6.9 %collective-permute-done.3.pre_hbm = bf16[384,768]{1,0:T(8,128)(2,1)S(1)} collective-permute-done((bf16[384,768]{1,0:T(8,128)(2,1)}, bf16[384,768]{1,0:T(8,128)(2,1)S(1)}, u32[]{:S(2)}, u32[]{:S(2)}) %collective-permute-start.3) | collective-permute-done | bytes 589856 | tf_op jit(solution)/shard_map/ppermute | solution.py:21
  111.4 0.0 copy-start.9
  111.4 0.8 copy-done.9
  112.2 3.9 %shard_map.104 = (bf16[384,1024]{1,0:T(8,128)(2,1)}, bf16[384,768]{1,0:T(8,128)(2,1)}) custom-call(bf16[384,768]{1,0:T(8,128)(2,1)} %copy-done.9, f32[768,384]{1,0:T(8,128)} %get-tuple-element.37.partial_hbm, bf16[768,384]{1,0:T(8,128)(2,1)} %copy-done.8, bf16[384,384]{1,0:T(8,128)(2,1)} %get-tuple-element.26.act_hbm, bf16[768,1024]{1,0:T(8,128)(2,1)} %bitcast.21), custom_call_target="tpu_custom_call" | custom-call | flops 99999997952 | bytes 5603328 | tf_op jit(solution)/shard_map/pallas_call | solution.py:84
  116.1 0.6 collective-permute-start.4
  116.6 11.6 %collective-permute-done.5.other_rows_hbm = bf16[384,1024]{1,0:T(8,128)(2,1)S(1)} collective-permute-done((bf16[384,1024]{1,0:T(8,128)(2,1)S(1)}, bf16[384,1024]{1,0:T(8,128)(2,1)S(1)}, u32[]{:S(2)}, u32[]{:S(2)}) %collective-permute-start.5) | collective-permute-done | bytes 786464 | tf_op jit(solution)/shard_map/ppermute | solution.py:21
  128.2 0.0 copy-start.6
  128.2 0.9 copy-done.6
  129.1 4.8 %shard_map.106 = (bf16[1024,384]{1,0:T(8,128)(2,1)}, bf16[1024,384]{1,0:T(8,128)(2,1)}) custom-call(bf16[384,2048]{1,0:T(8,128)(2,1)} %bitcast.5.rows_hbm, bf16[384,1024]{1,0:T(8,128)(2,1)} %copy-done.6, bf16[384,768]{1,0:T(8,128)(2,1)} %get-tuple-element.29.sides_hbm, bf16[384,768]{1,0:T(8,128)(2,1)} %get-tuple-element.30.other_sides_hbm), custom_call_target="tpu_custom_call" | custom-call | flops 99999997952 | bytes 5111808 | tf_op jit(solution)/shard_map/pallas_call | solution.py:84
  134.0 11.0 %collective-permute-done.4.other_hbm = bf16[384,1024]{1,0:T(8,128)(2,1)S(1)} collective-permute-done((bf16[384,1024]{1,0:T(8,128)(2,1)}, bf16[384,1024]{1,0:T(8,128)(2,1)S(1)}, u32[]{:S(2)}, u32[]{:S(2)}) %collective-permute-start.4) | collective-permute-done | bytes 786464 | tf_op jit(solution)/shard_map/ppermute | solution.py:21
  145.0 0.0 copy-start.2
  145.0 0.0 all-to-all-done.2
  145.0 0.9 copy-done.2
  145.9 3.0 %shard_map.105 = (bf16[128,2048]{1,0:T(8,128)(2,1)}, bf16[384,2048]{1,0:T(8,128)(2,1)}) custom-call(bf16[384,128]{1,0:T(8,128)(2,1)} %get-tuple-element.19.place_hbm, bf16[384,2048]{1,0:T(8,128)(2,1)} %bitcast.10.returned_hbm, bf16[384,1024]{1,0:T(8,128)(2,1)} %get-tuple-element.27.own_hbm, bf16[384,1024]{1,0:T(8,128)(2,1)} %copy-done.2), custom_call_target="tpu_custom_call" | custom-call | flops 201326592 | bytes 5341184 | tf_op jit(solution)/shard_map/pallas_call | solution.py:84
  (1 shorter events, 0.0 us)
Async XLA Ops:
  0.6 53.1 %copy-start = (bf16[1,384,1024]{2,1,0:T(8,128)(2,1)S(1)}, bf16[1,384,1024]{2,1,0:T(8,128)(2,1)}, u32[]{:S(2)}) copy-start(bf16[1,384,1024]{2,1,0:T(8,128)(2,1)} %param.13) | copy-start | bytes 2359300
  3.4 7.6 %copy-start.3 = (bf16[128,2048]{1,0:T(8,128)(2,1)S(1)}, bf16[128,2048]{1,0:T(8,128)(2,1)}, u32[]{:S(2)}) copy-start(bf16[128,2048]{1,0:T(8,128)(2,1)} %param.7) | copy-start | bytes 1572868
  3.4 7.6 %copy-start.4 = (bf16[384,128]{1,0:T(8,128)(2,1)S(1)}, bf16[384,128]{1,0:T(8,128)(2,1)}, u32[]{:S(2)}) copy-start(bf16[384,128]{1,0:T(8,128)(2,1)} %get-tuple-element.19.place_hbm) | copy-start | bytes 294916
  3.5 42.2 %all-to-all-start = ((bf16[32,24,1024]{2,1,0:T(8,128)(2,1)}), bf16[32,24,1024]{2,1,0:T(8,128)(2,1)S(1)}, u32[]{:S(2)}, u32[]{:S(2)}) async-start(bf16[32,24,1024]{2,1,0:T(8,128)(2,1)} %bitcast.22), calls=%async_computation | async-start | bytes 3145728 | tf_op jit(solution)/shard_map/all_to_all | solution.py:25
  9.8 35.9 %collective-permute-start = (bf16[1024,384]{1,0:T(8,128)(2,1)}, bf16[1024,384]{1,0:T(8,128)(2,1)}, u32[]{:S(2)}, u32[]{:S(2)}) collective-permute-start(bf16[1024,384]{1,0:T(8,128)(2,1)} %bitcast.24), channel_id=1, source_target_pairs={{0,16},{16,0},{1,17},{17,1},{2,18},{18,2},{3,19},{19,3},{4,20},{20... | collective-permute-start | bytes 2359304 | tf_op jit(solution)/shard_map/ppermute | solution.py:21
  45.6 8.1 %copy-start.1 = (bf16[32,24,1024]{2,1,0:T(8,128)(2,1)}, bf16[32,24,1024]{2,1,0:T(8,128)(2,1)S(1)}, u32[]{:S(2)}) copy-start(bf16[32,24,1024]{2,1,0:T(8,128)(2,1)S(1)} %all-to-all-done) | copy-start | bytes 4718596
  45.6 7.6 %copy-start.5 = (bf16[1,1024,384]{2,1,0:T(8,128)(2,1)S(1)}, bf16[1,1024,384]{2,1,0:T(8,128)(2,1)}, u32[]{:S(2)}) copy-start(bf16[1,1024,384]{2,1,0:T(8,128)(2,1)} %param.12) | copy-start | bytes 2359300
  45.6 43.9 %all-to-all-start.1 = ((bf16[16,24,2048]{2,1,0:T(8,128)(2,1)}), bf16[16,24,2048]{2,1,0:T(8,128)(2,1)}, u32[]{:S(2)}, u32[]{:S(2)}) async-start(bf16[16,24,2048]{2,1,0:T(8,128)(2,1)} %bitcast.4), calls=%async_computation.1 | async-start | bytes 3145728 | tf_op jit(solution)/shard_map/all_to_all | solution.py:25
  53.2 18.8 %collective-permute-start.1 = (bf16[1024,384]{1,0:T(8,128)(2,1)S(1)}, bf16[1024,384]{1,0:T(8,128)(2,1)S(1)}, u32[]{:S(2)}, u32[]{:S(2)}) collective-permute-start(bf16[1024,384]{1,0:T(8,128)(2,1)S(1)} %bitcast.27), channel_id=1, source_target_pairs={{0,16},{16,0},{1,17},{17,1},{2,18},{18,2},{3,19},{19,3},{4,20},{20... | collective-permute-start | bytes 2359304 | tf_op jit(solution)/shard_map/ppermute | solution.py:21
  55.8 28.9 %collective-permute-start.2 = (bf16[768,384]{1,0:T(8,128)(2,1)S(1)}, bf16[768,384]{1,0:T(8,128)(2,1)S(1)}, u32[]{:S(2)}, u32[]{:S(2)}) collective-permute-start(bf16[768,384]{1,0:T(8,128)(2,1)S(1)} %get-tuple-element.36), channel_id=1, source_target_pairs={{0,16},{16,0},{1,17},{17,1},{2,18},{18,2},{3,19},{19,3},{4,20},{20... | collective-permute-start | bytes 1769480 | tf_op jit(solution)/shard_map/ppermute | solution.py:21
  72.1 0.9 copy-start.7
  84.7 4.8 %copy-start.8 = (bf16[768,384]{1,0:T(8,128)(2,1)}, bf16[768,384]{1,0:T(8,128)(2,1)S(1)}, u32[]{:S(2)}) copy-start(bf16[768,384]{1,0:T(8,128)(2,1)S(1)} %collective-permute-done.2.remote_hbm) | copy-start | bytes 1769476
  96.3 15.1 %collective-permute-start.3 = (bf16[384,768]{1,0:T(8,128)(2,1)}, bf16[384,768]{1,0:T(8,128)(2,1)S(1)}, u32[]{:S(2)}, u32[]{:S(2)}) collective-permute-start(bf16[384,768]{1,0:T(8,128)(2,1)} %get-tuple-element.25), channel_id=1, source_target_pairs={{0,16},{16,0},{1,17},{17,1},{2,18},{18,2},{3,19},{19,3},{4,20},{20... | collective-permute-start | bytes 1769480 | tf_op jit(solution)/shard_map/ppermute | solution.py:21
  98.0 30.2 %collective-permute-start.5 = (bf16[384,1024]{1,0:T(8,128)(2,1)S(1)}, bf16[384,1024]{1,0:T(8,128)(2,1)S(1)}, u32[]{:S(2)}, u32[]{:S(2)}) collective-permute-start(bf16[384,1024]{1,0:T(8,128)(2,1)S(1)} %slice.12), channel_id=1, source_target_pairs={{0,16},{16,0},{1,17},{17,1},{2,18},{18,2},{3,19},{19,3},{4,20},{20... | collective-permute-start | bytes 2359304 | tf_op jit(solution)/shard_map/ppermute | solution.py:21
  99.1 45.9 %all-to-all-start.2 = ((bf16[16,24,2048]{2,1,0:T(8,128)(2,1)}), bf16[16,24,2048]{2,1,0:T(8,128)(2,1)}, u32[]{:S(2)}, u32[]{:S(2)}) async-start(bf16[16,24,2048]{2,1,0:T(8,128)(2,1)} %bitcast.9), calls=%async_computation.2 | async-start | bytes 3145728 | tf_op jit(solution)/shard_map/all_to_all | solution.py:25
  111.4 0.8 copy-start.9
  116.1 28.9 %collective-permute-start.4 = (bf16[384,1024]{1,0:T(8,128)(2,1)}, bf16[384,1024]{1,0:T(8,128)(2,1)S(1)}, u32[]{:S(2)}, u32[]{:S(2)}) collective-permute-start(bf16[384,1024]{1,0:T(8,128)(2,1)} %get-tuple-element.27.own_hbm), channel_id=1, source_target_pairs={{0,16},{16,0},{1,17},{17,1},{2,18},{18,2},{3,19},{19,3},{4,20},{20... | collective-permute-start | bytes 2359304 | tf_op jit(solution)/shard_map/ppermute | solution.py:21
  128.2 0.9 copy-start.6
  145.0 0.9 copy-start.2

commit v3 on v2

v3 whole, which is shorter than its diff:
```python
import functools

import jax
import jax.numpy as jnp
from jax import lax
from jax.experimental import pallas as pl
from jax.experimental.pallas import tpu as pltpu
from jax.sharding import PartitionSpec as P

BF16 = jnp.bfloat16
F32 = jnp.float32
BOTH = ("dp", "expert")
LATE_FLOPS = 100_000_000_000
LANES = 128


def dot(a, b, contract):
    return lax.dot_general(a, b, ((contract[:1], contract[1:]), ((), ())), preferred_element_type=F32)


def swap(x):
    return lax.ppermute(x, "dp", [(0, 1), (1, 0)])


def exchange(x, axes):
    return lax.all_to_all(x, axes, split_axis=0, concat_axis=0, tiled=True)


def place_matrix(expert_ids, experts, depth):
    entries = expert_ids.size
    flat_ids = expert_ids.reshape(entries)
    order = jnp.arange(entries, dtype=jnp.int32)
    onehot = (flat_ids[:, None] == jnp.arange(experts, dtype=jnp.int32)[None, :]).astype(BF16)
    earlier = (order[None, :] < order[:, None]).astype(BF16)
    before = dot(earlier, onehot, (1, 0))
    ranking = jnp.sum(before * onehot.astype(F32), axis=1).astype(jnp.int32)
    slot_of_entry = flat_ids * depth + ranking
    return (
        jnp.arange(experts * depth, dtype=jnp.int32)[:, None] == slot_of_entry[None, :]
    ).astype(BF16)


def sides_of(gate_pre, up_pre, hidden_grad):
    sigmoid = jax.nn.sigmoid(gate_pre)
    silu_value = gate_pre * sigmoid
    activated = (silu_value * up_pre).astype(BF16)
    gate_side = (hidden_grad * up_pre * sigmoid * (1.0 + gate_pre * (1.0 - sigmoid))).astype(BF16)
    up_side = (hidden_grad * silu_value).astype(BF16)
    return activated, jnp.concatenate([gate_side, up_side], axis=1)


def sum_parts(first, second):
    return (first.astype(BF16).astype(F32) + second.astype(BF16).astype(F32)).astype(BF16)


def scaled_rows(out_grad, gates):
    return (
        (gates[:, :, None] * out_grad.astype(F32)[:, None, :])
        .astype(BF16)
        .reshape(gates.size, out_grad.shape[1])
    )


def token_rows(tokens, per_token):
    return jnp.repeat(tokens, per_token, axis=0) if per_token > 1 else tokens


def sum_choices(picked, per_token):
    if per_token > 1:
        picked = jnp.sum(picked.reshape(-1, per_token, picked.shape[1]).astype(F32), axis=1)
    return picked.astype(BF16)


MIB = 1 << 20
IN_HBM = pl.BlockSpec(memory_space=pltpu.HBM)


def shape(*dims, dtype=BF16):
    return jax.ShapeDtypeStruct(dims, dtype)


def call(kernel, out_shapes, scratch, copies, flops, *operands):
    moved = sum(x.size * x.dtype.itemsize for x in operands)
    moved += sum(x.size * x.dtype.itemsize for x in out_shapes)
    return pl.pallas_call(
        kernel,
        out_shape=list(out_shapes),
        in_specs=[IN_HBM] * len(operands),
        out_specs=[IN_HBM] * len(out_shapes),
        scratch_shapes=[pltpu.VMEM(x.shape, x.dtype) for x in scratch]
        + [pltpu.SemaphoreType.DMA((copies,))],
        compiler_params=pltpu.CompilerParams(vmem_limit_bytes=64 * MIB),
        cost_estimate=pl.CostEstimate(flops=flops, bytes_accessed=moved, transcendentals=0),
    )(*operands)


class Mover:
    def __init__(self, semaphores):
        self.semaphores, self.count = semaphores, 0

    def start(self, source, target):
        copy = pltpu.make_async_copy(source, target, self.semaphores.at[self.count])
        self.count += 1
        copy.start()
        return copy


def wait(*copies):
    for copy in copies:
        copy.wait()


def half_at(index, half):
    return pl.ds(pl.multiple_of(index * half, half), half)


def zero_one(condition):
    return condition.astype(F32).astype(BF16)


def lane_row(count):
    return lax.broadcasted_iota(jnp.int32, (1, count), 1)


def row_index(rows, columns):
    return lax.broadcasted_iota(jnp.int32, (rows, columns), 0)


def with_mark(rows, mark):
    return jnp.concatenate([rows, jnp.broadcast_to(mark, (rows.shape[0], LANES))], axis=1).astype(BF16)


def ranks(ids, experts):
    entries = ids.shape[1]
    onehot = (row_index(experts, entries) == ids).astype(F32)
    earlier = zero_one(
        row_index(entries, entries) < lax.broadcasted_iota(jnp.int32, (entries, entries), 1)
    )
    before = dot(onehot.astype(BF16), earlier, (1, 0))
    return jnp.sum(before * onehot, axis=0, keepdims=True).astype(jnp.int32)


def scaled_half(grad, gates):
    entries = grad.shape[0]
    weight = jnp.broadcast_to(gates, (entries, entries)).T[:, :1]
    return (weight * grad.astype(F32)).astype(BF16)


def kernel_inputs(
    experts, depth, base,
    ids_hbm, gates_hbm, tokens_hbm, grad_hbm,
    send_hbm, pool_hbm, place_hbm, marks_hbm, scaled_hbm,
    ids, gates, tokens, grad, send, pool, place, marks, scaled, sems,
):
    entries = ids.shape[1]
    half = tokens.shape[1] // 2
    extra = depth - base
    me = lax.axis_index("dp")
    move = Mover(sems)
    small = [move.start(ids_hbm, ids), move.start(gates_hbm, gates)]
    loads = [
        move.start(
            tokens_hbm.at[:, half_at(where, half)], tokens.at[:, pl.ds(part * half, half)]
        )
        for part, where in enumerate((me, 1 - me))
    ]
    grads = move.start(grad_hbm.at[:, half_at(1 - me, half)], grad)
    wait(*small)
    rank = ranks(ids[...], experts)
    over = rank >= base
    kept_slot = jnp.where(over, -1, ids[...] * base + rank)
    into = zero_one(row_index(experts * base, entries) == kept_slot)
    position = jnp.where(over, rank - base, -extra - 1)
    row = row_index(2 * extra, entries)
    stores = []
    pooled = 0.0
    for part in range(2):
        wait(loads[part])
        columns = slice(part * half, (part + 1) * half)
        table = tokens[:, columns]
        send[:, columns] = dot(into, table, (1, 0)).astype(BF16)
        stores.append(
            move.start(
                send.at[:, pl.ds(part * half, half)], send_hbm.at[:, pl.ds(part * half, half)]
            )
        )
        pooled = pooled + dot(zero_one(row == position + part * extra), table, (1, 0))
    pool[...] = with_mark(pooled, jnp.zeros((1, 1), F32))
    place[...] = zero_one(row_index(experts * depth, entries) == ids[...] * depth + rank)
    is_hot = jnp.max(jnp.where(over, ids[...], -1)) == lax.axis_index("expert")
    marks[...] = jnp.broadcast_to(is_hot.astype(F32), marks.shape)
    wait(grads)
    scaled[:entries] = scaled_half(grad[...], gates[...])
    scaled[entries:] = jnp.broadcast_to(
        jnp.concatenate(
            [ids[...].astype(F32), jnp.zeros((1, half - entries), F32)], axis=1
        ),
        (scaled.shape[0] - entries, half),
    ).astype(BF16)
    stores += [
        move.start(source, target)
        for source, target in (
            (scaled, scaled_hbm),
            (pool, pool_hbm),
            (place, place_hbm),
            (marks, marks_hbm),
        )
    ]
    wait(*stores)


def kernel_grads(
    experts, depth, base,
    ids_hbm, gates_hbm, grad_hbm, other_hbm,
    theirs_hbm, own_hbm, pool_hbm,
    ids, gates, grad, other, theirs, own, pool, sems,
):
    entries = ids.shape[1]
    extra = depth - base
    half = grad.shape[1]
    me = lax.axis_index("dp")
    move = Mover(sems)
    loads = [
        move.start(source, target)
        for source, target in (
            (other_hbm, other),
            (ids_hbm, ids),
            (gates_hbm, gates),
            (grad_hbm.at[:, half_at(me, half)], grad),
        )
    ]
    wait(*loads)
    row = row_index(2 * extra, entries)
    pooled, mark = 0.0, 0.0
    stores = []
    for which, target, out in ((1, theirs, theirs_hbm), (0, own, own_hbm)):
        if which == 0:
            of, rows = ids[...], scaled_half(grad[...], gates[...])
        else:
            of = other[entries:, :entries].astype(F32)[:1].astype(jnp.int32)
            rows = other[:entries]
        rank = ranks(of, experts)
        over = rank >= base
        slot = jnp.where(over, -1, of * base + rank)
        position = jnp.where(over, rank - base, -extra - 1)
        target[...] = dot(zero_one(row_index(experts * base, entries) == slot), rows, (1, 0)).astype(BF16)
        stores.append(move.start(target, out))
        pooled = pooled + dot(zero_one(row == position + which * extra), rows, (1, 0))
        crowded = jnp.sum(over.astype(F32), axis=1, keepdims=True) > extra
        mark = mark + crowded.astype(F32)
    pool[...] = with_mark(pooled, mark)
    wait(move.start(pool, pool_hbm), *stores)


def pool_rows(pool, marks, which, extra, half):
    sources = pool.shape[0] // (4 * extra)
    rows = row_index(sources * extra, pool.shape[0])
    columns = lax.broadcasted_iota(jnp.int32, (sources * extra, pool.shape[0]), 1)
    source = lax.shift_right_logical(rows, extra.bit_length() - 1) ^ lax.axis_index("expert")
    target = source * (4 * extra) + which * extra + (rows & (extra - 1))
    select = ((columns == target).astype(F32) * marks[0:1, 0:1]).astype(BF16)
    return dot(select, pool[:, :half], (1, 0)).astype(BF16)


def weight_copies(move, joined, own, other):
    half, hidden = own[0].shape
    return [
        [
            move.start(source, joined.at[pl.ds(at, half), pl.ds(part * hidden, hidden)])
            for part, source in enumerate(pair)
        ]
        for at, pair in ((0, own), (half, other))
    ]


def kernel_base(
    rows_hbm, gate_hbm, up_hbm, other_gate_hbm, other_up_hbm,
    pre_hbm, sent_hbm,
    rows, joined, pre_at, sent, sems,
):
    half = joined.shape[0] // 2
    move = Mover(sems)
    weights = weight_copies(move, joined, (gate_hbm, up_hbm), (other_gate_hbm, other_up_hbm))
    loads = [
        move.start(rows_hbm.at[:, pl.ds(part * half, half)], rows.at[:, pl.ds(part * half, half)])
        for part in range(2)
    ]
    wait(loads[0], *weights[0])
    pre = dot(rows[:, :half], joined[:half], (1, 0))
    wait(loads[1], *weights[1])
    pre = pre + dot(rows[:, half:], joined[half:], (1, 0))
    pre_at[...] = pre
    sent[...] = pre.astype(BF16)
    wait(move.start(sent, sent_hbm), move.start(pre_at, pre_hbm))


def kernel_late(
    extra,
    pool_hbm, marks_hbm, hidden_hbm, gate_hbm, up_hbm, other_gate_hbm, other_up_hbm,
    pre_hbm, late_hbm, packet_hbm,
    pool, marks, joined, pre_at, rows, packet, sems,
):
    half = joined.shape[0] // 2
    both = joined.shape[1]
    late = rows.shape[0]
    move = Mover(sems)
    pooled = [move.start(pool_hbm, pool), move.start(marks_hbm, marks)]
    weights = weight_copies(move, joined, (gate_hbm, up_hbm), (other_gate_hbm, other_up_hbm))
    wait(*pooled)
    rows[...] = pool_rows(pool, marks, 0, extra, half)
    packet[:late] = pool_rows(pool, marks, 1, extra, half)
    stores = [move.start(rows, late_hbm)]
    wait(*weights[0])
    pre = dot(rows[...], joined[:half], (1, 0))
    wait(*weights[1])
    pre = pre + dot(packet[:late], joined[half:], (1, 0))
    pre_at[...] = pre
    stores.append(move.start(pre_at, pre_hbm))
    packet[late : 2 * late, :both] = pre.astype(BF16)
    packet[late : 2 * late, both:] = jnp.zeros((late, half - both), BF16)
    mark = jnp.max(pool[:, half:].astype(F32), axis=0, keepdims=True)[:, :1]
    packet[2 * late :] = jnp.broadcast_to(mark, (packet.shape[0] - 2 * late, half)).astype(BF16)
    stores.append(move.start(packet, packet_hbm))
    wait(*stores)


def kernel_hidden(
    extra,
    recv_hbm, pool_hbm, marks_hbm, down_hbm, _rows_hbm,
    sent_hbm, grads_hbm,
    pool, marks, down, grads, sent, sems,
):
    half = down.shape[1]
    kept = recv_hbm.shape[0]
    move = Mover(sems)
    load = move.start(recv_hbm, grads.at[pl.ds(0, kept)])
    small = [
        move.start(source, target)
        for source, target in ((pool_hbm, pool), (marks_hbm, marks), (down_hbm, down))
    ]
    wait(*small)
    grads[kept:] = pool_rows(pool, marks, 3, extra, half)
    wait(load)
    sent[...] = dot(grads[...], down[...], (1, 1)).astype(BF16)
    wait(move.start(sent, sent_hbm), move.start(grads, grads_hbm))


def kernel_stack(pool_hbm, received_hbm, _one_hbm, _other_hbm, stacked_hbm, pool, sems):
    move = Mover(sems)
    wait(
        *[
            move.start(source, pool.at[:, part])
            for part, source in enumerate((pool_hbm, received_hbm))
        ]
    )
    wait(move.start(pool, stacked_hbm))


def kernel_slot(
    base, depth,
    recv_hbm, pool_hbm, marks_hbm, down_hbm, remote_hbm, pre_hbm, late_pre_hbm,
    gate_hbm, up_hbm, other_gate_hbm, other_up_hbm,
    slot_hbm, act_hbm, sides_hbm, hidden_hbm, grads_hbm,
    pool, marks, down, remote, pre, joined, slot, act, sides, hidden_at, grads, sems,
):
    slots, hidden = act.shape
    half = grads.shape[1]
    extra = depth - base
    kept = recv_hbm.shape[0]
    move = Mover(sems)
    load = move.start(recv_hbm, grads.at[pl.ds(0, kept)])
    first = [
        move.start(source, target)
        for source, target in ((pool_hbm, pool), (marks_hbm, marks), (down_hbm, down))
    ]
    second = [
        move.start(source, target)
        for source, target in (
            (remote_hbm, remote),
            (pre_hbm, pre.at[pl.ds(0, kept)]),
            (late_pre_hbm, pre.at[pl.ds(kept, slots - kept)]),
        )
    ]
    weights = weight_copies(move, joined, (gate_hbm, up_hbm), (other_gate_hbm, other_up_hbm))
    wait(*first)
    grads[kept:] = pool_rows(pool, marks, 2, extra, half)
    wait(load)
    stores = [move.start(grads, grads_hbm)]
    hidden_grad = dot(grads[...], down[...], (1, 1))
    wait(*second)
    hidden_grad = hidden_grad + remote[...].astype(F32)
    hidden_at[...] = hidden_grad.astype(BF16)
    activated, both = sides_of(pre[:, :hidden], pre[:, hidden:], hidden_grad)
    act[...] = activated
    sides[...] = both
    stores += [
        move.start(source, target)
        for source, target in ((hidden_at, hidden_hbm), (act, act_hbm), (sides, sides_hbm))
    ]
    at = lane_row(slots)
    late = at - kept
    target = jnp.where(
        at < kept,
        lax.shift_right_logical(at, base.bit_length() - 1) * depth + (at & (base - 1)),
        lax.shift_right_arithmetic(late, extra.bit_length() - 1) * depth
        + base
        + (late & (extra - 1)),
    )
    order = zero_one(row_index(slots, slots) == target)
    both = dot(order, both, (1, 0)).astype(BF16)
    for part in range(2):
        wait(*weights[part])
        columns = pl.ds(part * half, half)
        slot[:, part * half : (part + 1) * half] = dot(
            both, joined[part * half : (part + 1) * half], (1, 1)
        ).astype(BF16)
        stores.append(move.start(slot.at[:, columns], slot_hbm.at[:, columns]))
    wait(*stores)


def kernel_down(
    pre_hbm, packet_hbm, hidden_hbm, act_hbm, grads_hbm, other_grads_hbm,
    down_hbm, sides_hbm,
    pre, hidden_at, act, grads, other_grads, down, sides, sems,
):
    slots, hidden = act.shape
    kept = pre_hbm.shape[0]
    move = Mover(sems)
    first = [
        move.start(pre_hbm, pre.at[pl.ds(0, kept)]),
        move.start(
            packet_hbm.at[pl.ds(slots - kept, slots - kept), pl.ds(0, 2 * hidden)],
            pre.at[pl.ds(kept, slots - kept)],
        ),
        move.start(hidden_hbm, hidden_at),
    ]
    second = [
        move.start(source, target)
        for source, target in (
            (act_hbm, act),
            (grads_hbm, grads),
            (other_grads_hbm, other_grads),
        )
    ]
    wait(*first)
    act_other, sides_other = sides_of(
        pre[:, :hidden].astype(F32), pre[:, hidden:].astype(F32), hidden_at[...].astype(F32)
    )
    sides[...] = sides_other
    stores = [move.start(sides, sides_hbm)]
    wait(*second)
    down[...] = sum_parts(
        dot(act[...], grads[...], (0, 0)), dot(act_other, other_grads[...], (0, 0))
    )
    stores.append(move.start(down, down_hbm))
    wait(*stores)


def kernel_joined(
    rows_hbm, late_rows_hbm, other_rows_hbm, packet_hbm, sides_hbm, other_sides_hbm,
    gate_hbm, up_hbm,
    rows, other_rows, sides, other_sides, joined, sems,
):
    slots, half = rows.shape
    kept = rows_hbm.shape[0]
    hidden = sides.shape[1] // 2
    base, late = pl.ds(0, kept), pl.ds(kept, slots - kept)
    move = Mover(sems)
    loads = [
        move.start(source, target)
        for source, target in (
            (rows_hbm.at[:, pl.ds(0, half)], rows.at[base]),
            (late_rows_hbm, rows.at[late]),
            (sides_hbm, sides),
            (other_rows_hbm, other_rows.at[base]),
            (packet_hbm.at[pl.ds(0, slots - kept)], other_rows.at[late]),
            (other_sides_hbm, other_sides),
        )
    ]
    wait(*loads)
    stores = []
    for at, target in ((0, gate_hbm), (hidden, up_hbm)):
        columns = slice(at, at + hidden)
        joined[:, columns] = sum_parts(
            dot(rows[...], sides[:, columns], (0, 0)),
            dot(other_rows[...], other_sides[:, columns], (0, 0)),
        )
        stores.append(move.start(joined.at[:, pl.ds(at, hidden)], target))
    wait(*stores)


def kernel_final(
    place_hbm, returned_hbm, own_hbm, other_hbm, input_hbm, down_hbm, place, returned, out, down, sems
):
    half = out.shape[1] // 2
    me = lax.axis_index("dp")
    move = Mover(sems)
    loads = [move.start(place_hbm, place)] + [
        move.start(
            returned_hbm.at[:, pl.ds(part * half, half)], returned.at[:, pl.ds(part * half, half)]
        )
        for part in range(2)
    ]
    at = half_at(me, half), half_at(1 - me, half)
    down_loads = [
        move.start(source, down.at[part]) for part, source in enumerate((own_hbm, other_hbm))
    ]
    wait(*loads[:2])
    stores = []
    for part in range(2):
        columns = slice(part * half, (part + 1) * half)
        out[:, columns] = dot(place[...], returned[:, columns], (0, 0)).astype(BF16)
        stores.append(
            move.start(out.at[:, pl.ds(part * half, half)], input_hbm.at[:, at[part]])
        )
        wait(down_loads[part])
        stores.append(move.start(down.at[part], down_hbm.at[:, at[part]]))
        if part == 0:
            wait(loads[2])
    wait(*stores)


def on_pair(tokens, out_grad, expert_ids, gates, w_gate, w_up, w_down):
    experts = lax.axis_size("expert")
    width = tokens.shape[1]
    per_token = expert_ids.shape[1]
    hidden = w_gate.shape[2]
    entries = expert_ids.size
    depth = 3 * entries // experts
    base = 2 * entries // experts
    extra = depth - base
    slots = experts * depth
    kept = experts * base
    half = width // 2
    late = slots - kept
    ids, weights = expert_ids.reshape(1, entries), gates.reshape(1, entries)
    grad_rows = token_rows(out_grad, per_token)
    int_row, float_row = shape(1, entries, dtype=jnp.int32), shape(1, entries, dtype=F32)
    pool_shape = shape(2 * extra, half + LANES)
    marks_shape = shape(8, LANES, dtype=F32)

    send_inputs, input_pool, place, marks, scaled = call(
        functools.partial(kernel_inputs, experts, depth, base),
        (
            shape(kept, width),
            pool_shape,
            shape(slots, entries),
            marks_shape,
            shape(entries + 16, half),
        ),
        (
            int_row,
            float_row,
            shape(entries, width),
            shape(entries, half),
            shape(kept, width),
            pool_shape,
            shape(slots, entries),
            marks_shape,
            shape(entries + 16, half),
        ),
        11,
        2 * kept * entries * width,
        ids,
        weights,
        token_rows(tokens, per_token),
        grad_rows,
    )
    rows_in = exchange(send_inputs.reshape(experts, base, width), "expert").reshape(kept, width)
    other_scaled = swap(scaled)
    other_gate = swap(w_gate[0])
    rows_half, base_half, by_hidden = shape(slots, half), shape(kept, half), shape(slots, hidden)
    send_theirs, send_own, grad_pool = call(
        functools.partial(kernel_grads, experts, depth, base),
        (base_half, base_half, pool_shape),
        (
            int_row,
            float_row,
            shape(entries, half),
            shape(entries + 16, half),
            base_half,
            base_half,
            pool_shape,
        ),
        7,
        4 * kept * entries * width,
        ids,
        weights,
        grad_rows,
        other_scaled,
    )

    def from_distance(x, distance):
        return lax.ppermute(x, "expert", [(at, at ^ distance) for at in range(experts)])

    step = experts // 4
    pool = jnp.concatenate([input_pool, grad_pool], axis=0)
    pool = jnp.stack([pool] + [from_distance(pool, at * step) for at in range(1, 4)], axis=0)
    rows_in, other_gate, send_theirs, pool = lax.optimization_barrier(
        (rows_in, other_gate, send_theirs, pool)
    )
    grads_theirs = exchange(send_theirs.reshape(experts, base, half), "expert")
    other_weights = other_gate, swap(w_up[0])
    other_rows = swap(rows_in[:, half:])
    own_weights = w_gate[0], w_up[0]
    pre, sent_pre = call(
        kernel_base,
        (shape(kept, 2 * hidden, dtype=F32), shape(kept, 2 * hidden)),
        (
            shape(kept, width),
            shape(width, 2 * hidden),
            shape(kept, 2 * hidden, dtype=F32),
            shape(kept, 2 * hidden),
        ),
        9,
        0,
        rows_in,
        *own_weights,
        *other_weights,
    )
    other_pre = swap(sent_pre)
    while step > 1:
        step //= 2
        early = pool.shape[0] == 4
        (pool,) = call(
            kernel_stack,
            (shape(pool.shape[0], 2, *pool.shape[1:]),),
            (shape(pool.shape[0], 2, *pool.shape[1:]),),
            3,
            LATE_FLOPS if early else 0,
            pool,
            from_distance(pool, step),
            *((other_weights[1], other_weights[0]) if early else (sent_pre, sent_pre)),
        )
        pool = pool.reshape(-1, *pool.shape[2:])
    pool = pool.reshape(-1, half + LANES)
    grads_theirs, send_own, sent_pre = lax.optimization_barrier((grads_theirs, send_own, sent_pre))
    recv_theirs = grads_theirs.reshape(kept, half)
    recv_own = exchange(send_own.reshape(experts, base, half), "expert").reshape(kept, half)

    sent, grads_theirs = call(
        functools.partial(kernel_hidden, extra),
        (by_hidden, rows_half),
        (shape(*pool.shape), marks_shape, shape(hidden, half), rows_half, by_hidden),
        6,
        2 * slots * hidden * half,
        recv_theirs,
        pool,
        marks,
        w_down[0],
        other_rows,
    )
    remote = swap(sent)
    late_pre, late_rows, packet = call(
        functools.partial(kernel_late, extra),
        (
            shape(late, 2 * hidden, dtype=F32),
            shape(late, half),
            shape(2 * late + 16, half),
        ),
        (
            shape(*pool.shape),
            marks_shape,
            shape(width, 2 * hidden),
            shape(late, 2 * hidden, dtype=F32),
            shape(late, half),
            shape(2 * late + 16, half),
        ),
        9,
        4 * late * hidden * width,
        pool,
        marks,
        sent,
        *own_weights,
        *other_weights,
    )
    remote, packet = lax.optimization_barrier((remote, packet))
    other_packet = swap(packet)
    slot_grad, act, sides, hidden_grad, grads_own = call(
        functools.partial(kernel_slot, base, depth),
        (shape(slots, width), by_hidden, shape(slots, 2 * hidden), by_hidden, rows_half),
        (
            shape(*pool.shape),
            marks_shape,
            shape(hidden, half),
            by_hidden,
            shape(slots, 2 * hidden, dtype=F32),
            shape(width, 2 * hidden),
            shape(slots, width),
            by_hidden,
            shape(slots, 2 * hidden),
            by_hidden,
            rows_half,
        ),
        17,
        4 * slots * hidden * width,
        recv_own,
        pool,
        marks,
        w_down[0],
        remote,
        pre,
        late_pre,
        *own_weights,
        *other_weights,
    )
    other_hidden = swap(hidden_grad)
    returned = exchange(slot_grad.reshape(experts, depth, width), "expert").reshape(slots, width)

    own_down, other_sides = call(
        kernel_down,
        (shape(hidden, half), shape(slots, 2 * hidden)),
        (
            shape(slots, 2 * hidden),
            by_hidden,
            by_hidden,
            rows_half,
            rows_half,
            shape(hidden, half),
            shape(slots, 2 * hidden),
        ),
        8,
        LATE_FLOPS,
        other_pre,
        other_packet,
        other_hidden,
        act,
        grads_own,
        grads_theirs,
    )
    other_down = swap(own_down)
    gate_grad, up_grad = call(
        kernel_joined,
        (shape(half, hidden), shape(half, hidden)),
        (
            rows_half,
            rows_half,
            shape(slots, 2 * hidden),
            shape(slots, 2 * hidden),
            shape(half, 2 * hidden),
        ),
        8,
        8 * slots * hidden * half,
        rows_in,
        late_rows,
        other_rows,
        other_packet,
        sides,
        other_sides,
    )
    picked, down_grad = call(
        kernel_final,
        (shape(entries, width), shape(hidden, width)),
        (
            shape(slots, entries),
            shape(slots, width),
            shape(entries, width),
            shape(2, hidden, half),
        ),
        9,
        2 * slots * entries * width,
        place,
        returned,
        own_down,
        other_down,
    )
    crowded = jnp.maximum(jnp.max(packet[2 * late :]), jnp.max(other_packet[2 * late :])) > 0.0
    return crowded, (sum_choices(picked, per_token), gate_grad[None], up_grad[None], down_grad[None])


def on_device(*arguments):
    if lax.axis_size("dp") != 2:
        return on_any(*arguments)
    crowded, results = on_pair(*arguments)
    return lax.while_loop(
        lambda state: state[0], lambda state: (False, on_any(*arguments)), (crowded, results)
    )[1]


def on_any(tokens, out_grad, expert_ids, gates, w_gate, w_up, w_down):
    experts = lax.axis_size("expert")
    width = tokens.shape[1]
    per_token = expert_ids.shape[1]
    hidden = w_gate.shape[2]
    depth = 3 * expert_ids.size // experts
    slots = experts * depth

    pair = lax.axis_size("dp") == 2
    first = lax.axis_index("dp") == 0

    def gather(x, axis):
        if not pair:
            return lax.all_gather(x, "dp", axis=axis, tiled=True)
        other = swap(x)
        return jnp.concatenate([jnp.where(first, x, other), jnp.where(first, other, x)], axis=axis)

    joined = gather(jnp.concatenate([w_gate[0], w_up[0]], axis=1), 0)
    down = gather(w_down[0], 1)
    place = place_matrix(expert_ids, experts, depth)

    def dispatch(table):
        sent = dot(place, table, (1, 0)).astype(BF16).reshape(experts, depth, width)
        return exchange(sent, "expert").reshape(slots, width)

    rows_in = dispatch(token_rows(tokens, per_token))
    grads_in = dispatch(scaled_rows(out_grad, gates))
    preact = dot(rows_in, joined, (1, 0))
    activated, sides = sides_of(
        preact[:, :hidden], preact[:, hidden:], dot(grads_in, down, (1, 1))
    )
    slot_grad = dot(sides, joined, (1, 1)).astype(BF16)
    returned = exchange(slot_grad.reshape(experts, depth, width), "expert").reshape(slots, width)
    down_part = dot(activated, grads_in, (0, 0)).astype(BF16)
    joined_part = dot(rows_in, sides, (0, 0)).astype(BF16)
    if pair:
        low, high = jnp.split(joined_part, 2, axis=0)
        down_grad = sum_parts(down_part, swap(down_part))
        joined_grad = sum_parts(jnp.where(first, low, high), swap(jnp.where(first, high, low)))
    else:
        down_grad = lax.psum(down_part, "dp")
        joined_grad = lax.psum_scatter(joined_part, "dp", scatter_dimension=0, tiled=True)
    input_grad = sum_choices(dot(place, returned, (0, 0)), per_token)
    return (
        input_grad,
        joined_grad[:, :hidden][None],
        joined_grad[:, hidden:][None],
        down_grad[None],
    )


def solution(mesh):
    rows = P(BOTH, None)
    in_specs = (
        rows,
        rows,
        rows,
        rows,
        P("expert", "dp", None),
        P("expert", "dp", None),
        P("expert", None, "dp"),
    )
    out_specs = (
        rows,
        P("expert", "dp", None),
        P("expert", "dp", None),
        P("expert", None, None),
    )
    return jax.shard_map(
        on_device, mesh=mesh, in_specs=in_specs, out_specs=out_specs, check_vma=False
    )
```

time: 150 us -> 140 us (0.933)
  waiting for transfers between devices: 94.2 us -> 48 us
  starting transfers between devices: 24.2 us -> 42 us
  Pallas kernels: 21.3 us -> 38.8 us
  matrix products: 3.76 us -> 0 us
  other arithmetic: 0.04 us -> 3.69 us
  between operations: 0.73 us -> 2.27 us
    ppermute x6 -> x9, waiting for transfers between devices: 89.4 us -> 28.1 us  [swap(): return lax.ppermute(x, 'dp', [(0, 1), (1, 0)])]
    pallas_call x5 -> x11, Pallas kernels: 21.3 us -> 38.8 us  [call(): pl.pallas_call(kernel, out_shape=list(out_shapes), in_specs=[IN_HBM] * le...]
    ppermute x0 -> x5, waiting for transfers between devices: none -> 13.9 us  [from_distance(): lax.ppermute(x, 'expert', [(at, at ^ distance) for at in range(experts)])]
    all_to_all x3 -> x4, starting transfers between devices: 19.3 us -> 28.1 us  [exchange(): return lax.all_to_all(x, axes, split_axis=0, concat_axis=0, tiled=True)]
    ppermute x0 -> x5, starting transfers between devices: none -> 4.75 us  [from_distance(): lax.ppermute(x, 'expert', [(at, at ^ distance) for at in range(experts)])]
    ppermute x6 -> x9, starting transfers between devices: 4.92 us -> 9.22 us  [swap(): return lax.ppermute(x, 'dp', [(0, 1), (1, 0)])]
    dot_general x2 -> x0, matrix products: 3.76 us -> none  [dot(): lax.dot_general(a, b, ((contract[:1], contract[1:]), ((), ())), preferred...]
    reduce_max x0 -> x2, other arithmetic: none -> 2.76 us  [the longest x1 1.38 us: on_pair(): jnp.max(packet[2 * late:])]
  transfers between devices with their start and end apart: 9 -> 18, of which waited for: 7 -> 9; matrix products, arithmetic and copies ran while one was open for 3% -> 5% of each run, Pallas kernels for 6% -> 24%
where the time goes in v3:
time: 140 us; the launch traced here: 139 us
  waiting for transfers between devices  48 us (34%)
  starting transfers between devices  42 us (30%)
  Pallas kernels  38.8 us (28%)
  local copies, waits for them, and re-layouts  4.58 us (3%)
  other arithmetic  3.69 us (3%)
  between operations  2.27 us (2%)
    pallas_call x11, Pallas kernels, call(): pl.pallas_call(kernel, out_shape=list(out_shapes), in_specs=[IN_HBM] * le...  38.8 us
    ppermute x9, waiting for transfers between devices, swap(): return lax.ppermute(x, 'dp', [(0, 1), (1, 0)])  28.1 us
    all_to_all x4, starting transfers between devices, exchange(): return lax.all_to_all(x, axes, split_axis=0, concat_axis=0, tiled=True)  28.1 us
    ppermute x5, waiting for transfers between devices, from_distance(): lax.ppermute(x, 'expert', [(at, at ^ distance) for at in range(experts)])  13.9 us
    ppermute x9, starting transfers between devices, swap(): return lax.ppermute(x, 'dp', [(0, 1), (1, 0)])  9.22 us
    all_to_all x4, waiting for transfers between devices, exchange(): return lax.all_to_all(x, axes, split_axis=0, concat_axis=0, tiled=True)  6 us
    ppermute x5, starting transfers between devices, from_distance(): lax.ppermute(x, 'expert', [(at, at ^ distance) for at in range(experts)])  4.75 us
  transfers between devices with their start and end apart: 18, of which 9 were waited for; matrix products, arithmetic and copies ran while one was open for 5% of the time, Pallas kernels for 24%

profile of v3, /device:TPU:13, one launch (start us, length us, event | category | flops | bytes accessed | tf_op | source)
XLA Modules:
  0.0 139.4 jit_solution(9491514748772059156)
XLA Ops:
  0.6 2.7 %shard_map.102 = (bf16[256,2048]{1,0:T(8,128)(2,1)}, bf16[16,1152]{1,0:T(8,128)(2,1)}, bf16[384,128]{1,0:T(8,128)(2,1)}, f32[8,128]{1,0:T(8,128)}, bf16[144,1024]{1,0:T(8,128)(2,1)}) custom-call(s32[1,128]{1,0:T(1,128)} %bitcast.69, f32[1,128]{1,0:T(1,128)} %bitcast.66, bf16[128,2048]{1,0:T(8,128)(2,1)} %tokens_hbm.1, bf16[128,2048]{1,0:T(8,128)(2,1)} %grad_hbm.3), custom_call_target="tpu_custom_call" | custom-call | flops 134217728 | bytes 2532352 | tf_op jit(solution)/shard_map/pallas_call | solution.py:85
  3.3 0.0 copy-start.12
  3.3 0.0 copy-start.10
  3.3 6.7 %all-to-all-start.3 = ((bf16[16,16,2048]{2,1,0:T(8,128)(2,1)}), bf16[16,16,2048]{2,1,0:T(8,128)(2,1)}, u32[]{:S(2)}, u32[]{:S(2)}) async-start(bf16[16,16,2048]{2,1,0:T(8,128)(2,1)} %bitcast.57), calls=%async_computation.3 | async-start | bytes 2097152 | tf_op jit(solution)/shard_map/all_to_all | solution.py:26
  10.0 0.0 copy-done.12
  10.0 1.3 collective-permute-start.5
  11.3 0.3 collective-permute-start.4
  11.6 1.2 collective-permute-start.9
  12.8 0.0 copy-done.10
  12.8 0.6 constant_dynamic-update-slice_fusion.1
  13.4 5.0 %collective-permute-done.5.other_hbm = bf16[144,1024]{1,0:T(8,128)(2,1)} collective-permute-done((bf16[144,1024]{1,0:T(8,128)(2,1)S(1)}, bf16[144,1024]{1,0:T(8,128)(2,1)}, u32[]{:S(2)}, u32[]{:S(2)}) %collective-permute-start.5) | collective-permute-done | bytes 294944 | tf_op jit(solution)/shard_map/ppermute | solution.py:22
  18.4 2.6 %shard_map.103 = (bf16[256,1024]{1,0:T(8,128)(2,1)}, bf16[256,1024]{1,0:T(8,128)(2,1)}, bf16[16,1152]{1,0:T(8,128)(2,1)}) custom-call(s32[1,128]{1,0:T(1,128)} %bitcast.70, f32[1,128]{1,0:T(1,128)} %bitcast.67, bf16[128,2048]{1,0:T(8,128)(2,1)} %grad_hbm.3, bf16[144,1024]{1,0:T(8,128)(2,1)} %collective-permute-done.5.other_hbm), custom_call_target="tpu_custom_call" | custom-call | flops 268435456 | bytes 1905664 | tf_op jit(solution)/shard_map/pallas_call | solution.py:85
  21.1 1.4 constant_dynamic-update-slice_fusion
  22.4 1.2 collective-permute-start.8
  23.6 1.2 collective-permute-start.7
  24.8 0.9 collective-permute-start.6
  25.7 13.9 %collective-permute-done.8 = bf16[32,1152]{1,0:T(8,128)(2,1)S(1)} collective-permute-done((bf16[32,1152]{1,0:T(8,128)(2,1)}, bf16[32,1152]{1,0:T(8,128)(2,1)S(1)}, u32[]{:S(2)}, u32[]{:S(2)}) %collective-permute-start.8) | collective-permute-done | bytes 73760 | tf_op jit(solution)/shard_map/ppermute | solution.py:594
  39.6 0.0 collective-permute-done.7
  39.6 0.0 collective-permute-done.6
  39.6 0.9 pad_maximum_fusion.7.pool_hbm
  40.6 0.0 copy-start.9
  40.6 0.0 collective-permute-done.4.other_gate_hbm._other_hbm
  40.6 0.0 all-to-all-done.3
  40.6 0.7 copy-done.9
  41.3 0.2 collective-permute-start.10
  41.5 8.7 %all-to-all-start.4 = ((bf16[16,16,1024]{2,1,0:T(8,128)(2,1)}), bf16[16,16,1024]{2,1,0:T(8,128)(2,1)}, u32[]{:S(2)}, u32[]{:S(2)}) async-start(bf16[16,16,1024]{2,1,0:T(8,128)(2,1)} %bitcast.61), calls=%async_computation.4 | async-start | bytes 1048576 | tf_op jit(solution)/shard_map/all_to_all | solution.py:26
  50.2 2.0 %collective-permute-done.9.other_up_hbm._one_hbm = bf16[1024,384]{1,0:T(8,128)(2,1)} collective-permute-done((bf16[1024,384]{1,0:T(8,128)(2,1)}, bf16[1024,384]{1,0:T(8,128)(2,1)}, u32[]{:S(2)}, u32[]{:S(2)}) %collective-permute-start.9) | collective-permute-done | bytes 786464 | tf_op jit(solution)/shard_map/ppermute | solution.py:22
  52.1 0.0 collective-permute-done.10.received_hbm
  52.1 1.9 %shard_map.105 = bf16[4,2,32,1152]{3,2,1,0:T(8,128)(2,1)} custom-call(bf16[4,32,1152]{2,1,0:T(8,128)(2,1)} %copy-done.9, bf16[4,32,1152]{2,1,0:T(8,128)(2,1)} %collective-permute-done.10.received_hbm, bf16[1024,384]{1,0:T(8,128)(2,1)} %collective-permute-done.9.other_up_hbm._one_hbm, bf16[1024,384]{1,0:T(8,128)(2,1)} %collective-permute-done.4.other_gate_hbm._other_hbm), custom_call_target="tpu_custom_call" | custom-call | flops 99999997952 | bytes 2752512 | tf_op jit(solution)/shard_map/pallas_call | solution.py:85
  54.0 1.3 collective-permute-start.11
  55.3 1.9 %slice.21 = bf16[256,1024]{1,0:T(8,128)(2,1)} slice(bf16[256,2048]{1,0:T(8,128)(2,1)} %bitcast.17.rows_hbm), slice={[0:256], [1024:2048]} | slice | bytes 1048576 | tf_op jit(solution)/shard_map/slice | solution.py:604
  57.2 1.2 collective-permute-start.12
  58.4 4.2 %shard_map.104 = (f32[256,768]{1,0:T(8,128)}, bf16[256,768]{1,0:T(8,128)(2,1)}) custom-call(bf16[256,2048]{1,0:T(8,128)(2,1)} %bitcast.17.rows_hbm, bf16[1024,384]{1,0:T(8,128)(2,1)} %bitcast.18.gate_hbm, bf16[1024,384]{1,0:T(8,128)(2,1)} %bitcast.24.up_hbm, bf16[1024,384]{1,0:T(8,128)(2,1)} %collective-permute-done.4.other_gate_hbm._other_hbm, ...), custom_call_target="tpu_custom_call" | custom-call | bytes 5373952 | tf_op jit(solution)/shard_map/pallas_call | solution.py:85
  62.6 1.6 %all-to-all-done.4 = bf16[16,16,1024]{2,1,0:T(8,128)(2,1)} async-done(((bf16[16,16,1024]{2,1,0:T(8,128)(2,1)}), bf16[16,16,1024]{2,1,0:T(8,128)(2,1)}, u32[]{:S(2)}, u32[]{:S(2)}) %all-to-all-start.4) | async-done | bytes 524320 | tf_op jit(solution)/shard_map/all_to_all | solution.py:26
  64.2 4.7 %all-to-all-start.5 = ((bf16[16,16,1024]{2,1,0:T(8,128)(2,1)}), bf16[16,16,1024]{2,1,0:T(8,128)(2,1)}, u32[]{:S(2)}, u32[]{:S(2)}) async-start(bf16[16,16,1024]{2,1,0:T(8,128)(2,1)} %bitcast.60), calls=%async_computation.5 | async-start | bytes 1048576 | tf_op jit(solution)/shard_map/all_to_all | solution.py:26
  68.9 0.0 collective-permute-done.11.received_hbm
  68.9 2.3 %shard_map.106 = bf16[8,2,32,1152]{3,2,1,0:T(8,128)(2,1)} custom-call(bf16[8,32,1152]{2,1,0:T(8,128)(2,1)} %bitcast.59, bf16[8,32,1152]{2,1,0:T(8,128)(2,1)} %collective-permute-done.11.received_hbm, bf16[256,768]{1,0:T(8,128)(2,1)} %get-tuple-element.107._one_hbm._other_hbm, bf16[256,768]{1,0:T(8,128)(2,1)} %get-tuple-element.107._one_hbm._other_hbm), custom_call_target="tpu_custom_call" | custom-call | bytes 3145728 | tf_op jit(solution)/shard_map/pallas_call | solution.py:85
  71.2 0.0 collective-permute-done.12._rows_hbm.other_rows_hbm
  71.2 3.6 %shard_map.107 = (bf16[384,384]{1,0:T(8,128)(2,1)}, bf16[384,1024]{1,0:T(8,128)(2,1)}) custom-call(bf16[256,1024]{1,0:T(8,128)(2,1)} %bitcast.25.recv_hbm, bf16[512,1152]{1,0:T(8,128)(2,1)} %bitcast.53, f32[8,128]{1,0:T(8,128)} %get-tuple-element.110.marks_hbm, bf16[384,1024]{1,0:T(8,128)(2,1)} %bitcast.28.down_hbm, ...), custom_call_target="tpu_custom_call" | custom-call | flops 301989888 | bytes 4100096 | tf_op jit(solution)/shard_map/pallas_call | solution.py:85
  74.9 1.3 collective-permute-start.13
  76.1 3.9 %shard_map.108 = (f32[128,768]{1,0:T(8,128)}, bf16[128,1024]{1,0:T(8,128)(2,1)}, bf16[272,1024]{1,0:T(8,128)(2,1)}) custom-call(bf16[512,1152]{1,0:T(8,128)(2,1)} %bitcast.54, f32[8,128]{1,0:T(8,128)} %get-tuple-element.110.marks_hbm, bf16[384,384]{1,0:T(8,128)(2,1)} %get-tuple-element.111.hidden_hbm, bf16[1024,384]{1,0:T(8,128)(2,1)} %bitcast.18.gate_hbm, ...), custom_call_target="tpu_custom_call" | custom-call | flops 402653184 | bytes 5836800 | tf_op jit(solution)/shard_map/pallas_call | solution.py:85
  80.1 3.2 %collective-permute-done.13.remote_hbm = bf16[384,384]{1,0:T(8,128)(2,1)} collective-permute-done((bf16[384,384]{1,0:T(8,128)(2,1)}, bf16[384,384]{1,0:T(8,128)(2,1)}, u32[]{:S(2)}, u32[]{:S(2)}) %collective-permute-start.13) | collective-permute-done | bytes 294944 | tf_op jit(solution)/shard_map/ppermute | solution.py:22
  83.2 1.2 collective-permute-start.14
  84.4 0.3 collective-permute-start.15
  84.7 0.0 all-to-all-done.5
  84.7 6.0 %shard_map.109 = (bf16[384,2048]{1,0:T(8,128)(2,1)}, bf16[384,384]{1,0:T(8,128)(2,1)}, bf16[384,768]{1,0:T(8,128)(2,1)}, bf16[384,384]{1,0:T(8,128)(2,1)}, bf16[384,1024]{1,0:T(8,128)(2,1)}) custom-call(bf16[256,1024]{1,0:T(8,128)(2,1)} %bitcast.30.recv_hbm, bf16[512,1152]{1,0:T(8,128)(2,1)} %bitcast.55, f32[8,128]{1,0:T(8,128)} %get-tuple-element.110.marks_hbm, ...), custom_call_target="tpu_custom_call" | custom-call | flops 1207959552 | bytes 10653696 | tf_op jit(solution)/shard_map/pallas_call | solution.py:85
  90.7 1.3 collective-permute-start.16
  91.9 8.0 %all-to-all-start.6 = ((bf16[16,24,2048]{2,1,0:T(8,128)(2,1)}), bf16[16,24,2048]{2,1,0:T(8,128)(2,1)}, u32[]{:S(2)}, u32[]{:S(2)}) async-start(bf16[16,24,2048]{2,1,0:T(8,128)(2,1)} %bitcast.56), calls=%async_computation.6 | async-start | bytes 3145728 | tf_op jit(solution)/shard_map/all_to_all | solution.py:26
  99.9 4.7 %collective-permute-done.15.pre_hbm = bf16[256,768]{1,0:T(8,128)(2,1)} collective-permute-done((bf16[256,768]{1,0:T(8,128)(2,1)}, bf16[256,768]{1,0:T(8,128)(2,1)}, u32[]{:S(2)}, u32[]{:S(2)}) %collective-permute-start.15) | collective-permute-done | bytes 393248 | tf_op jit(solution)/shard_map/ppermute | solution.py:22
  104.7 0.0 collective-permute-done.14.packet_hbm
  104.7 6.3 %collective-permute-done.16.hidden_hbm = bf16[384,384]{1,0:T(8,128)(2,1)} collective-permute-done((bf16[384,384]{1,0:T(8,128)(2,1)}, bf16[384,384]{1,0:T(8,128)(2,1)}, u32[]{:S(2)}, u32[]{:S(2)}) %collective-permute-start.16) | collective-permute-done | bytes 294944 | tf_op jit(solution)/shard_map/ppermute | solution.py:22
  111.0 3.8 %shard_map.110 = (bf16[384,1024]{1,0:T(8,128)(2,1)}, bf16[384,768]{1,0:T(8,128)(2,1)}) custom-call(bf16[256,768]{1,0:T(8,128)(2,1)} %collective-permute-done.15.pre_hbm, bf16[272,1024]{1,0:T(8,128)(2,1)} %collective-permute-done.14.packet_hbm, bf16[384,384]{1,0:T(8,128)(2,1)} %collective-permute-done.16.hidden_hbm, ...), custom_call_target="tpu_custom_call" | custom-call | flops 99999997952 | bytes 4489216 | tf_op jit(solution)/shard_map/pallas_call | solution.py:85
  114.7 1.3 collective-permute-start.17
  116.0 1.4 slice_reduce_fusion.1
  117.4 1.4 slice_reduce_fusion
  120.1 4.8 %shard_map.112 = (bf16[1024,384]{1,0:T(8,128)(2,1)}, bf16[1024,384]{1,0:T(8,128)(2,1)}) custom-call(bf16[256,2048]{1,0:T(8,128)(2,1)} %bitcast.17.rows_hbm, bf16[128,1024]{1,0:T(8,128)(2,1)} %get-tuple-element.126.late_rows_hbm, bf16[256,1024]{1,0:T(8,128)(2,1)} %collective-permute-done.12._rows_hbm.other_rows_hbm, ...), custom_call_target="tpu_custom_call" | custom-call | flops 1207959552 | bytes 5144576 | tf_op jit(solution)/shard_map/pallas_call | solution.py:85
  124.9 6.9 %collective-permute-done.17.other_hbm = bf16[384,1024]{1,0:T(8,128)(2,1)} collective-permute-done((bf16[384,1024]{1,0:T(8,128)(2,1)}, bf16[384,1024]{1,0:T(8,128)(2,1)}, u32[]{:S(2)}, u32[]{:S(2)}) %collective-permute-start.17) | collective-permute-done | bytes 786464 | tf_op jit(solution)/shard_map/ppermute | solution.py:22
  131.8 4.4 %all-to-all-done.6 = bf16[16,24,2048]{2,1,0:T(8,128)(2,1)} async-done(((bf16[16,24,2048]{2,1,0:T(8,128)(2,1)}), bf16[16,24,2048]{2,1,0:T(8,128)(2,1)}, u32[]{:S(2)}, u32[]{:S(2)}) %all-to-all-start.6) | async-done | bytes 1572896 | tf_op jit(solution)/shard_map/all_to_all | solution.py:26
  136.2 3.0 %shard_map.111 = (bf16[128,2048]{1,0:T(8,128)(2,1)}, bf16[384,2048]{1,0:T(8,128)(2,1)}) custom-call(bf16[384,128]{1,0:T(8,128)(2,1)} %get-tuple-element.114.place_hbm, bf16[384,2048]{1,0:T(8,128)(2,1)} %bitcast.32.returned_hbm, bf16[384,1024]{1,0:T(8,128)(2,1)} %get-tuple-element.124.own_hbm, bf16[384,1024]{1,0:T(8,128)(2,1)} %collective-permute-done.17.other_hbm), custom_call_target="tpu_custom_call" | custom-call | flops 201326592 | bytes 5341184 | tf_op jit(solution)/shard_map/pallas_call | solution.py:85
  (1 shorter events, 0.0 us)
Async XLA Ops:
  3.3 6.7 %copy-start.12 = (bf16[144,1024]{1,0:T(8,128)(2,1)S(1)}, bf16[144,1024]{1,0:T(8,128)(2,1)}, u32[]{:S(2)}) copy-start(bf16[144,1024]{1,0:T(8,128)(2,1)} %get-tuple-element.99) | copy-start | bytes 884740
  3.3 9.5 %copy-start.10 = (bf16[16,1152]{1,0:T(8,128)(2,1)S(1)}, bf16[16,1152]{1,0:T(8,128)(2,1)}, u32[]{:S(2)}) copy-start(bf16[16,1152]{1,0:T(8,128)(2,1)} %get-tuple-element.101) | copy-start | bytes 110596
  3.3 37.3 %all-to-all-start.3 = ((bf16[16,16,2048]{2,1,0:T(8,128)(2,1)}), bf16[16,16,2048]{2,1,0:T(8,128)(2,1)}, u32[]{:S(2)}, u32[]{:S(2)}) async-start(bf16[16,16,2048]{2,1,0:T(8,128)(2,1)} %bitcast.57), calls=%async_computation.3 | async-start | bytes 2097152 | tf_op jit(solution)/shard_map/all_to_all | solution.py:26
  10.0 8.4 %collective-permute-start.5 = (bf16[144,1024]{1,0:T(8,128)(2,1)S(1)}, bf16[144,1024]{1,0:T(8,128)(2,1)}, u32[]{:S(2)}, u32[]{:S(2)}) collective-permute-start(bf16[144,1024]{1,0:T(8,128)(2,1)S(1)} %copy-done.12), channel_id=1, source_target_pairs={{0,16},{16,0},{1,17},{17,1},{2,18},{18,2},{3,19},{19,3},{4,20},{20... | collective-permute-start | bytes 884744 | tf_op jit(solution)/shard_map/ppermute | solution.py:22
  11.3 29.3 %collective-permute-start.4 = (bf16[1024,384]{1,0:T(8,128)(2,1)}, bf16[1024,384]{1,0:T(8,128)(2,1)}, u32[]{:S(2)}, u32[]{:S(2)}) collective-permute-start(bf16[1024,384]{1,0:T(8,128)(2,1)} %bitcast.18.gate_hbm), channel_id=1, source_target_pairs={{0,16},{16,0},{1,17},{17,1},{2,18},{18,2},{3,19},{19,3},{4,20},{20... | collective-permute-start | bytes 2359304 | tf_op jit(solution)/shard_map/ppermute | solution.py:22
  11.6 40.6 %collective-permute-start.9 = (bf16[1024,384]{1,0:T(8,128)(2,1)}, bf16[1024,384]{1,0:T(8,128)(2,1)}, u32[]{:S(2)}, u32[]{:S(2)}) collective-permute-start(bf16[1024,384]{1,0:T(8,128)(2,1)} %bitcast.24.up_hbm), channel_id=1, source_target_pairs={{0,16},{16,0},{1,17},{17,1},{2,18},{18,2},{3,19},{19,3},{4,20},{20... | collective-permute-start | bytes 2359304 | tf_op jit(solution)/shard_map/ppermute | solution.py:22
  22.4 17.2 %collective-permute-start.8 = (bf16[32,1152]{1,0:T(8,128)(2,1)}, bf16[32,1152]{1,0:T(8,128)(2,1)S(1)}, u32[]{:S(2)}, u32[]{:S(2)}) collective-permute-start(bf16[32,1152]{1,0:T(8,128)(2,1)} %constant_dynamic-update-slice_fusion), channel_id=1, source_target_pairs={{0,12},{1,13},{2,14},{3,15},{4,8},{5,9},{6,10},{7,11},{8,4},{9,5},... | collective-permute-start | bytes 221192 | tf_op jit(solution)/shard_map/ppermute | solution.py:594
  23.6 16.0 %collective-permute-start.7 = (bf16[32,1152]{1,0:T(8,128)(2,1)}, bf16[32,1152]{1,0:T(8,128)(2,1)S(1)}, u32[]{:S(2)}, u32[]{:S(2)}) collective-permute-start(bf16[32,1152]{1,0:T(8,128)(2,1)} %constant_dynamic-update-slice_fusion), channel_id=1, source_target_pairs={{0,8},{1,9},{2,10},{3,11},{4,12},{5,13},{6,14},{7,15},{8,0},{9,1},... | collective-permute-start | bytes 221192 | tf_op jit(solution)/shard_map/ppermute | solution.py:594
  24.8 14.8 %collective-permute-start.6 = (bf16[32,1152]{1,0:T(8,128)(2,1)}, bf16[32,1152]{1,0:T(8,128)(2,1)S(1)}, u32[]{:S(2)}, u32[]{:S(2)}) collective-permute-start(bf16[32,1152]{1,0:T(8,128)(2,1)} %constant_dynamic-update-slice_fusion), channel_id=1, source_target_pairs={{0,4},{1,5},{2,6},{3,7},{4,0},{5,1},{6,2},{7,3},{8,12},{9,13},{10,... | collective-permute-start | bytes 221192 | tf_op jit(solution)/shard_map/ppermute | solution.py:594
  40.6 0.7 copy-start.9
  41.3 10.9 %collective-permute-start.10 = (bf16[4,32,1152]{2,1,0:T(8,128)(2,1)S(1)}, bf16[4,32,1152]{2,1,0:T(8,128)(2,1)}, u32[]{:S(2)}, u32[]{:S(2)}) collective-permute-start(bf16[4,32,1152]{2,1,0:T(8,128)(2,1)S(1)} %pad_maximum_fusion.7.pool_hbm), channel_id=1, source_target_pairs={{0,2},{1,3},{2,0},{3,1},{4,6},{5,7},{6,4},{7,5},{8,10},{9,11},{10,... | collective-permute-start | bytes 884744 | tf_op jit(solution)/shard_map/ppermute | solution.py:594
  41.5 22.7 %all-to-all-start.4 = ((bf16[16,16,1024]{2,1,0:T(8,128)(2,1)}), bf16[16,16,1024]{2,1,0:T(8,128)(2,1)}, u32[]{:S(2)}, u32[]{:S(2)}) async-start(bf16[16,16,1024]{2,1,0:T(8,128)(2,1)} %bitcast.61), calls=%async_computation.4 | async-start | bytes 1048576 | tf_op jit(solution)/shard_map/all_to_all | solution.py:26
  54.0 14.8 %collective-permute-start.11 = (bf16[8,32,1152]{2,1,0:T(8,128)(2,1)}, bf16[8,32,1152]{2,1,0:T(8,128)(2,1)}, u32[]{:S(2)}, u32[]{:S(2)}) collective-permute-start(bf16[8,32,1152]{2,1,0:T(8,128)(2,1)} %bitcast.58), channel_id=1, source_target_pairs={{0,1},{1,0},{2,3},{3,2},{4,5},{5,4},{6,7},{7,6},{8,9},{9,8},{10,11... | collective-permute-start | bytes 1769480 | tf_op jit(solution)/shard_map/ppermute | solution.py:594
  57.2 14.1 %collective-permute-start.12 = (bf16[256,1024]{1,0:T(8,128)(2,1)}, bf16[256,1024]{1,0:T(8,128)(2,1)}, u32[]{:S(2)}, u32[]{:S(2)}) collective-permute-start(bf16[256,1024]{1,0:T(8,128)(2,1)} %slice.21), channel_id=1, source_target_pairs={{0,16},{16,0},{1,17},{17,1},{2,18},{18,2},{3,19},{19,3},{4,20},{20... | collective-permute-start | bytes 1572872 | tf_op jit(solution)/shard_map/ppermute | solution.py:22
  64.2 20.5 %all-to-all-start.5 = ((bf16[16,16,1024]{2,1,0:T(8,128)(2,1)}), bf16[16,16,1024]{2,1,0:T(8,128)(2,1)}, u32[]{:S(2)}, u32[]{:S(2)}) async-start(bf16[16,16,1024]{2,1,0:T(8,128)(2,1)} %bitcast.60), calls=%async_computation.5 | async-start | bytes 1048576 | tf_op jit(solution)/shard_map/all_to_all | solution.py:26
  74.9 8.4 %collective-permute-start.13 = (bf16[384,384]{1,0:T(8,128)(2,1)}, bf16[384,384]{1,0:T(8,128)(2,1)}, u32[]{:S(2)}, u32[]{:S(2)}) collective-permute-start(bf16[384,384]{1,0:T(8,128)(2,1)} %get-tuple-element.111.hidden_hbm), channel_id=1, source_target_pairs={{0,16},{16,0},{1,17},{17,1},{2,18},{18,2},{3,19},{19,3},{4,20},{20... | collective-permute-start | bytes 884744 | tf_op jit(solution)/shard_map/ppermute | solution.py:22
  83.2 21.4 %collective-permute-start.14 = (bf16[272,1024]{1,0:T(8,128)(2,1)}, bf16[272,1024]{1,0:T(8,128)(2,1)}, u32[]{:S(2)}, u32[]{:S(2)}) collective-permute-start(bf16[272,1024]{1,0:T(8,128)(2,1)} %get-tuple-element.113), channel_id=1, source_target_pairs={{0,16},{16,0},{1,17},{17,1},{2,18},{18,2},{3,19},{19,3},{4,20},{20... | collective-permute-start | bytes 1671176 | tf_op jit(solution)/shard_map/ppermute | solution.py:22
  84.4 20.2 %collective-permute-start.15 = (bf16[256,768]{1,0:T(8,128)(2,1)}, bf16[256,768]{1,0:T(8,128)(2,1)}, u32[]{:S(2)}, u32[]{:S(2)}) collective-permute-start(bf16[256,768]{1,0:T(8,128)(2,1)} %get-tuple-element.107._one_hbm._other_hbm), channel_id=1, source_target_pairs={{0,16},{16,0},{1,17},{17,1},{2,18},{18,2},{3,19},{19,3},{4,20},{20... | collective-permute-start | bytes 1179656 | tf_op jit(solution)/shard_map/ppermute | solution.py:22
  90.7 20.3 %collective-permute-start.16 = (bf16[384,384]{1,0:T(8,128)(2,1)}, bf16[384,384]{1,0:T(8,128)(2,1)}, u32[]{:S(2)}, u32[]{:S(2)}) collective-permute-start(bf16[384,384]{1,0:T(8,128)(2,1)} %get-tuple-element.120), channel_id=1, source_target_pairs={{0,16},{16,0},{1,17},{17,1},{2,18},{18,2},{3,19},{19,3},{4,20},{20... | collective-permute-start | bytes 884744 | tf_op jit(solution)/shard_map/ppermute | solution.py:22
  91.9 44.3 %all-to-all-start.6 = ((bf16[16,24,2048]{2,1,0:T(8,128)(2,1)}), bf16[16,24,2048]{2,1,0:T(8,128)(2,1)}, u32[]{:S(2)}, u32[]{:S(2)}) async-start(bf16[16,24,2048]{2,1,0:T(8,128)(2,1)} %bitcast.56), calls=%async_computation.6 | async-start | bytes 3145728 | tf_op jit(solution)/shard_map/all_to_all | solution.py:26
  114.7 17.1 %collective-permute-start.17 = (bf16[384,1024]{1,0:T(8,128)(2,1)}, bf16[384,1024]{1,0:T(8,128)(2,1)}, u32[]{:S(2)}, u32[]{:S(2)}) collective-permute-start(bf16[384,1024]{1,0:T(8,128)(2,1)} %get-tuple-element.124.own_hbm), channel_id=1, source_target_pairs={{0,16},{16,0},{1,17},{17,1},{2,18},{18,2},{3,19},{19,3},{4,20},{20... | collective-permute-start | bytes 2359304 | tf_op jit(solution)/shard_map/ppermute | solution.py:22

commit v4 on v3

--- a/solution.py
+++ b/solution.py
@@ -252,16 +252,6 @@
     wait(move.start(pool, pool_hbm), *stores)
 
 
-def pool_rows(pool, marks, which, extra, half):
-    sources = pool.shape[0] // (4 * extra)
-    rows = row_index(sources * extra, pool.shape[0])
-    columns = lax.broadcasted_iota(jnp.int32, (sources * extra, pool.shape[0]), 1)
-    source = lax.shift_right_logical(rows, extra.bit_length() - 1) ^ lax.axis_index("expert")
-    target = source * (4 * extra) + which * extra + (rows & (extra - 1))
-    select = ((columns == target).astype(F32) * marks[0:1, 0:1]).astype(BF16)
-    return dot(select, pool[:, :half], (1, 0)).astype(BF16)
-
-
 def weight_copies(move, joined, own, other):
     half, hidden = own[0].shape
     return [
@@ -295,54 +285,87 @@
 
 
 def kernel_late(
-    extra,
-    pool_hbm, marks_hbm, hidden_hbm, gate_hbm, up_hbm, other_gate_hbm, other_up_hbm,
-    pre_hbm, late_hbm, packet_hbm,
-    pool, marks, joined, pre_at, rows, packet, sems,
+    lates_hbm, mark_hbm, base_hbm, _hidden_hbm, gate_hbm, up_hbm, other_gate_hbm, other_up_hbm,
+    pre_hbm, sent_hbm, late_hbm, send_hbm,
+    mark, joined, pre_at, sent, rows, send, sems,
 ):
     half = joined.shape[0] // 2
-    both = joined.shape[1]
     late = rows.shape[0]
-    move = Mover(sems)
-    pooled = [move.start(pool_hbm, pool), move.start(marks_hbm, marks)]
+    kept = base_hbm.shape[0]
+    move = Mover(sems)
+    pooled = [
+        move.start(source, target)
+        for source, target in (
+            (lates_hbm.at[0], rows),
+            (lates_hbm.at[1], send),
+            (mark_hbm, mark),
+        )
+    ]
+    above = move.start(base_hbm, sent.at[pl.ds(0, kept)])
     weights = weight_copies(move, joined, (gate_hbm, up_hbm), (other_gate_hbm, other_up_hbm))
     wait(*pooled)
-    rows[...] = pool_rows(pool, marks, 0, extra, half)
-    packet[:late] = pool_rows(pool, marks, 1, extra, half)
-    stores = [move.start(rows, late_hbm)]
+    stores = [move.start(rows, late_hbm), move.start(send, send_hbm)]
     wait(*weights[0])
     pre = dot(rows[...], joined[:half], (1, 0))
     wait(*weights[1])
-    pre = pre + dot(packet[:late], joined[half:], (1, 0))
+    pre = pre + dot(send[...], joined[half:], (1, 0))
     pre_at[...] = pre
-    stores.append(move.start(pre_at, pre_hbm))
-    packet[late : 2 * late, :both] = pre.astype(BF16)
-    packet[late : 2 * late, both:] = jnp.zeros((late, half - both), BF16)
-    mark = jnp.max(pool[:, half:].astype(F32), axis=0, keepdims=True)[:, :1]
-    packet[2 * late :] = jnp.broadcast_to(mark, (packet.shape[0] - 2 * late, half)).astype(BF16)
-    stores.append(move.start(packet, packet_hbm))
+    sent[kept : kept + late] = pre.astype(BF16)
+    sent[kept + late :] = jnp.broadcast_to(
+        mark[0:1, 0:1], (sent.shape[0] - kept - late, sent.shape[1])
+    ).astype(BF16)
+    wait(above)
+    stores += [move.start(pre_at, pre_hbm), move.start(sent, sent_hbm)]
     wait(*stores)
 
 
 def kernel_hidden(
-    extra,
-    recv_hbm, pool_hbm, marks_hbm, down_hbm, _rows_hbm,
+    recv_hbm, lates_hbm, down_hbm, _rows_hbm,
     sent_hbm, grads_hbm,
-    pool, marks, down, grads, sent, sems,
-):
-    half = down.shape[1]
+    down, grads, sent, sems,
+):
     kept = recv_hbm.shape[0]
     move = Mover(sems)
-    load = move.start(recv_hbm, grads.at[pl.ds(0, kept)])
-    small = [
-        move.start(source, target)
-        for source, target in ((pool_hbm, pool), (marks_hbm, marks), (down_hbm, down))
-    ]
-    wait(*small)
-    grads[kept:] = pool_rows(pool, marks, 3, extra, half)
-    wait(load)
+    wait(
+        move.start(recv_hbm, grads.at[pl.ds(0, kept)]),
+        move.start(lates_hbm.at[3], grads.at[pl.ds(kept, grads.shape[0] - kept)]),
+        move.start(down_hbm, down),
+    )
     sent[...] = dot(grads[...], down[...], (1, 1)).astype(BF16)
     wait(move.start(sent, sent_hbm), move.start(grads, grads_hbm))
+
+
+def kernel_pools(
+    extra,
+    pool_hbm, received_hbm, marks_hbm, _place_hbm,
+    lates_hbm, mark_hbm,
+    pool, marks, lates, mark_at, sems,
+):
+    kinds, late, half = lates.shape
+    blocks = pool.shape[0]
+    move = Mover(sems)
+    wait(
+        move.start(marks_hbm, marks),
+        *[
+            move.start(source, pool.at[:, part])
+            for part, source in enumerate((pool_hbm, received_hbm))
+        ],
+    )
+    entries = pool[...].reshape(2 * blocks * kinds * extra, pool.shape[-1])
+    total = entries.shape[0]
+    rows = row_index(total, 1)
+    bits = extra.bit_length() - 1
+    kind = lax.shift_right_logical(rows, late.bit_length() - 1)
+    source = lax.shift_right_logical(rows & (late - 1), bits) ^ lax.axis_index("expert")
+    target = source * (kinds * extra) + kind * extra + (rows & (extra - 1))
+    columns = lax.broadcasted_iota(jnp.int32, (total, total), 1)
+    select = ((columns == target).astype(F32) * marks[0:1, 0:1]).astype(BF16)
+    picked = dot(select, entries[:, :half], (1, 0)).astype(BF16)
+    for which in range(kinds):
+        lates[which] = picked[which * late : (which + 1) * late]
+    mark = jnp.max(entries[:, half:].astype(F32), axis=0, keepdims=True)
+    mark_at[...] = jnp.broadcast_to(mark, mark_at.shape)
+    wait(move.start(lates, lates_hbm), move.start(mark_at, mark_hbm))
 
 
 def kernel_stack(pool_hbm, received_hbm, _one_hbm, _other_hbm, stacked_hbm, pool, sems):
@@ -358,20 +381,23 @@
 
 def kernel_slot(
     base, depth,
-    recv_hbm, pool_hbm, marks_hbm, down_hbm, remote_hbm, pre_hbm, late_pre_hbm,
+    recv_hbm, lates_hbm, down_hbm, remote_hbm, pre_hbm, late_pre_hbm,
     gate_hbm, up_hbm, other_gate_hbm, other_up_hbm,
     slot_hbm, act_hbm, sides_hbm, hidden_hbm, grads_hbm,
-    pool, marks, down, remote, pre, joined, slot, act, sides, hidden_at, grads, sems,
+    down, remote, pre, joined, slot, act, sides, hidden_at, grads, sems,
 ):
     slots, hidden = act.shape
     half = grads.shape[1]
     extra = depth - base
     kept = recv_hbm.shape[0]
     move = Mover(sems)
-    load = move.start(recv_hbm, grads.at[pl.ds(0, kept)])
     first = [
         move.start(source, target)
-        for source, target in ((pool_hbm, pool), (marks_hbm, marks), (down_hbm, down))
+        for source, target in (
+            (recv_hbm, grads.at[pl.ds(0, kept)]),
+            (lates_hbm.at[2], grads.at[pl.ds(kept, slots - kept)]),
+            (down_hbm, down),
+        )
     ]
     second = [
         move.start(source, target)
@@ -383,8 +409,6 @@
     ]
     weights = weight_copies(move, joined, (gate_hbm, up_hbm), (other_gate_hbm, other_up_hbm))
     wait(*first)
-    grads[kept:] = pool_rows(pool, marks, 2, extra, half)
-    wait(load)
     stores = [move.start(grads, grads_hbm)]
     hidden_grad = dot(grads[...], down[...], (1, 1))
     wait(*second)
@@ -419,19 +443,14 @@
 
 
 def kernel_down(
-    pre_hbm, packet_hbm, hidden_hbm, act_hbm, grads_hbm, other_grads_hbm,
+    pre_hbm, hidden_hbm, act_hbm, grads_hbm, other_grads_hbm,
     down_hbm, sides_hbm,
     pre, hidden_at, act, grads, other_grads, down, sides, sems,
 ):
     slots, hidden = act.shape
-    kept = pre_hbm.shape[0]
     move = Mover(sems)
     first = [
-        move.start(pre_hbm, pre.at[pl.ds(0, kept)]),
-        move.start(
-            packet_hbm.at[pl.ds(slots - kept, slots - kept), pl.ds(0, 2 * hidden)],
-            pre.at[pl.ds(kept, slots - kept)],
-        ),
+        move.start(pre_hbm.at[pl.ds(0, slots)], pre),
         move.start(hidden_hbm, hidden_at),
     ]
     second = [
@@ -457,7 +476,7 @@
 
 
 def kernel_joined(
-    rows_hbm, late_rows_hbm, other_rows_hbm, packet_hbm, sides_hbm, other_sides_hbm,
+    rows_hbm, late_rows_hbm, other_rows_hbm, other_late_hbm, sides_hbm, other_sides_hbm,
     gate_hbm, up_hbm,
     rows, other_rows, sides, other_sides, joined, sems,
 ):
@@ -473,7 +492,7 @@
             (late_rows_hbm, rows.at[late]),
             (sides_hbm, sides),
             (other_rows_hbm, other_rows.at[base]),
-            (packet_hbm.at[pl.ds(0, slots - kept)], other_rows.at[late]),
+            (other_late_hbm, other_rows.at[late]),
             (other_sides_hbm, other_sides),
         )
     ]
@@ -618,70 +637,88 @@
         *own_weights,
         *other_weights,
     )
-    other_pre = swap(sent_pre)
-    while step > 1:
+    step //= 2
+    (pool,) = call(
+        kernel_stack,
+        (shape(4, 2, *pool.shape[1:]),),
+        (shape(4, 2, *pool.shape[1:]),),
+        3,
+        LATE_FLOPS,
+        pool,
+        from_distance(pool, step),
+        other_weights[1],
+        other_weights[0],
+    )
+    pool = pool.reshape(-1, *pool.shape[2:])
+    while step > 2:
         step //= 2
-        early = pool.shape[0] == 4
-        (pool,) = call(
-            kernel_stack,
-            (shape(pool.shape[0], 2, *pool.shape[1:]),),
-            (shape(pool.shape[0], 2, *pool.shape[1:]),),
-            3,
-            LATE_FLOPS if early else 0,
-            pool,
-            from_distance(pool, step),
-            *((other_weights[1], other_weights[0]) if early else (sent_pre, sent_pre)),
-        )
+        pool = jnp.stack([pool, from_distance(pool, step)], axis=1)
         pool = pool.reshape(-1, *pool.shape[2:])
-    pool = pool.reshape(-1, half + LANES)
-    grads_theirs, send_own, sent_pre = lax.optimization_barrier((grads_theirs, send_own, sent_pre))
+    late = slots - kept
+    lates, mark = call(
+        functools.partial(kernel_pools, extra),
+        (shape(4, late, half), marks_shape),
+        (
+            shape(pool.shape[0], 2, *pool.shape[1:]),
+            marks_shape,
+            shape(4, late, half),
+            marks_shape,
+        ),
+        5,
+        0,
+        pool,
+        from_distance(pool, 1),
+        marks,
+        sent_pre,
+    )
+    grads_theirs, send_own, sent_pre = lax.optimization_barrier(
+        (grads_theirs, send_own, sent_pre)
+    )
     recv_theirs = grads_theirs.reshape(kept, half)
     recv_own = exchange(send_own.reshape(experts, base, half), "expert").reshape(kept, half)
 
     sent, grads_theirs = call(
-        functools.partial(kernel_hidden, extra),
+        kernel_hidden,
         (by_hidden, rows_half),
-        (shape(*pool.shape), marks_shape, shape(hidden, half), rows_half, by_hidden),
-        6,
+        (shape(hidden, half), rows_half, by_hidden),
+        5,
         2 * slots * hidden * half,
         recv_theirs,
-        pool,
-        marks,
+        lates,
         w_down[0],
         other_rows,
     )
     remote = swap(sent)
-    late_pre, late_rows, packet = call(
-        functools.partial(kernel_late, extra),
+    late_pre, sent_late, late_rows, send_late = call(
+        kernel_late,
         (
             shape(late, 2 * hidden, dtype=F32),
+            shape(slots + 16, 2 * hidden),
             shape(late, half),
-            shape(2 * late + 16, half),
-        ),
-        (
-            shape(*pool.shape),
+            shape(late, half),
+        ),
+        (
             marks_shape,
             shape(width, 2 * hidden),
             shape(late, 2 * hidden, dtype=F32),
+            shape(slots + 16, 2 * hidden),
             shape(late, half),
-            shape(2 * late + 16, half),
-        ),
-        9,
-        4 * late * hidden * width,
-        pool,
-        marks,
+            shape(late, half),
+        ),
+        12,
+        6_000_000_000,
+        lates,
+        mark,
+        sent_pre,
         sent,
         *own_weights,
         *other_weights,
     )
-    remote, packet = lax.optimization_barrier((remote, packet))
-    other_packet = swap(packet)
+    other_pre = swap(sent_late)
     slot_grad, act, sides, hidden_grad, grads_own = call(
         functools.partial(kernel_slot, base, depth),
         (shape(slots, width), by_hidden, shape(slots, 2 * hidden), by_hidden, rows_half),
         (
-            shape(*pool.shape),
-            marks_shape,
             shape(hidden, half),
             by_hidden,
             shape(slots, 2 * hidden, dtype=F32),
@@ -695,8 +732,7 @@
         17,
         4 * slots * hidden * width,
         recv_own,
-        pool,
-        marks,
+        lates,
         w_down[0],
         remote,
         pre,
@@ -705,6 +741,8 @@
         *other_weights,
     )
     other_hidden = swap(hidden_grad)
+    hidden_grad, send_late = lax.optimization_barrier((hidden_grad, send_late))
+    other_late_rows = swap(send_late)
     returned = exchange(slot_grad.reshape(experts, depth, width), "expert").reshape(slots, width)
 
     own_down, other_sides = call(
@@ -722,12 +760,12 @@
         8,
         LATE_FLOPS,
         other_pre,
-        other_packet,
         other_hidden,
         act,
         grads_own,
         grads_theirs,
     )
+    own_down, other_late_rows = lax.optimization_barrier((own_down, other_late_rows))
     other_down = swap(own_down)
     gate_grad, up_grad = call(
         kernel_joined,
@@ -744,7 +782,7 @@
         rows_in,
         late_rows,
         other_rows,
-        other_packet,
+        other_late_rows,
         sides,
         other_sides,
     )
@@ -764,7 +802,7 @@
         own_down,
         other_down,
     )
-    crowded = jnp.maximum(jnp.max(packet[2 * late :]), jnp.max(other_packet[2 * late :])) > 0.0
+    crowded = jnp.maximum(jnp.max(sent_late[slots:]), jnp.max(other_pre[slots:])) > 0.0
     return crowded, (sum_choices(picked, per_token), gate_grad[None], up_grad[None], down_grad[None])
 
 

time: 140 us -> 140 us (level)
    all_to_all x4, waiting for transfers between devices: 6 us -> 10.1 us  [exchange(): return lax.all_to_all(x, axes, split_axis=0, concat_axis=0, tiled=True)]
    ppermute x9, waiting for transfers between devices: 28.1 us -> 24 us  [swap(): return lax.ppermute(x, 'dp', [(0, 1), (1, 0)])]
where the time goes in v4:
time: 140 us; the launch traced here: 139 us
  waiting for transfers between devices  48 us (34%)
  starting transfers between devices  41.4 us (30%)
  Pallas kernels  38.7 us (28%)
  local copies, waits for them, and re-layouts  4.58 us (3%)
  other arithmetic  3.64 us (3%)
  between operations  2.27 us (2%)
    pallas_call x11, Pallas kernels, call(): pl.pallas_call(kernel, out_shape=list(out_shapes), in_specs=[IN_HBM] * le...  38.7 us
    all_to_all x4, starting transfers between devices, exchange(): return lax.all_to_all(x, axes, split_axis=0, concat_axis=0, tiled=True)  28.3 us
    ppermute x9, waiting for transfers between devices, swap(): return lax.ppermute(x, 'dp', [(0, 1), (1, 0)])  24 us
    ppermute x5, waiting for transfers between devices, from_distance(): lax.ppermute(x, 'expert', [(at, at ^ distance) for at in range(experts)])  13.9 us
    all_to_all x4, waiting for transfers between devices, exchange(): return lax.all_to_all(x, axes, split_axis=0, concat_axis=0, tiled=True)  10.1 us
    ppermute x9, starting transfers between devices, swap(): return lax.ppermute(x, 'dp', [(0, 1), (1, 0)])  8.28 us
    ppermute x5, starting transfers between devices, from_distance(): lax.ppermute(x, 'expert', [(at, at ^ distance) for at in range(experts)])  4.75 us
  transfers between devices with their start and end apart: 18, of which 9 were waited for; matrix products, arithmetic and copies ran while one was open for 5% of the time, Pallas kernels for 24%

profile of v4, /device:TPU:13, one launch (start us, length us, event | category | flops | bytes accessed | tf_op | source)
XLA Modules:
  0.0 138.7 jit_solution(15715000212874528343)
XLA Ops:
  0.6 2.7 %shard_map.102 = (bf16[256,2048]{1,0:T(8,128)(2,1)}, bf16[16,1152]{1,0:T(8,128)(2,1)}, bf16[384,128]{1,0:T(8,128)(2,1)}, f32[8,128]{1,0:T(8,128)}, bf16[144,1024]{1,0:T(8,128)(2,1)}) custom-call(s32[1,128]{1,0:T(1,128)} %bitcast.65, f32[1,128]{1,0:T(1,128)} %bitcast.62, bf16[128,2048]{1,0:T(8,128)(2,1)} %tokens_hbm.1, bf16[128,2048]{1,0:T(8,128)(2,1)} %grad_hbm.3), custom_call_target="tpu_custom_call" | custom-call | flops 134217728 | bytes 2532352 | tf_op jit(solution)/shard_map/pallas_call | solution.py:85
  3.3 0.0 copy-start.12
  3.3 0.0 copy-start.10
  3.3 6.7 %all-to-all-start.3 = ((bf16[16,16,2048]{2,1,0:T(8,128)(2,1)}), bf16[16,16,2048]{2,1,0:T(8,128)(2,1)}, u32[]{:S(2)}, u32[]{:S(2)}) async-start(bf16[16,16,2048]{2,1,0:T(8,128)(2,1)} %bitcast.53), calls=%async_computation.3 | async-start | bytes 2097152 | tf_op jit(solution)/shard_map/all_to_all | solution.py:26
  10.0 0.0 copy-done.12
  10.0 1.3 collective-permute-start.5
  11.3 0.3 collective-permute-start.4
  11.6 1.2 collective-permute-start.10
  12.8 0.0 copy-done.10
  12.8 0.6 constant_dynamic-update-slice_fusion.1
  13.4 5.0 %collective-permute-done.5.other_hbm = bf16[144,1024]{1,0:T(8,128)(2,1)} collective-permute-done((bf16[144,1024]{1,0:T(8,128)(2,1)S(1)}, bf16[144,1024]{1,0:T(8,128)(2,1)}, u32[]{:S(2)}, u32[]{:S(2)}) %collective-permute-start.5) | collective-permute-done | bytes 294944 | tf_op jit(solution)/shard_map/ppermute | solution.py:22
  18.4 2.6 %shard_map.103 = (bf16[256,1024]{1,0:T(8,128)(2,1)}, bf16[256,1024]{1,0:T(8,128)(2,1)}, bf16[16,1152]{1,0:T(8,128)(2,1)}) custom-call(s32[1,128]{1,0:T(1,128)} %bitcast.66, f32[1,128]{1,0:T(1,128)} %bitcast.63, bf16[128,2048]{1,0:T(8,128)(2,1)} %grad_hbm.3, bf16[144,1024]{1,0:T(8,128)(2,1)} %collective-permute-done.5.other_hbm), custom_call_target="tpu_custom_call" | custom-call | flops 268435456 | bytes 1905664 | tf_op jit(solution)/shard_map/pallas_call | solution.py:85
  21.1 1.4 %constant_dynamic-update-slice_fusion = bf16[32,1152]{1,0:T(8,128)(2,1)} fusion(bf16[32,1152]{1,0:T(8,128)(2,1)} %constant_dynamic-update-slice_fusion.1, bf16[16,1152]{1,0:T(8,128)(2,1)} %get-tuple-element.107), kind=kLoop, calls=%fused_computation.50 | loop fusion | bytes 73728 | tf_op jit(solution)/shard_map/concatenate | solution.py:616
  22.5 1.2 collective-permute-start.8
  23.7 1.2 collective-permute-start.7
  24.8 0.9 collective-permute-start.6
  25.8 13.9 %collective-permute-done.8 = bf16[32,1152]{1,0:T(8,128)(2,1)S(1)} collective-permute-done((bf16[32,1152]{1,0:T(8,128)(2,1)}, bf16[32,1152]{1,0:T(8,128)(2,1)S(1)}, u32[]{:S(2)}, u32[]{:S(2)}) %collective-permute-start.8) | collective-permute-done | bytes 73760 | tf_op jit(solution)/shard_map/ppermute | solution.py:613
  39.6 0.0 collective-permute-done.7
  39.6 0.0 collective-permute-done.6
  39.6 0.9 pad_maximum_fusion.7.pool_hbm
  40.6 0.0 copy-start.9
  40.6 0.0 collective-permute-done.4._other_hbm.other_gate_hbm
  40.6 0.0 all-to-all-done.3
  40.6 0.7 copy-done.9
  41.3 0.2 collective-permute-start.9
  41.5 8.7 %all-to-all-start.4 = ((bf16[16,16,1024]{2,1,0:T(8,128)(2,1)}), bf16[16,16,1024]{2,1,0:T(8,128)(2,1)}, u32[]{:S(2)}, u32[]{:S(2)}) async-start(bf16[16,16,1024]{2,1,0:T(8,128)(2,1)} %bitcast.57), calls=%async_computation.4 | async-start | bytes 1048576 | tf_op jit(solution)/shard_map/all_to_all | solution.py:26
  50.2 2.0 %collective-permute-done.10._one_hbm.other_up_hbm = bf16[1024,384]{1,0:T(8,128)(2,1)} collective-permute-done((bf16[1024,384]{1,0:T(8,128)(2,1)}, bf16[1024,384]{1,0:T(8,128)(2,1)}, u32[]{:S(2)}, u32[]{:S(2)}) %collective-permute-start.10) | collective-permute-done | bytes 786464 | tf_op jit(solution)/shard_map/ppermute | solution.py:22
  52.1 0.0 collective-permute-done.9.received_hbm
  52.1 1.9 %shard_map.104 = bf16[4,2,32,1152]{3,2,1,0:T(8,128)(2,1)} custom-call(bf16[4,32,1152]{2,1,0:T(8,128)(2,1)} %copy-done.9, bf16[4,32,1152]{2,1,0:T(8,128)(2,1)} %collective-permute-done.9.received_hbm, bf16[1024,384]{1,0:T(8,128)(2,1)} %collective-permute-done.10._one_hbm.other_up_hbm, bf16[1024,384]{1,0:T(8,128)(2,1)} %collective-permute-done.4._other_hbm.other_gate_hbm), custom_call_target="tpu_custom_call" | custom-call | flops 99999997952 | bytes 2752512 | tf_op jit(solution)/shard_map/pallas_call | solution.py:85
  54.0 1.3 collective-permute-start.11
  55.3 1.9 %slice.21 = bf16[256,1024]{1,0:T(8,128)(2,1)} slice(bf16[256,2048]{1,0:T(8,128)(2,1)} %bitcast.17.rows_hbm), slice={[0:256], [1024:2048]} | slice | bytes 1048576 | tf_op jit(solution)/shard_map/slice | solution.py:623
  57.2 1.2 collective-permute-start.12
  58.4 4.2 %shard_map.105 = (f32[256,768]{1,0:T(8,128)}, bf16[256,768]{1,0:T(8,128)(2,1)}) custom-call(bf16[256,2048]{1,0:T(8,128)(2,1)} %bitcast.17.rows_hbm, bf16[1024,384]{1,0:T(8,128)(2,1)} %bitcast.18.gate_hbm, bf16[1024,384]{1,0:T(8,128)(2,1)} %bitcast.23.up_hbm, bf16[1024,384]{1,0:T(8,128)(2,1)} %collective-permute-done.4._other_hbm.other_gate_hbm, ...), custom_call_target="tpu_custom_call" | custom-call | bytes 5373952 | tf_op jit(solution)/shard_map/pallas_call | solution.py:85
  62.6 1.6 %all-to-all-done.4 = bf16[16,16,1024]{2,1,0:T(8,128)(2,1)} async-done(((bf16[16,16,1024]{2,1,0:T(8,128)(2,1)}), bf16[16,16,1024]{2,1,0:T(8,128)(2,1)}, u32[]{:S(2)}, u32[]{:S(2)}) %all-to-all-start.4) | async-done | bytes 524320 | tf_op jit(solution)/shard_map/all_to_all | solution.py:26
  64.2 4.7 %all-to-all-start.5 = ((bf16[16,16,1024]{2,1,0:T(8,128)(2,1)}), bf16[16,16,1024]{2,1,0:T(8,128)(2,1)}, u32[]{:S(2)}, u32[]{:S(2)}) async-start(bf16[16,16,1024]{2,1,0:T(8,128)(2,1)} %bitcast.56), calls=%async_computation.5 | async-start | bytes 1048576 | tf_op jit(solution)/shard_map/all_to_all | solution.py:26
  68.9 0.0 collective-permute-done.11.received_hbm
  68.9 3.0 %shard_map.106 = (bf16[4,128,1024]{2,1,0:T(8,128)(2,1)}, f32[8,128]{1,0:T(8,128)}) custom-call(bf16[8,32,1152]{2,1,0:T(8,128)(2,1)} %bitcast.55, bf16[8,32,1152]{2,1,0:T(8,128)(2,1)} %collective-permute-done.11.received_hbm, f32[8,128]{1,0:T(8,128)} %get-tuple-element.110.marks_hbm, bf16[256,768]{1,0:T(8,128)(2,1)} %get-tuple-element.117._place_hbm.base_hbm), custom_call_target="tpu_custom_call" | custom-call | bytes 2629632 | tf_op jit(solution)/shard_map/pallas_call | solution.py:85
  71.9 0.0 collective-permute-done.12._rows_hbm.other_rows_hbm
  72.0 3.0 %shard_map.107 = (bf16[384,384]{1,0:T(8,128)(2,1)}, bf16[384,1024]{1,0:T(8,128)(2,1)}) custom-call(bf16[256,1024]{1,0:T(8,128)(2,1)} %bitcast.26.recv_hbm, bf16[4,128,1024]{2,1,0:T(8,128)(2,1)} %get-tuple-element.113.lates_hbm, bf16[384,1024]{1,0:T(8,128)(2,1)} %bitcast.27.down_hbm, bf16[256,1024]{1,0:T(8,128)(2,1)} %collective-permute-done.12._rows_hbm.other_rows_hbm), custom_call_target="tpu_custom_call" | custom-call | flops 301989888 | bytes 3964928 | tf_op jit(solution)/shard_map/pallas_call | solution.py:85
  75.0 1.3 collective-permute-start.14
  76.2 4.0 %shard_map.108 = (f32[128,768]{1,0:T(8,128)}, bf16[400,768]{1,0:T(8,128)(2,1)}, bf16[128,1024]{1,0:T(8,128)(2,1)}, bf16[128,1024]{1,0:T(8,128)(2,1)}) custom-call(bf16[4,128,1024]{2,1,0:T(8,128)(2,1)} %get-tuple-element.113.lates_hbm, f32[8,128]{1,0:T(8,128)} %get-tuple-element.114.mark_hbm, bf16[256,768]{1,0:T(8,128)(2,1)} %get-tuple-element.117._place_hbm.base_hbm, ...), custom_call_target="tpu_custom_call" | custom-call | flops 6000000000 | bytes 6418432 | tf_op jit(solution)/shard_map/pallas_call | solution.py:85
  80.2 0.3 collective-permute-start.13
  80.5 3.0 %collective-permute-done.14.remote_hbm = bf16[384,384]{1,0:T(8,128)(2,1)} collective-permute-done((bf16[384,384]{1,0:T(8,128)(2,1)}, bf16[384,384]{1,0:T(8,128)(2,1)}, u32[]{:S(2)}, u32[]{:S(2)}) %collective-permute-start.14) | collective-permute-done | bytes 294944 | tf_op jit(solution)/shard_map/ppermute | solution.py:22
  83.6 0.0 all-to-all-done.5
  83.6 5.7 %shard_map.109 = (bf16[384,2048]{1,0:T(8,128)(2,1)}, bf16[384,384]{1,0:T(8,128)(2,1)}, bf16[384,768]{1,0:T(8,128)(2,1)}, bf16[384,384]{1,0:T(8,128)(2,1)}, bf16[384,1024]{1,0:T(8,128)(2,1)}) custom-call(bf16[256,1024]{1,0:T(8,128)(2,1)} %bitcast.29.recv_hbm, bf16[4,128,1024]{2,1,0:T(8,128)(2,1)} %get-tuple-element.113.lates_hbm, ...), custom_call_target="tpu_custom_call" | custom-call | flops 1207959552 | bytes 10518528 | tf_op jit(solution)/shard_map/pallas_call | solution.py:85
  89.3 1.3 collective-permute-start.15
  90.6 0.3 collective-permute-start.16
  90.8 8.2 %all-to-all-start.6 = ((bf16[16,24,2048]{2,1,0:T(8,128)(2,1)}), bf16[16,24,2048]{2,1,0:T(8,128)(2,1)}, u32[]{:S(2)}, u32[]{:S(2)}) async-start(bf16[16,24,2048]{2,1,0:T(8,128)(2,1)} %bitcast.52), calls=%async_computation.6 | async-start | bytes 3145728 | tf_op jit(solution)/shard_map/all_to_all | solution.py:26
  99.1 0.0 collective-permute-done.13.pre_hbm
  99.1 4.0 %collective-permute-done.15.hidden_hbm = bf16[384,384]{1,0:T(8,128)(2,1)} collective-permute-done((bf16[384,384]{1,0:T(8,128)(2,1)}, bf16[384,384]{1,0:T(8,128)(2,1)}, u32[]{:S(2)}, u32[]{:S(2)}) %collective-permute-start.15) | collective-permute-done | bytes 294944 | tf_op jit(solution)/shard_map/ppermute | solution.py:22
  103.1 3.7 %shard_map.110 = (bf16[384,1024]{1,0:T(8,128)(2,1)}, bf16[384,768]{1,0:T(8,128)(2,1)}) custom-call(bf16[400,768]{1,0:T(8,128)(2,1)} %collective-permute-done.13.pre_hbm, bf16[384,384]{1,0:T(8,128)(2,1)} %collective-permute-done.15.hidden_hbm, bf16[384,384]{1,0:T(8,128)(2,1)} %get-tuple-element.127.act_hbm, bf16[384,1024]{1,0:T(8,128)(2,1)} %get-tuple-element.128.grads_hbm, ...), custom_call_target="tpu_custom_call" | custom-call | flops 99999997952 | bytes 4153344 | tf_op jit(solution)/shard_map/pallas_call | solution.py:85
  106.8 1.9 %collective-permute-done.16.other_late_hbm = bf16[128,1024]{1,0:T(8,128)(2,1)} collective-permute-done((bf16[128,1024]{1,0:T(8,128)(2,1)}, bf16[128,1024]{1,0:T(8,128)(2,1)}, u32[]{:S(2)}, u32[]{:S(2)}) %collective-permute-start.16) | collective-permute-done | bytes 262176 | tf_op jit(solution)/shard_map/ppermute | solution.py:22
  108.7 1.2 collective-permute-start.17
  109.9 1.4 slice_reduce_fusion.1
  111.2 1.4 slice_reduce_fusion
  113.9 4.8 %shard_map.112 = (bf16[1024,384]{1,0:T(8,128)(2,1)}, bf16[1024,384]{1,0:T(8,128)(2,1)}) custom-call(bf16[256,2048]{1,0:T(8,128)(2,1)} %bitcast.17.rows_hbm, bf16[128,1024]{1,0:T(8,128)(2,1)} %get-tuple-element.135.late_rows_hbm, bf16[256,1024]{1,0:T(8,128)(2,1)} %collective-permute-done.12._rows_hbm.other_rows_hbm, ...), custom_call_target="tpu_custom_call" | custom-call | flops 1207959552 | bytes 4849664 | tf_op jit(solution)/shard_map/pallas_call | solution.py:85
  118.8 8.1 %collective-permute-done.17.other_hbm = bf16[384,1024]{1,0:T(8,128)(2,1)} collective-permute-done((bf16[384,1024]{1,0:T(8,128)(2,1)}, bf16[384,1024]{1,0:T(8,128)(2,1)}, u32[]{:S(2)}, u32[]{:S(2)}) %collective-permute-start.17) | collective-permute-done | bytes 786464 | tf_op jit(solution)/shard_map/ppermute | solution.py:22
  126.8 8.5 %all-to-all-done.6 = bf16[16,24,2048]{2,1,0:T(8,128)(2,1)} async-done(((bf16[16,24,2048]{2,1,0:T(8,128)(2,1)}), bf16[16,24,2048]{2,1,0:T(8,128)(2,1)}, u32[]{:S(2)}, u32[]{:S(2)}) %all-to-all-start.6) | async-done | bytes 1572896 | tf_op jit(solution)/shard_map/all_to_all | solution.py:26
  135.3 3.0 %shard_map.111 = (bf16[128,2048]{1,0:T(8,128)(2,1)}, bf16[384,2048]{1,0:T(8,128)(2,1)}) custom-call(bf16[384,128]{1,0:T(8,128)(2,1)} %get-tuple-element.121.place_hbm, bf16[384,2048]{1,0:T(8,128)(2,1)} %bitcast.31.returned_hbm, bf16[384,1024]{1,0:T(8,128)(2,1)} %get-tuple-element.133.own_hbm, bf16[384,1024]{1,0:T(8,128)(2,1)} %collective-permute-done.17.other_hbm), custom_call_target="tpu_custom_call" | custom-call | flops 201326592 | bytes 5341184 | tf_op jit(solution)/shard_map/pallas_call | solution.py:85
  138.4 0.2 while.15
Async XLA Ops:
  3.3 6.7 %copy-start.12 = (bf16[144,1024]{1,0:T(8,128)(2,1)S(1)}, bf16[144,1024]{1,0:T(8,128)(2,1)}, u32[]{:S(2)}) copy-start(bf16[144,1024]{1,0:T(8,128)(2,1)} %get-tuple-element.104) | copy-start | bytes 884740
  3.3 9.5 %copy-start.10 = (bf16[16,1152]{1,0:T(8,128)(2,1)S(1)}, bf16[16,1152]{1,0:T(8,128)(2,1)}, u32[]{:S(2)}) copy-start(bf16[16,1152]{1,0:T(8,128)(2,1)} %get-tuple-element.106) | copy-start | bytes 110596
  3.3 37.2 %all-to-all-start.3 = ((bf16[16,16,2048]{2,1,0:T(8,128)(2,1)}), bf16[16,16,2048]{2,1,0:T(8,128)(2,1)}, u32[]{:S(2)}, u32[]{:S(2)}) async-start(bf16[16,16,2048]{2,1,0:T(8,128)(2,1)} %bitcast.53), calls=%async_computation.3 | async-start | bytes 2097152 | tf_op jit(solution)/shard_map/all_to_all | solution.py:26
  10.0 8.4 %collective-permute-start.5 = (bf16[144,1024]{1,0:T(8,128)(2,1)S(1)}, bf16[144,1024]{1,0:T(8,128)(2,1)}, u32[]{:S(2)}, u32[]{:S(2)}) collective-permute-start(bf16[144,1024]{1,0:T(8,128)(2,1)S(1)} %copy-done.12), channel_id=1, source_target_pairs={{0,16},{16,0},{1,17},{17,1},{2,18},{18,2},{3,19},{19,3},{4,20},{20... | collective-permute-start | bytes 884744 | tf_op jit(solution)/shard_map/ppermute | solution.py:22
  11.3 29.3 %collective-permute-start.4 = (bf16[1024,384]{1,0:T(8,128)(2,1)}, bf16[1024,384]{1,0:T(8,128)(2,1)}, u32[]{:S(2)}, u32[]{:S(2)}) collective-permute-start(bf16[1024,384]{1,0:T(8,128)(2,1)} %bitcast.18.gate_hbm), channel_id=1, source_target_pairs={{0,16},{16,0},{1,17},{17,1},{2,18},{18,2},{3,19},{19,3},{4,20},{20... | collective-permute-start | bytes 2359304 | tf_op jit(solution)/shard_map/ppermute | solution.py:22
  11.6 40.6 %collective-permute-start.10 = (bf16[1024,384]{1,0:T(8,128)(2,1)}, bf16[1024,384]{1,0:T(8,128)(2,1)}, u32[]{:S(2)}, u32[]{:S(2)}) collective-permute-start(bf16[1024,384]{1,0:T(8,128)(2,1)} %bitcast.23.up_hbm), channel_id=1, source_target_pairs={{0,16},{16,0},{1,17},{17,1},{2,18},{18,2},{3,19},{19,3},{4,20},{20... | collective-permute-start | bytes 2359304 | tf_op jit(solution)/shard_map/ppermute | solution.py:22
  22.5 17.1 %collective-permute-start.8 = (bf16[32,1152]{1,0:T(8,128)(2,1)}, bf16[32,1152]{1,0:T(8,128)(2,1)S(1)}, u32[]{:S(2)}, u32[]{:S(2)}) collective-permute-start(bf16[32,1152]{1,0:T(8,128)(2,1)} %constant_dynamic-update-slice_fusion), channel_id=1, source_target_pairs={{0,12},{1,13},{2,14},{3,15},{4,8},{5,9},{6,10},{7,11},{8,4},{9,5},... | collective-permute-start | bytes 221192 | tf_op jit(solution)/shard_map/ppermute | solution.py:613
  23.7 15.9 %collective-permute-start.7 = (bf16[32,1152]{1,0:T(8,128)(2,1)}, bf16[32,1152]{1,0:T(8,128)(2,1)S(1)}, u32[]{:S(2)}, u32[]{:S(2)}) collective-permute-start(bf16[32,1152]{1,0:T(8,128)(2,1)} %constant_dynamic-update-slice_fusion), channel_id=1, source_target_pairs={{0,8},{1,9},{2,10},{3,11},{4,12},{5,13},{6,14},{7,15},{8,0},{9,1},... | collective-permute-start | bytes 221192 | tf_op jit(solution)/shard_map/ppermute | solution.py:613
  24.8 14.8 %collective-permute-start.6 = (bf16[32,1152]{1,0:T(8,128)(2,1)}, bf16[32,1152]{1,0:T(8,128)(2,1)S(1)}, u32[]{:S(2)}, u32[]{:S(2)}) collective-permute-start(bf16[32,1152]{1,0:T(8,128)(2,1)} %constant_dynamic-update-slice_fusion), channel_id=1, source_target_pairs={{0,4},{1,5},{2,6},{3,7},{4,0},{5,1},{6,2},{7,3},{8,12},{9,13},{10,... | collective-permute-start | bytes 221192 | tf_op jit(solution)/shard_map/ppermute | solution.py:613
  40.6 0.7 copy-start.9
  41.3 10.9 %collective-permute-start.9 = (bf16[4,32,1152]{2,1,0:T(8,128)(2,1)S(1)}, bf16[4,32,1152]{2,1,0:T(8,128)(2,1)}, u32[]{:S(2)}, u32[]{:S(2)}) collective-permute-start(bf16[4,32,1152]{2,1,0:T(8,128)(2,1)S(1)} %pad_maximum_fusion.7.pool_hbm), channel_id=1, source_target_pairs={{0,2},{1,3},{2,0},{3,1},{4,6},{5,7},{6,4},{7,5},{8,10},{9,11},{10,... | collective-permute-start | bytes 884744 | tf_op jit(solution)/shard_map/ppermute | solution.py:613
  41.5 22.7 %all-to-all-start.4 = ((bf16[16,16,1024]{2,1,0:T(8,128)(2,1)}), bf16[16,16,1024]{2,1,0:T(8,128)(2,1)}, u32[]{:S(2)}, u32[]{:S(2)}) async-start(bf16[16,16,1024]{2,1,0:T(8,128)(2,1)} %bitcast.57), calls=%async_computation.4 | async-start | bytes 1048576 | tf_op jit(solution)/shard_map/all_to_all | solution.py:26
  54.0 14.9 %collective-permute-start.11 = (bf16[8,32,1152]{2,1,0:T(8,128)(2,1)}, bf16[8,32,1152]{2,1,0:T(8,128)(2,1)}, u32[]{:S(2)}, u32[]{:S(2)}) collective-permute-start(bf16[8,32,1152]{2,1,0:T(8,128)(2,1)} %bitcast.54), channel_id=1, source_target_pairs={{0,1},{1,0},{2,3},{3,2},{4,5},{5,4},{6,7},{7,6},{8,9},{9,8},{10,11... | collective-permute-start | bytes 1769480 | tf_op jit(solution)/shard_map/ppermute | solution.py:613
  57.2 14.8 %collective-permute-start.12 = (bf16[256,1024]{1,0:T(8,128)(2,1)}, bf16[256,1024]{1,0:T(8,128)(2,1)}, u32[]{:S(2)}, u32[]{:S(2)}) collective-permute-start(bf16[256,1024]{1,0:T(8,128)(2,1)} %slice.21), channel_id=1, source_target_pairs={{0,16},{16,0},{1,17},{17,1},{2,18},{18,2},{3,19},{19,3},{4,20},{20... | collective-permute-start | bytes 1572872 | tf_op jit(solution)/shard_map/ppermute | solution.py:22
  64.2 19.4 %all-to-all-start.5 = ((bf16[16,16,1024]{2,1,0:T(8,128)(2,1)}), bf16[16,16,1024]{2,1,0:T(8,128)(2,1)}, u32[]{:S(2)}, u32[]{:S(2)}) async-start(bf16[16,16,1024]{2,1,0:T(8,128)(2,1)} %bitcast.56), calls=%async_computation.5 | async-start | bytes 1048576 | tf_op jit(solution)/shard_map/all_to_all | solution.py:26
  75.0 8.6 %collective-permute-start.14 = (bf16[384,384]{1,0:T(8,128)(2,1)}, bf16[384,384]{1,0:T(8,128)(2,1)}, u32[]{:S(2)}, u32[]{:S(2)}) collective-permute-start(bf16[384,384]{1,0:T(8,128)(2,1)} %get-tuple-element.119._hidden_hbm), channel_id=1, source_target_pairs={{0,16},{16,0},{1,17},{17,1},{2,18},{18,2},{3,19},{19,3},{4,20},{20... | collective-permute-start | bytes 884744 | tf_op jit(solution)/shard_map/ppermute | solution.py:22
  80.2 18.9 %collective-permute-start.13 = (bf16[400,768]{1,0:T(8,128)(2,1)}, bf16[400,768]{1,0:T(8,128)(2,1)}, u32[]{:S(2)}, u32[]{:S(2)}) collective-permute-start(bf16[400,768]{1,0:T(8,128)(2,1)} %get-tuple-element.120), channel_id=1, source_target_pairs={{0,16},{16,0},{1,17},{17,1},{2,18},{18,2},{3,19},{19,3},{4,20},{20... | collective-permute-start | bytes 1843208 | tf_op jit(solution)/shard_map/ppermute | solution.py:22
  89.3 13.8 %collective-permute-start.15 = (bf16[384,384]{1,0:T(8,128)(2,1)}, bf16[384,384]{1,0:T(8,128)(2,1)}, u32[]{:S(2)}, u32[]{:S(2)}) collective-permute-start(bf16[384,384]{1,0:T(8,128)(2,1)} %get-tuple-element.126), channel_id=1, source_target_pairs={{0,16},{16,0},{1,17},{17,1},{2,18},{18,2},{3,19},{19,3},{4,20},{20... | collective-permute-start | bytes 884744 | tf_op jit(solution)/shard_map/ppermute | solution.py:22
  90.6 18.1 %collective-permute-start.16 = (bf16[128,1024]{1,0:T(8,128)(2,1)}, bf16[128,1024]{1,0:T(8,128)(2,1)}, u32[]{:S(2)}, u32[]{:S(2)}) collective-permute-start(bf16[128,1024]{1,0:T(8,128)(2,1)} %get-tuple-element.132), channel_id=1, source_target_pairs={{0,16},{16,0},{1,17},{17,1},{2,18},{18,2},{3,19},{19,3},{4,20},{20... | collective-permute-start | bytes 786440 | tf_op jit(solution)/shard_map/ppermute | solution.py:22
  90.8 44.5 %all-to-all-start.6 = ((bf16[16,24,2048]{2,1,0:T(8,128)(2,1)}), bf16[16,24,2048]{2,1,0:T(8,128)(2,1)}, u32[]{:S(2)}, u32[]{:S(2)}) async-start(bf16[16,24,2048]{2,1,0:T(8,128)(2,1)} %bitcast.52), calls=%async_computation.6 | async-start | bytes 3145728 | tf_op jit(solution)/shard_map/all_to_all | solution.py:26
  108.7 18.2 %collective-permute-start.17 = (bf16[384,1024]{1,0:T(8,128)(2,1)}, bf16[384,1024]{1,0:T(8,128)(2,1)}, u32[]{:S(2)}, u32[]{:S(2)}) collective-permute-start(bf16[384,1024]{1,0:T(8,128)(2,1)} %get-tuple-element.133.own_hbm), channel_id=1, source_target_pairs={{0,16},{16,0},{1,17},{17,1},{2,18},{18,2},{3,19},{19,3},{4,20},{20... | collective-permute-start | bytes 2359304 | tf_op jit(solution)/shard_map/ppermute | solution.py:22

commit v5 on v4

--- a/solution.py
+++ b/solution.py
@@ -285,7 +285,7 @@
 
 
 def kernel_late(
-    lates_hbm, mark_hbm, base_hbm, _hidden_hbm, gate_hbm, up_hbm, other_gate_hbm, other_up_hbm,
+    lates_hbm, mark_hbm, base_hbm, _hidden_hbm, _rows_hbm, gate_hbm, up_hbm, other_gate_hbm, other_up_hbm,
     pre_hbm, sent_hbm, late_hbm, send_hbm,
     mark, joined, pre_at, sent, rows, send, sems,
 ):
@@ -319,31 +319,18 @@
     wait(*stores)
 
 
-def kernel_hidden(
-    recv_hbm, lates_hbm, down_hbm, _rows_hbm,
-    sent_hbm, grads_hbm,
-    down, grads, sent, sems,
-):
-    kept = recv_hbm.shape[0]
-    move = Mover(sems)
-    wait(
-        move.start(recv_hbm, grads.at[pl.ds(0, kept)]),
-        move.start(lates_hbm.at[3], grads.at[pl.ds(kept, grads.shape[0] - kept)]),
-        move.start(down_hbm, down),
-    )
-    sent[...] = dot(grads[...], down[...], (1, 1)).astype(BF16)
-    wait(move.start(sent, sent_hbm), move.start(grads, grads_hbm))
-
-
 def kernel_pools(
     extra,
-    pool_hbm, received_hbm, marks_hbm, _place_hbm,
-    lates_hbm, mark_hbm,
-    pool, marks, lates, mark_at, sems,
+    pool_hbm, received_hbm, marks_hbm, recv_hbm, down_hbm, _place_hbm,
+    sent_hbm, grads_hbm, lates_hbm, mark_hbm,
+    pool, marks, lates, mark_at, down, grads, sent, sems,
 ):
-    kinds, late, half = lates.shape
+    late, half = lates.shape[1:]
+    kinds = lates.shape[0] + 1
     blocks = pool.shape[0]
-    move = Mover(sems)
+    kept = recv_hbm.shape[0]
+    move = Mover(sems)
+    loads = [move.start(recv_hbm, grads.at[pl.ds(0, kept)]), move.start(down_hbm, down)]
     wait(
         move.start(marks_hbm, marks),
         *[
@@ -361,11 +348,15 @@
     columns = lax.broadcasted_iota(jnp.int32, (total, total), 1)
     select = ((columns == target).astype(F32) * marks[0:1, 0:1]).astype(BF16)
     picked = dot(select, entries[:, :half], (1, 0)).astype(BF16)
-    for which in range(kinds):
+    grads[kept:] = picked[(kinds - 1) * late :]
+    wait(*loads)
+    sent[...] = dot(grads[...], down[...], (1, 1)).astype(BF16)
+    stores = [move.start(sent, sent_hbm), move.start(grads, grads_hbm)]
+    for which in range(kinds - 1):
         lates[which] = picked[which * late : (which + 1) * late]
     mark = jnp.max(entries[:, half:].astype(F32), axis=0, keepdims=True)
     mark_at[...] = jnp.broadcast_to(mark, mark_at.shape)
-    wait(move.start(lates, lates_hbm), move.start(mark_at, mark_hbm))
+    wait(move.start(lates, lates_hbm), move.start(mark_at, mark_hbm), *stores)
 
 
 def kernel_stack(pool_hbm, received_hbm, _one_hbm, _other_hbm, stacked_hbm, pool, sems):
@@ -655,38 +646,33 @@
         pool = jnp.stack([pool, from_distance(pool, step)], axis=1)
         pool = pool.reshape(-1, *pool.shape[2:])
     late = slots - kept
-    lates, mark = call(
+    other_half_pool = from_distance(pool, 1)
+    grads_theirs, send_own, sent_pre = lax.optimization_barrier(
+        (grads_theirs, send_own, sent_pre)
+    )
+    recv_theirs = grads_theirs.reshape(kept, half)
+    recv_own = exchange(send_own.reshape(experts, base, half), "expert").reshape(kept, half)
+
+    sent, grads_theirs, lates, mark = call(
         functools.partial(kernel_pools, extra),
-        (shape(4, late, half), marks_shape),
+        (by_hidden, rows_half, shape(3, late, half), marks_shape),
         (
             shape(pool.shape[0], 2, *pool.shape[1:]),
             marks_shape,
-            shape(4, late, half),
+            shape(3, late, half),
             marks_shape,
-        ),
-        5,
-        0,
+            shape(hidden, half),
+            rows_half,
+            by_hidden,
+        ),
+        9,
+        2 * slots * hidden * half,
         pool,
-        from_distance(pool, 1),
+        other_half_pool,
         marks,
+        recv_theirs,
+        w_down[0],
         sent_pre,
-    )
-    grads_theirs, send_own, sent_pre = lax.optimization_barrier(
-        (grads_theirs, send_own, sent_pre)
-    )
-    recv_theirs = grads_theirs.reshape(kept, half)
-    recv_own = exchange(send_own.reshape(experts, base, half), "expert").reshape(kept, half)
-
-    sent, grads_theirs = call(
-        kernel_hidden,
-        (by_hidden, rows_half),
-        (shape(hidden, half), rows_half, by_hidden),
-        5,
-        2 * slots * hidden * half,
-        recv_theirs,
-        lates,
-        w_down[0],
-        other_rows,
     )
     remote = swap(sent)
     late_pre, sent_late, late_rows, send_late = call(
@@ -711,6 +697,7 @@
         mark,
         sent_pre,
         sent,
+        other_rows,
         *own_weights,
         *other_weights,
     )

time: 140 us -> 138 us (0.986)
  Pallas kernels: 38.7 us -> 37 us
    pallas_call x11 -> x10, Pallas kernels: 38.7 us -> 37 us  [call(): pl.pallas_call(kernel, out_shape=list(out_shapes), in_specs=[IN_HBM] * le...]
  transfers between devices with their start and end apart: 18 -> 18, of which waited for: 9 -> 10; matrix products, arithmetic and copies ran while one was open for 5% -> 6% of each run, Pallas kernels for 24% -> 23%
where the time goes in v5:
time: 138 us; the launch traced here: 137 us
  waiting for transfers between devices  49 us (36%)
  starting transfers between devices  40.3 us (29%)
  Pallas kernels  37 us (27%)
  local copies, waits for them, and re-layouts  4.6 us (3%)
  other arithmetic  3.64 us (3%)
  between operations  2.25 us (2%)
    pallas_call x10, Pallas kernels, call(): pl.pallas_call(kernel, out_shape=list(out_shapes), in_specs=[IN_HBM] * le...  37 us
    all_to_all x4, starting transfers between devices, exchange(): return lax.all_to_all(x, axes, split_axis=0, concat_axis=0, tiled=True)  27.3 us
    ppermute x9, waiting for transfers between devices, swap(): return lax.ppermute(x, 'dp', [(0, 1), (1, 0)])  24 us
    ppermute x5, waiting for transfers between devices, from_distance(): lax.ppermute(x, 'expert', [(at, at ^ distance) for at in range(experts)])  13.9 us
    all_to_all x4, waiting for transfers between devices, exchange(): return lax.all_to_all(x, axes, split_axis=0, concat_axis=0, tiled=True)  11.1 us
    ppermute x9, starting transfers between devices, swap(): return lax.ppermute(x, 'dp', [(0, 1), (1, 0)])  8.28 us
    ppermute x5, starting transfers between devices, from_distance(): lax.ppermute(x, 'expert', [(at, at ^ distance) for at in range(experts)])  4.75 us
  transfers between devices with their start and end apart: 18, of which 10 were waited for; matrix products, arithmetic and copies ran while one was open for 6% of the time, Pallas kernels for 23%

profile of v5, /device:TPU:13, one launch (start us, length us, event | category | flops | bytes accessed | tf_op | source)
XLA Modules:
  0.0 137.0 jit_solution(2043081927940500148)
XLA Ops:
  0.6 2.7 %shard_map.102 = (bf16[256,2048]{1,0:T(8,128)(2,1)}, bf16[16,1152]{1,0:T(8,128)(2,1)}, bf16[384,128]{1,0:T(8,128)(2,1)}, f32[8,128]{1,0:T(8,128)}, bf16[144,1024]{1,0:T(8,128)(2,1)}) custom-call(s32[1,128]{1,0:T(1,128)} %bitcast.65, f32[1,128]{1,0:T(1,128)} %bitcast.62, bf16[128,2048]{1,0:T(8,128)(2,1)} %tokens_hbm.1, bf16[128,2048]{1,0:T(8,128)(2,1)} %grad_hbm.3), custom_call_target="tpu_custom_call" | custom-call | flops 134217728 | bytes 2532352 | tf_op jit(solution)/shard_map/pallas_call | solution.py:85
  3.3 0.0 copy-start.12
  3.3 0.0 copy-start.10
  3.3 6.7 %all-to-all-start.3 = ((bf16[16,16,2048]{2,1,0:T(8,128)(2,1)}), bf16[16,16,2048]{2,1,0:T(8,128)(2,1)}, u32[]{:S(2)}, u32[]{:S(2)}) async-start(bf16[16,16,2048]{2,1,0:T(8,128)(2,1)} %bitcast.53), calls=%async_computation.3 | async-start | bytes 2097152 | tf_op jit(solution)/shard_map/all_to_all | solution.py:26
  10.0 0.0 copy-done.12
  10.0 1.3 collective-permute-start.5
  11.3 0.3 collective-permute-start.4
  11.6 1.2 collective-permute-start.10
  12.8 0.0 copy-done.10
  12.8 0.6 constant_dynamic-update-slice_fusion.1
  13.4 5.0 %collective-permute-done.5.other_hbm = bf16[144,1024]{1,0:T(8,128)(2,1)} collective-permute-done((bf16[144,1024]{1,0:T(8,128)(2,1)S(1)}, bf16[144,1024]{1,0:T(8,128)(2,1)}, u32[]{:S(2)}, u32[]{:S(2)}) %collective-permute-start.5) | collective-permute-done | bytes 294944 | tf_op jit(solution)/shard_map/ppermute | solution.py:22
  18.4 2.6 %shard_map.103 = (bf16[256,1024]{1,0:T(8,128)(2,1)}, bf16[256,1024]{1,0:T(8,128)(2,1)}, bf16[16,1152]{1,0:T(8,128)(2,1)}) custom-call(s32[1,128]{1,0:T(1,128)} %bitcast.66, f32[1,128]{1,0:T(1,128)} %bitcast.63, bf16[128,2048]{1,0:T(8,128)(2,1)} %grad_hbm.3, bf16[144,1024]{1,0:T(8,128)(2,1)} %collective-permute-done.5.other_hbm), custom_call_target="tpu_custom_call" | custom-call | flops 268435456 | bytes 1905664 | tf_op jit(solution)/shard_map/pallas_call | solution.py:85
  21.1 1.4 %constant_dynamic-update-slice_fusion = bf16[32,1152]{1,0:T(8,128)(2,1)} fusion(bf16[32,1152]{1,0:T(8,128)(2,1)} %constant_dynamic-update-slice_fusion.1, bf16[16,1152]{1,0:T(8,128)(2,1)} %get-tuple-element.107), kind=kLoop, calls=%fused_computation.50 | loop fusion | bytes 73728 | tf_op jit(solution)/shard_map/concatenate | solution.py:607
  22.5 1.2 collective-permute-start.8
  23.6 1.2 collective-permute-start.7
  24.8 0.9 collective-permute-start.6
  25.7 13.9 %collective-permute-done.8 = bf16[32,1152]{1,0:T(8,128)(2,1)S(1)} collective-permute-done((bf16[32,1152]{1,0:T(8,128)(2,1)}, bf16[32,1152]{1,0:T(8,128)(2,1)S(1)}, u32[]{:S(2)}, u32[]{:S(2)}) %collective-permute-start.8) | collective-permute-done | bytes 73760 | tf_op jit(solution)/shard_map/ppermute | solution.py:604
  39.6 0.0 collective-permute-done.7
  39.6 0.0 collective-permute-done.6
  39.6 0.9 pad_maximum_fusion.7.pool_hbm
  40.5 0.0 copy-start.9
  40.6 0.0 collective-permute-done.4._other_hbm.other_gate_hbm
  40.6 0.0 all-to-all-done.3
  40.6 0.7 copy-done.9
  41.3 0.2 collective-permute-start.9
  41.5 8.7 %all-to-all-start.4 = ((bf16[16,16,1024]{2,1,0:T(8,128)(2,1)}), bf16[16,16,1024]{2,1,0:T(8,128)(2,1)}, u32[]{:S(2)}, u32[]{:S(2)}) async-start(bf16[16,16,1024]{2,1,0:T(8,128)(2,1)} %bitcast.57), calls=%async_computation.4 | async-start | bytes 1048576 | tf_op jit(solution)/shard_map/all_to_all | solution.py:26
  50.2 2.0 %collective-permute-done.10._one_hbm.other_up_hbm = bf16[1024,384]{1,0:T(8,128)(2,1)} collective-permute-done((bf16[1024,384]{1,0:T(8,128)(2,1)}, bf16[1024,384]{1,0:T(8,128)(2,1)}, u32[]{:S(2)}, u32[]{:S(2)}) %collective-permute-start.10) | collective-permute-done | bytes 786464 | tf_op jit(solution)/shard_map/ppermute | solution.py:22
  52.1 0.0 collective-permute-done.9.received_hbm
  52.1 1.9 %shard_map.104 = bf16[4,2,32,1152]{3,2,1,0:T(8,128)(2,1)} custom-call(bf16[4,32,1152]{2,1,0:T(8,128)(2,1)} %copy-done.9, bf16[4,32,1152]{2,1,0:T(8,128)(2,1)} %collective-permute-done.9.received_hbm, bf16[1024,384]{1,0:T(8,128)(2,1)} %collective-permute-done.10._one_hbm.other_up_hbm, bf16[1024,384]{1,0:T(8,128)(2,1)} %collective-permute-done.4._other_hbm.other_gate_hbm), custom_call_target="tpu_custom_call" | custom-call | flops 99999997952 | bytes 2752512 | tf_op jit(solution)/shard_map/pallas_call | solution.py:85
  54.0 1.3 collective-permute-start.11
  55.3 1.9 %slice.21 = bf16[256,1024]{1,0:T(8,128)(2,1)} slice(bf16[256,2048]{1,0:T(8,128)(2,1)} %bitcast.17.rows_hbm), slice={[0:256], [1024:2048]} | slice | bytes 1048576 | tf_op jit(solution)/shard_map/slice | solution.py:614
  57.2 1.2 collective-permute-start.12
  58.4 4.2 %shard_map.105 = (f32[256,768]{1,0:T(8,128)}, bf16[256,768]{1,0:T(8,128)(2,1)}) custom-call(bf16[256,2048]{1,0:T(8,128)(2,1)} %bitcast.17.rows_hbm, bf16[1024,384]{1,0:T(8,128)(2,1)} %bitcast.18.gate_hbm, bf16[1024,384]{1,0:T(8,128)(2,1)} %bitcast.23.up_hbm, bf16[1024,384]{1,0:T(8,128)(2,1)} %collective-permute-done.4._other_hbm.other_gate_hbm, ...), custom_call_target="tpu_custom_call" | custom-call | bytes 5373952 | tf_op jit(solution)/shard_map/pallas_call | solution.py:85
  62.6 1.6 %all-to-all-done.4 = bf16[16,16,1024]{2,1,0:T(8,128)(2,1)} async-done(((bf16[16,16,1024]{2,1,0:T(8,128)(2,1)}), bf16[16,16,1024]{2,1,0:T(8,128)(2,1)}, u32[]{:S(2)}, u32[]{:S(2)}) %all-to-all-start.4) | async-done | bytes 524320 | tf_op jit(solution)/shard_map/all_to_all | solution.py:26
  64.2 4.7 %all-to-all-start.5 = ((bf16[16,16,1024]{2,1,0:T(8,128)(2,1)}), bf16[16,16,1024]{2,1,0:T(8,128)(2,1)}, u32[]{:S(2)}, u32[]{:S(2)}) async-start(bf16[16,16,1024]{2,1,0:T(8,128)(2,1)} %bitcast.56), calls=%async_computation.5 | async-start | bytes 1048576 | tf_op jit(solution)/shard_map/all_to_all | solution.py:26
  68.9 0.0 collective-permute-done.11.received_hbm
  68.9 4.3 %shard_map.106 = (bf16[384,384]{1,0:T(8,128)(2,1)}, bf16[384,1024]{1,0:T(8,128)(2,1)}, bf16[3,128,1024]{2,1,0:T(8,128)(2,1)}, f32[8,128]{1,0:T(8,128)}) custom-call(bf16[8,32,1152]{2,1,0:T(8,128)(2,1)} %bitcast.55, bf16[8,32,1152]{2,1,0:T(8,128)(2,1)} %collective-permute-done.11.received_hbm, f32[8,128]{1,0:T(8,128)} %get-tuple-element.110.marks_hbm, ...), custom_call_target="tpu_custom_call" | custom-call | flops 301989888 | bytes 4759552 | tf_op jit(solution)/shard_map/pallas_call | solution.py:85
  73.2 1.3 collective-permute-start.14
  74.5 0.0 collective-permute-done.12._rows_hbm.other_rows_hbm
  74.5 4.0 %shard_map.107 = (f32[128,768]{1,0:T(8,128)}, bf16[400,768]{1,0:T(8,128)(2,1)}, bf16[128,1024]{1,0:T(8,128)(2,1)}, bf16[128,1024]{1,0:T(8,128)(2,1)}) custom-call(bf16[3,128,1024]{2,1,0:T(8,128)(2,1)} %get-tuple-element.117.lates_hbm, f32[8,128]{1,0:T(8,128)} %get-tuple-element.118.mark_hbm, bf16[256,768]{1,0:T(8,128)(2,1)} %get-tuple-element.116._place_hbm.base_hbm, ...), custom_call_target="tpu_custom_call" | custom-call | flops 6000000000 | bytes 6680576 | tf_op jit(solution)/shard_map/pallas_call | solution.py:85
  78.5 0.3 collective-permute-start.13
  78.8 3.0 %collective-permute-done.14.remote_hbm = bf16[384,384]{1,0:T(8,128)(2,1)} collective-permute-done((bf16[384,384]{1,0:T(8,128)(2,1)}, bf16[384,384]{1,0:T(8,128)(2,1)}, u32[]{:S(2)}, u32[]{:S(2)}) %collective-permute-start.14) | collective-permute-done | bytes 294944 | tf_op jit(solution)/shard_map/ppermute | solution.py:22
  81.8 1.0 all-to-all-done.5
  82.9 5.7 %shard_map.108 = (bf16[384,2048]{1,0:T(8,128)(2,1)}, bf16[384,384]{1,0:T(8,128)(2,1)}, bf16[384,768]{1,0:T(8,128)(2,1)}, bf16[384,384]{1,0:T(8,128)(2,1)}, bf16[384,1024]{1,0:T(8,128)(2,1)}) custom-call(bf16[256,1024]{1,0:T(8,128)(2,1)} %bitcast.29.recv_hbm, bf16[3,128,1024]{2,1,0:T(8,128)(2,1)} %get-tuple-element.117.lates_hbm, ...), custom_call_target="tpu_custom_call" | custom-call | flops 1207959552 | bytes 10256384 | tf_op jit(solution)/shard_map/pallas_call | solution.py:85
  88.6 1.3 collective-permute-start.15
  89.9 0.3 collective-permute-start.16
  90.1 7.2 %all-to-all-start.6 = ((bf16[16,24,2048]{2,1,0:T(8,128)(2,1)}), bf16[16,24,2048]{2,1,0:T(8,128)(2,1)}, u32[]{:S(2)}, u32[]{:S(2)}) async-start(bf16[16,24,2048]{2,1,0:T(8,128)(2,1)} %bitcast.52), calls=%async_computation.6 | async-start | bytes 3145728 | tf_op jit(solution)/shard_map/all_to_all | solution.py:26
  97.3 0.0 collective-permute-done.13.pre_hbm
  97.3 4.0 %collective-permute-done.15.hidden_hbm = bf16[384,384]{1,0:T(8,128)(2,1)} collective-permute-done((bf16[384,384]{1,0:T(8,128)(2,1)}, bf16[384,384]{1,0:T(8,128)(2,1)}, u32[]{:S(2)}, u32[]{:S(2)}) %collective-permute-start.15) | collective-permute-done | bytes 294944 | tf_op jit(solution)/shard_map/ppermute | solution.py:22
  101.3 3.7 %shard_map.109 = (bf16[384,1024]{1,0:T(8,128)(2,1)}, bf16[384,768]{1,0:T(8,128)(2,1)}) custom-call(bf16[400,768]{1,0:T(8,128)(2,1)} %collective-permute-done.13.pre_hbm, bf16[384,384]{1,0:T(8,128)(2,1)} %collective-permute-done.15.hidden_hbm, bf16[384,384]{1,0:T(8,128)(2,1)} %get-tuple-element.127.act_hbm, bf16[384,1024]{1,0:T(8,128)(2,1)} %get-tuple-element.128.grads_hbm, ...), custom_call_target="tpu_custom_call" | custom-call | flops 99999997952 | bytes 4153344 | tf_op jit(solution)/shard_map/pallas_call | solution.py:85
  105.1 1.9 %collective-permute-done.16.other_late_hbm = bf16[128,1024]{1,0:T(8,128)(2,1)} collective-permute-done((bf16[128,1024]{1,0:T(8,128)(2,1)}, bf16[128,1024]{1,0:T(8,128)(2,1)}, u32[]{:S(2)}, u32[]{:S(2)}) %collective-permute-start.16) | collective-permute-done | bytes 262176 | tf_op jit(solution)/shard_map/ppermute | solution.py:22
  107.0 1.2 collective-permute-start.17
  108.2 1.4 slice_reduce_fusion.1
  109.5 1.4 slice_reduce_fusion
  112.2 4.8 %shard_map.111 = (bf16[1024,384]{1,0:T(8,128)(2,1)}, bf16[1024,384]{1,0:T(8,128)(2,1)}) custom-call(bf16[256,2048]{1,0:T(8,128)(2,1)} %bitcast.17.rows_hbm, bf16[128,1024]{1,0:T(8,128)(2,1)} %get-tuple-element.135.late_rows_hbm, bf16[256,1024]{1,0:T(8,128)(2,1)} %collective-permute-done.12._rows_hbm.other_rows_hbm, ...), custom_call_target="tpu_custom_call" | custom-call | flops 1207959552 | bytes 4849664 | tf_op jit(solution)/shard_map/pallas_call | solution.py:85
  117.0 8.1 %collective-permute-done.17.other_hbm = bf16[384,1024]{1,0:T(8,128)(2,1)} collective-permute-done((bf16[384,1024]{1,0:T(8,128)(2,1)}, bf16[384,1024]{1,0:T(8,128)(2,1)}, u32[]{:S(2)}, u32[]{:S(2)}) %collective-permute-start.17) | collective-permute-done | bytes 786464 | tf_op jit(solution)/shard_map/ppermute | solution.py:22
  125.1 8.5 %all-to-all-done.6 = bf16[16,24,2048]{2,1,0:T(8,128)(2,1)} async-done(((bf16[16,24,2048]{2,1,0:T(8,128)(2,1)}), bf16[16,24,2048]{2,1,0:T(8,128)(2,1)}, u32[]{:S(2)}, u32[]{:S(2)}) %all-to-all-start.6) | async-done | bytes 1572896 | tf_op jit(solution)/shard_map/all_to_all | solution.py:26
  133.6 3.0 %shard_map.110 = (bf16[128,2048]{1,0:T(8,128)(2,1)}, bf16[384,2048]{1,0:T(8,128)(2,1)}) custom-call(bf16[384,128]{1,0:T(8,128)(2,1)} %get-tuple-element.121.place_hbm, bf16[384,2048]{1,0:T(8,128)(2,1)} %bitcast.31.returned_hbm, bf16[384,1024]{1,0:T(8,128)(2,1)} %get-tuple-element.133.own_hbm, bf16[384,1024]{1,0:T(8,128)(2,1)} %collective-permute-done.17.other_hbm), custom_call_target="tpu_custom_call" | custom-call | flops 201326592 | bytes 5341184 | tf_op jit(solution)/shard_map/pallas_call | solution.py:85
  136.7 0.2 while.15
Async XLA Ops:
  3.3 6.7 %copy-start.12 = (bf16[144,1024]{1,0:T(8,128)(2,1)S(1)}, bf16[144,1024]{1,0:T(8,128)(2,1)}, u32[]{:S(2)}) copy-start(bf16[144,1024]{1,0:T(8,128)(2,1)} %get-tuple-element.104) | copy-start | bytes 884740
  3.3 9.5 %copy-start.10 = (bf16[16,1152]{1,0:T(8,128)(2,1)S(1)}, bf16[16,1152]{1,0:T(8,128)(2,1)}, u32[]{:S(2)}) copy-start(bf16[16,1152]{1,0:T(8,128)(2,1)} %get-tuple-element.106) | copy-start | bytes 110596
  3.3 37.2 %all-to-all-start.3 = ((bf16[16,16,2048]{2,1,0:T(8,128)(2,1)}), bf16[16,16,2048]{2,1,0:T(8,128)(2,1)}, u32[]{:S(2)}, u32[]{:S(2)}) async-start(bf16[16,16,2048]{2,1,0:T(8,128)(2,1)} %bitcast.53), calls=%async_computation.3 | async-start | bytes 2097152 | tf_op jit(solution)/shard_map/all_to_all | solution.py:26
  10.0 8.4 %collective-permute-start.5 = (bf16[144,1024]{1,0:T(8,128)(2,1)S(1)}, bf16[144,1024]{1,0:T(8,128)(2,1)}, u32[]{:S(2)}, u32[]{:S(2)}) collective-permute-start(bf16[144,1024]{1,0:T(8,128)(2,1)S(1)} %copy-done.12), channel_id=1, source_target_pairs={{0,16},{16,0},{1,17},{17,1},{2,18},{18,2},{3,19},{19,3},{4,20},{20... | collective-permute-start | bytes 884744 | tf_op jit(solution)/shard_map/ppermute | solution.py:22
  11.3 29.3 %collective-permute-start.4 = (bf16[1024,384]{1,0:T(8,128)(2,1)}, bf16[1024,384]{1,0:T(8,128)(2,1)}, u32[]{:S(2)}, u32[]{:S(2)}) collective-permute-start(bf16[1024,384]{1,0:T(8,128)(2,1)} %bitcast.18.gate_hbm), channel_id=1, source_target_pairs={{0,16},{16,0},{1,17},{17,1},{2,18},{18,2},{3,19},{19,3},{4,20},{20... | collective-permute-start | bytes 2359304 | tf_op jit(solution)/shard_map/ppermute | solution.py:22
  11.6 40.6 %collective-permute-start.10 = (bf16[1024,384]{1,0:T(8,128)(2,1)}, bf16[1024,384]{1,0:T(8,128)(2,1)}, u32[]{:S(2)}, u32[]{:S(2)}) collective-permute-start(bf16[1024,384]{1,0:T(8,128)(2,1)} %bitcast.23.up_hbm), channel_id=1, source_target_pairs={{0,16},{16,0},{1,17},{17,1},{2,18},{18,2},{3,19},{19,3},{4,20},{20... | collective-permute-start | bytes 2359304 | tf_op jit(solution)/shard_map/ppermute | solution.py:22
  22.5 17.1 %collective-permute-start.8 = (bf16[32,1152]{1,0:T(8,128)(2,1)}, bf16[32,1152]{1,0:T(8,128)(2,1)S(1)}, u32[]{:S(2)}, u32[]{:S(2)}) collective-permute-start(bf16[32,1152]{1,0:T(8,128)(2,1)} %constant_dynamic-update-slice_fusion), channel_id=1, source_target_pairs={{0,12},{1,13},{2,14},{3,15},{4,8},{5,9},{6,10},{7,11},{8,4},{9,5},... | collective-permute-start | bytes 221192 | tf_op jit(solution)/shard_map/ppermute | solution.py:604
  23.6 16.0 %collective-permute-start.7 = (bf16[32,1152]{1,0:T(8,128)(2,1)}, bf16[32,1152]{1,0:T(8,128)(2,1)S(1)}, u32[]{:S(2)}, u32[]{:S(2)}) collective-permute-start(bf16[32,1152]{1,0:T(8,128)(2,1)} %constant_dynamic-update-slice_fusion), channel_id=1, source_target_pairs={{0,8},{1,9},{2,10},{3,11},{4,12},{5,13},{6,14},{7,15},{8,0},{9,1},... | collective-permute-start | bytes 221192 | tf_op jit(solution)/shard_map/ppermute | solution.py:604
  24.8 14.8 %collective-permute-start.6 = (bf16[32,1152]{1,0:T(8,128)(2,1)}, bf16[32,1152]{1,0:T(8,128)(2,1)S(1)}, u32[]{:S(2)}, u32[]{:S(2)}) collective-permute-start(bf16[32,1152]{1,0:T(8,128)(2,1)} %constant_dynamic-update-slice_fusion), channel_id=1, source_target_pairs={{0,4},{1,5},{2,6},{3,7},{4,0},{5,1},{6,2},{7,3},{8,12},{9,13},{10,... | collective-permute-start | bytes 221192 | tf_op jit(solution)/shard_map/ppermute | solution.py:604
  40.5 0.7 copy-start.9
  41.3 10.9 %collective-permute-start.9 = (bf16[4,32,1152]{2,1,0:T(8,128)(2,1)S(1)}, bf16[4,32,1152]{2,1,0:T(8,128)(2,1)}, u32[]{:S(2)}, u32[]{:S(2)}) collective-permute-start(bf16[4,32,1152]{2,1,0:T(8,128)(2,1)S(1)} %pad_maximum_fusion.7.pool_hbm), channel_id=1, source_target_pairs={{0,2},{1,3},{2,0},{3,1},{4,6},{5,7},{6,4},{7,5},{8,10},{9,11},{10,... | collective-permute-start | bytes 884744 | tf_op jit(solution)/shard_map/ppermute | solution.py:604
  41.5 22.7 %all-to-all-start.4 = ((bf16[16,16,1024]{2,1,0:T(8,128)(2,1)}), bf16[16,16,1024]{2,1,0:T(8,128)(2,1)}, u32[]{:S(2)}, u32[]{:S(2)}) async-start(bf16[16,16,1024]{2,1,0:T(8,128)(2,1)} %bitcast.57), calls=%async_computation.4 | async-start | bytes 1048576 | tf_op jit(solution)/shard_map/all_to_all | solution.py:26
  54.0 14.8 %collective-permute-start.11 = (bf16[8,32,1152]{2,1,0:T(8,128)(2,1)}, bf16[8,32,1152]{2,1,0:T(8,128)(2,1)}, u32[]{:S(2)}, u32[]{:S(2)}) collective-permute-start(bf16[8,32,1152]{2,1,0:T(8,128)(2,1)} %bitcast.54), channel_id=1, source_target_pairs={{0,1},{1,0},{2,3},{3,2},{4,5},{5,4},{6,7},{7,6},{8,9},{9,8},{10,11... | collective-permute-start | bytes 1769480 | tf_op jit(solution)/shard_map/ppermute | solution.py:604
  57.2 17.3 %collective-permute-start.12 = (bf16[256,1024]{1,0:T(8,128)(2,1)}, bf16[256,1024]{1,0:T(8,128)(2,1)}, u32[]{:S(2)}, u32[]{:S(2)}) collective-permute-start(bf16[256,1024]{1,0:T(8,128)(2,1)} %slice.21), channel_id=1, source_target_pairs={{0,16},{16,0},{1,17},{17,1},{2,18},{18,2},{3,19},{19,3},{4,20},{20... | collective-permute-start | bytes 1572872 | tf_op jit(solution)/shard_map/ppermute | solution.py:22
  64.2 18.7 %all-to-all-start.5 = ((bf16[16,16,1024]{2,1,0:T(8,128)(2,1)}), bf16[16,16,1024]{2,1,0:T(8,128)(2,1)}, u32[]{:S(2)}, u32[]{:S(2)}) async-start(bf16[16,16,1024]{2,1,0:T(8,128)(2,1)} %bitcast.56), calls=%async_computation.5 | async-start | bytes 1048576 | tf_op jit(solution)/shard_map/all_to_all | solution.py:26
  73.2 8.6 %collective-permute-start.14 = (bf16[384,384]{1,0:T(8,128)(2,1)}, bf16[384,384]{1,0:T(8,128)(2,1)}, u32[]{:S(2)}, u32[]{:S(2)}) collective-permute-start(bf16[384,384]{1,0:T(8,128)(2,1)} %get-tuple-element.119._hidden_hbm), channel_id=1, source_target_pairs={{0,16},{16,0},{1,17},{17,1},{2,18},{18,2},{3,19},{19,3},{4,20},{20... | collective-permute-start | bytes 884744 | tf_op jit(solution)/shard_map/ppermute | solution.py:22
  78.5 18.8 %collective-permute-start.13 = (bf16[400,768]{1,0:T(8,128)(2,1)}, bf16[400,768]{1,0:T(8,128)(2,1)}, u32[]{:S(2)}, u32[]{:S(2)}) collective-permute-start(bf16[400,768]{1,0:T(8,128)(2,1)} %get-tuple-element.120), channel_id=1, source_target_pairs={{0,16},{16,0},{1,17},{17,1},{2,18},{18,2},{3,19},{19,3},{4,20},{20... | collective-permute-start | bytes 1843208 | tf_op jit(solution)/shard_map/ppermute | solution.py:22
  88.6 12.7 %collective-permute-start.15 = (bf16[384,384]{1,0:T(8,128)(2,1)}, bf16[384,384]{1,0:T(8,128)(2,1)}, u32[]{:S(2)}, u32[]{:S(2)}) collective-permute-start(bf16[384,384]{1,0:T(8,128)(2,1)} %get-tuple-element.126), channel_id=1, source_target_pairs={{0,16},{16,0},{1,17},{17,1},{2,18},{18,2},{3,19},{19,3},{4,20},{20... | collective-permute-start | bytes 884744 | tf_op jit(solution)/shard_map/ppermute | solution.py:22
  89.9 17.1 %collective-permute-start.16 = (bf16[128,1024]{1,0:T(8,128)(2,1)}, bf16[128,1024]{1,0:T(8,128)(2,1)}, u32[]{:S(2)}, u32[]{:S(2)}) collective-permute-start(bf16[128,1024]{1,0:T(8,128)(2,1)} %get-tuple-element.132), channel_id=1, source_target_pairs={{0,16},{16,0},{1,17},{17,1},{2,18},{18,2},{3,19},{19,3},{4,20},{20... | collective-permute-start | bytes 786440 | tf_op jit(solution)/shard_map/ppermute | solution.py:22
  90.1 43.5 %all-to-all-start.6 = ((bf16[16,24,2048]{2,1,0:T(8,128)(2,1)}), bf16[16,24,2048]{2,1,0:T(8,128)(2,1)}, u32[]{:S(2)}, u32[]{:S(2)}) async-start(bf16[16,24,2048]{2,1,0:T(8,128)(2,1)} %bitcast.52), calls=%async_computation.6 | async-start | bytes 3145728 | tf_op jit(solution)/shard_map/all_to_all | solution.py:26
  107.0 18.2 %collective-permute-start.17 = (bf16[384,1024]{1,0:T(8,128)(2,1)}, bf16[384,1024]{1,0:T(8,128)(2,1)}, u32[]{:S(2)}, u32[]{:S(2)}) collective-permute-start(bf16[384,1024]{1,0:T(8,128)(2,1)} %get-tuple-element.133.own_hbm), channel_id=1, source_target_pairs={{0,16},{16,0},{1,17},{17,1},{2,18},{18,2},{3,19},{19,3},{4,20},{20... | collective-permute-start | bytes 2359304 | tf_op jit(solution)/shard_map/ppermute | solution.py:22

commit v6 on v5

--- a/solution.py
+++ b/solution.py
@@ -285,25 +285,24 @@
 
 
 def kernel_late(
-    lates_hbm, mark_hbm, base_hbm, _hidden_hbm, _rows_hbm, gate_hbm, up_hbm, other_gate_hbm, other_up_hbm,
+    extra,
+    pool_hbm, received_hbm, marks_hbm, base_hbm, _hidden_hbm, _rows_hbm, gate_hbm, up_hbm, other_gate_hbm, other_up_hbm,
     pre_hbm, sent_hbm, late_hbm, send_hbm,
-    mark, joined, pre_at, sent, rows, send, sems,
+    pool, marks, joined, pre_at, sent, rows, send, sems,
 ):
     half = joined.shape[0] // 2
     late = rows.shape[0]
     kept = base_hbm.shape[0]
     move = Mover(sems)
-    pooled = [
-        move.start(source, target)
-        for source, target in (
-            (lates_hbm.at[0], rows),
-            (lates_hbm.at[1], send),
-            (mark_hbm, mark),
-        )
-    ]
+    pooled = [move.start(marks_hbm, marks), *pool_copies(move, pool, pool_hbm, received_hbm)]
     above = move.start(base_hbm, sent.at[pl.ds(0, kept)])
     weights = weight_copies(move, joined, (gate_hbm, up_hbm), (other_gate_hbm, other_up_hbm))
     wait(*pooled)
+    entries = pool[...].reshape(4 * late, pool.shape[-1])
+    picked = two_kinds(entries, marks, 0, extra, half)
+    rows[...] = picked[:late]
+    send[...] = picked[late:]
+    mark = jnp.max(entries[:, half:].astype(F32), axis=0, keepdims=True)
     stores = [move.start(rows, late_hbm), move.start(send, send_hbm)]
     wait(*weights[0])
     pre = dot(rows[...], joined[:half], (1, 0))
@@ -319,44 +318,45 @@
     wait(*stores)
 
 
+def pool_copies(move, pool, pool_hbm, received_hbm):
+    return [
+        move.start(source, pool.at[:, part]) for part, source in enumerate((pool_hbm, received_hbm))
+    ]
+
+
+def two_kinds(entries, marks, first, extra, half):
+    late = entries.shape[0] // 4
+    rows = row_index(2 * late, 1)
+    bits = extra.bit_length() - 1
+    kind = first + lax.shift_right_logical(rows, late.bit_length() - 1)
+    source = lax.shift_right_logical(rows & (late - 1), bits) ^ lax.axis_index("expert")
+    target = source * (4 * extra) + kind * extra + (rows & (extra - 1))
+    columns = lax.broadcasted_iota(jnp.int32, (2 * late, 4 * late), 1)
+    select = ((columns == target).astype(F32) * marks[0:1, 0:1]).astype(BF16)
+    return dot(select, entries[:, :half], (1, 0)).astype(BF16)
+
+
 def kernel_pools(
     extra,
     pool_hbm, received_hbm, marks_hbm, recv_hbm, down_hbm, _place_hbm,
-    sent_hbm, grads_hbm, lates_hbm, mark_hbm,
-    pool, marks, lates, mark_at, down, grads, sent, sems,
+    sent_hbm, grads_hbm, own_hbm,
+    pool, marks, own, down, grads, sent, sems,
 ):
-    late, half = lates.shape[1:]
-    kinds = lates.shape[0] + 1
-    blocks = pool.shape[0]
+    late, half = own.shape
     kept = recv_hbm.shape[0]
     move = Mover(sems)
+    pooled = [move.start(marks_hbm, marks), *pool_copies(move, pool, pool_hbm, received_hbm)]
     loads = [move.start(recv_hbm, grads.at[pl.ds(0, kept)]), move.start(down_hbm, down)]
-    wait(
-        move.start(marks_hbm, marks),
-        *[
-            move.start(source, pool.at[:, part])
-            for part, source in enumerate((pool_hbm, received_hbm))
-        ],
-    )
-    entries = pool[...].reshape(2 * blocks * kinds * extra, pool.shape[-1])
-    total = entries.shape[0]
-    rows = row_index(total, 1)
-    bits = extra.bit_length() - 1
-    kind = lax.shift_right_logical(rows, late.bit_length() - 1)
-    source = lax.shift_right_logical(rows & (late - 1), bits) ^ lax.axis_index("expert")
-    target = source * (kinds * extra) + kind * extra + (rows & (extra - 1))
-    columns = lax.broadcasted_iota(jnp.int32, (total, total), 1)
-    select = ((columns == target).astype(F32) * marks[0:1, 0:1]).astype(BF16)
-    picked = dot(select, entries[:, :half], (1, 0)).astype(BF16)
-    grads[kept:] = picked[(kinds - 1) * late :]
+    wait(*pooled)
+    entries = pool[...].reshape(4 * late, pool.shape[-1])
+    picked = two_kinds(entries, marks, 2, extra, half)
+    own[...] = picked[:late]
+    grads[kept:] = picked[late:]
+    stores = [move.start(own, own_hbm)]
     wait(*loads)
+    stores.append(move.start(grads, grads_hbm))
     sent[...] = dot(grads[...], down[...], (1, 1)).astype(BF16)
-    stores = [move.start(sent, sent_hbm), move.start(grads, grads_hbm)]
-    for which in range(kinds - 1):
-        lates[which] = picked[which * late : (which + 1) * late]
-    mark = jnp.max(entries[:, half:].astype(F32), axis=0, keepdims=True)
-    mark_at[...] = jnp.broadcast_to(mark, mark_at.shape)
-    wait(move.start(lates, lates_hbm), move.start(mark_at, mark_hbm), *stores)
+    wait(move.start(sent, sent_hbm), *stores)
 
 
 def kernel_stack(pool_hbm, received_hbm, _one_hbm, _other_hbm, stacked_hbm, pool, sems):
@@ -372,7 +372,7 @@
 
 def kernel_slot(
     base, depth,
-    recv_hbm, lates_hbm, down_hbm, remote_hbm, pre_hbm, late_pre_hbm,
+    recv_hbm, late_hbm, down_hbm, remote_hbm, pre_hbm, late_pre_hbm,
     gate_hbm, up_hbm, other_gate_hbm, other_up_hbm,
     slot_hbm, act_hbm, sides_hbm, hidden_hbm, grads_hbm,
     down, remote, pre, joined, slot, act, sides, hidden_at, grads, sems,
@@ -386,7 +386,7 @@
         move.start(source, target)
         for source, target in (
             (recv_hbm, grads.at[pl.ds(0, kept)]),
-            (lates_hbm.at[2], grads.at[pl.ds(kept, slots - kept)]),
+            (late_hbm, grads.at[pl.ds(kept, slots - kept)]),
             (down_hbm, down),
         )
     ]
@@ -653,14 +653,13 @@
     recv_theirs = grads_theirs.reshape(kept, half)
     recv_own = exchange(send_own.reshape(experts, base, half), "expert").reshape(kept, half)
 
-    sent, grads_theirs, lates, mark = call(
+    sent, grads_theirs, late_own = call(
         functools.partial(kernel_pools, extra),
-        (by_hidden, rows_half, shape(3, late, half), marks_shape),
+        (by_hidden, rows_half, shape(late, half)),
         (
             shape(pool.shape[0], 2, *pool.shape[1:]),
             marks_shape,
-            shape(3, late, half),
-            marks_shape,
+            shape(late, half),
             shape(hidden, half),
             rows_half,
             by_hidden,
@@ -676,7 +675,7 @@
     )
     remote = swap(sent)
     late_pre, sent_late, late_rows, send_late = call(
-        kernel_late,
+        functools.partial(kernel_late, extra),
         (
             shape(late, 2 * hidden, dtype=F32),
             shape(slots + 16, 2 * hidden),
@@ -684,6 +683,7 @@
             shape(late, half),
         ),
         (
+            shape(pool.shape[0], 2, *pool.shape[1:]),
             marks_shape,
             shape(width, 2 * hidden),
             shape(late, 2 * hidden, dtype=F32),
@@ -691,10 +691,11 @@
             shape(late, half),
             shape(late, half),
         ),
-        12,
+        14,
         6_000_000_000,
-        lates,
-        mark,
+        pool,
+        other_half_pool,
+        marks,
         sent_pre,
         sent,
         other_rows,
@@ -719,7 +720,7 @@
         17,
         4 * slots * hidden * width,
         recv_own,
-        lates,
+        late_own,
         w_down[0],
         remote,
         pre,

time: 138 us -> 137 us (level)
  transfers between devices with their start and end apart: 18 -> 18, of which waited for: 10 -> 10; matrix products, arithmetic and copies ran while one was open for 6% -> 6% of each run, Pallas kernels for 23% -> 22%
where the time goes in v6:
time: 137 us; the launch traced here: 136 us
  waiting for transfers between devices  50.1 us (37%)
  starting transfers between devices  39.1 us (29%)
  Pallas kernels  35.9 us (26%)
  local copies, waits for them, and re-layouts  4.57 us (3%)
  other arithmetic  3.64 us (3%)
  between operations  2.25 us (2%)
    pallas_call x10, Pallas kernels, call(): pl.pallas_call(kernel, out_shape=list(out_shapes), in_specs=[IN_HBM] * le...  35.9 us
    all_to_all x4, starting transfers between devices, exchange(): return lax.all_to_all(x, axes, split_axis=0, concat_axis=0, tiled=True)  26.1 us
    ppermute x9, waiting for transfers between devices, swap(): return lax.ppermute(x, 'dp', [(0, 1), (1, 0)])  23.8 us
    ppermute x5, waiting for transfers between devices, from_distance(): lax.ppermute(x, 'expert', [(at, at ^ distance) for at in range(experts)])  13.9 us
    all_to_all x4, waiting for transfers between devices, exchange(): return lax.all_to_all(x, axes, split_axis=0, concat_axis=0, tiled=True)  12.4 us
    ppermute x9, starting transfers between devices, swap(): return lax.ppermute(x, 'dp', [(0, 1), (1, 0)])  8.27 us
    ppermute x5, starting transfers between devices, from_distance(): lax.ppermute(x, 'expert', [(at, at ^ distance) for at in range(experts)])  4.75 us
  transfers between devices with their start and end apart: 18, of which 10 were waited for; matrix products, arithmetic and copies ran while one was open for 6% of the time, Pallas kernels for 22%

profile of v6, /device:TPU:13, one launch (start us, length us, event | category | flops | bytes accessed | tf_op | source)
XLA Modules:
  0.0 135.6 jit_solution(15458325107519904645)
XLA Ops:
  0.6 2.7 %shard_map.102 = (bf16[256,2048]{1,0:T(8,128)(2,1)}, bf16[16,1152]{1,0:T(8,128)(2,1)}, bf16[384,128]{1,0:T(8,128)(2,1)}, f32[8,128]{1,0:T(8,128)}, bf16[144,1024]{1,0:T(8,128)(2,1)}) custom-call(s32[1,128]{1,0:T(1,128)} %bitcast.66, f32[1,128]{1,0:T(1,128)} %bitcast.63, bf16[128,2048]{1,0:T(8,128)(2,1)} %tokens_hbm.1, bf16[128,2048]{1,0:T(8,128)(2,1)} %grad_hbm.3), custom_call_target="tpu_custom_call" | custom-call | flops 134217728 | bytes 2532352 | tf_op jit(solution)/shard_map/pallas_call | solution.py:85
  3.3 0.0 copy-start.12
  3.3 0.0 copy-start.10
  3.3 6.7 %all-to-all-start.3 = ((bf16[16,16,2048]{2,1,0:T(8,128)(2,1)}), bf16[16,16,2048]{2,1,0:T(8,128)(2,1)}, u32[]{:S(2)}, u32[]{:S(2)}) async-start(bf16[16,16,2048]{2,1,0:T(8,128)(2,1)} %bitcast.53), calls=%async_computation.3 | async-start | bytes 2097152 | tf_op jit(solution)/shard_map/all_to_all | solution.py:26
  10.0 0.0 copy-done.12
  10.0 1.3 collective-permute-start.5
  11.3 0.3 collective-permute-start.4
  11.6 1.2 collective-permute-start.10
  12.8 0.0 copy-done.10
  12.8 0.6 constant_dynamic-update-slice_fusion.1
  13.4 5.0 %collective-permute-done.5.other_hbm = bf16[144,1024]{1,0:T(8,128)(2,1)} collective-permute-done((bf16[144,1024]{1,0:T(8,128)(2,1)S(1)}, bf16[144,1024]{1,0:T(8,128)(2,1)}, u32[]{:S(2)}, u32[]{:S(2)}) %collective-permute-start.5) | collective-permute-done | bytes 294944 | tf_op jit(solution)/shard_map/ppermute | solution.py:22
  18.4 2.6 %shard_map.103 = (bf16[256,1024]{1,0:T(8,128)(2,1)}, bf16[256,1024]{1,0:T(8,128)(2,1)}, bf16[16,1152]{1,0:T(8,128)(2,1)}) custom-call(s32[1,128]{1,0:T(1,128)} %bitcast.67, f32[1,128]{1,0:T(1,128)} %bitcast.64, bf16[128,2048]{1,0:T(8,128)(2,1)} %grad_hbm.3, bf16[144,1024]{1,0:T(8,128)(2,1)} %collective-permute-done.5.other_hbm), custom_call_target="tpu_custom_call" | custom-call | flops 268435456 | bytes 1905664 | tf_op jit(solution)/shard_map/pallas_call | solution.py:85
  21.0 1.4 %constant_dynamic-update-slice_fusion = bf16[32,1152]{1,0:T(8,128)(2,1)} fusion(bf16[32,1152]{1,0:T(8,128)(2,1)} %constant_dynamic-update-slice_fusion.1, bf16[16,1152]{1,0:T(8,128)(2,1)} %get-tuple-element.106), kind=kLoop, calls=%fused_computation.50 | loop fusion | bytes 73728 | tf_op jit(solution)/shard_map/concatenate | solution.py:607
  22.4 1.2 collective-permute-start.8
  23.6 1.2 collective-permute-start.7
  24.8 0.9 collective-permute-start.6
  25.7 13.9 %collective-permute-done.8 = bf16[32,1152]{1,0:T(8,128)(2,1)S(1)} collective-permute-done((bf16[32,1152]{1,0:T(8,128)(2,1)}, bf16[32,1152]{1,0:T(8,128)(2,1)S(1)}, u32[]{:S(2)}, u32[]{:S(2)}) %collective-permute-start.8) | collective-permute-done | bytes 73760 | tf_op jit(solution)/shard_map/ppermute | solution.py:604
  39.6 0.0 collective-permute-done.7
  39.6 0.0 collective-permute-done.6
  39.6 0.9 pad_maximum_fusion.7.pool_hbm
  40.5 0.0 copy-start.9
  40.6 0.0 collective-permute-done.4._other_hbm.other_gate_hbm
  40.6 0.0 all-to-all-done.3
  40.6 0.7 copy-done.9
  41.3 0.2 collective-permute-start.9
  41.5 8.7 %all-to-all-start.4 = ((bf16[16,16,1024]{2,1,0:T(8,128)(2,1)}), bf16[16,16,1024]{2,1,0:T(8,128)(2,1)}, u32[]{:S(2)}, u32[]{:S(2)}) async-start(bf16[16,16,1024]{2,1,0:T(8,128)(2,1)} %bitcast.58), calls=%async_computation.4 | async-start | bytes 1048576 | tf_op jit(solution)/shard_map/all_to_all | solution.py:26
  50.2 2.0 %collective-permute-done.10._one_hbm.other_up_hbm = bf16[1024,384]{1,0:T(8,128)(2,1)} collective-permute-done((bf16[1024,384]{1,0:T(8,128)(2,1)}, bf16[1024,384]{1,0:T(8,128)(2,1)}, u32[]{:S(2)}, u32[]{:S(2)}) %collective-permute-start.10) | collective-permute-done | bytes 786464 | tf_op jit(solution)/shard_map/ppermute | solution.py:22
  52.1 0.0 collective-permute-done.9.received_hbm
  52.1 1.9 %shard_map.104 = bf16[4,2,32,1152]{3,2,1,0:T(8,128)(2,1)} custom-call(bf16[4,32,1152]{2,1,0:T(8,128)(2,1)} %copy-done.9, bf16[4,32,1152]{2,1,0:T(8,128)(2,1)} %collective-permute-done.9.received_hbm, bf16[1024,384]{1,0:T(8,128)(2,1)} %collective-permute-done.10._one_hbm.other_up_hbm, bf16[1024,384]{1,0:T(8,128)(2,1)} %collective-permute-done.4._other_hbm.other_gate_hbm), custom_call_target="tpu_custom_call" | custom-call | flops 99999997952 | bytes 2752512 | tf_op jit(solution)/shard_map/pallas_call | solution.py:85
  54.0 1.3 collective-permute-start.11
  55.3 1.9 %slice.21 = bf16[256,1024]{1,0:T(8,128)(2,1)} slice(bf16[256,2048]{1,0:T(8,128)(2,1)} %bitcast.17.rows_hbm), slice={[0:256], [1024:2048]} | slice | bytes 1048576 | tf_op jit(solution)/shard_map/slice | solution.py:614
  57.1 1.2 collective-permute-start.12
  58.4 4.2 %shard_map.105 = (f32[256,768]{1,0:T(8,128)}, bf16[256,768]{1,0:T(8,128)(2,1)}) custom-call(bf16[256,2048]{1,0:T(8,128)(2,1)} %bitcast.17.rows_hbm, bf16[1024,384]{1,0:T(8,128)(2,1)} %bitcast.18.gate_hbm, bf16[1024,384]{1,0:T(8,128)(2,1)} %bitcast.23.up_hbm, bf16[1024,384]{1,0:T(8,128)(2,1)} %collective-permute-done.4._other_hbm.other_gate_hbm, ...), custom_call_target="tpu_custom_call" | custom-call | bytes 5373952 | tf_op jit(solution)/shard_map/pallas_call | solution.py:85
  62.6 1.6 %all-to-all-done.4 = bf16[16,16,1024]{2,1,0:T(8,128)(2,1)} async-done(((bf16[16,16,1024]{2,1,0:T(8,128)(2,1)}), bf16[16,16,1024]{2,1,0:T(8,128)(2,1)}, u32[]{:S(2)}, u32[]{:S(2)}) %all-to-all-start.4) | async-done | bytes 524320 | tf_op jit(solution)/shard_map/all_to_all | solution.py:26
  64.2 4.7 %all-to-all-start.5 = ((bf16[16,16,1024]{2,1,0:T(8,128)(2,1)}), bf16[16,16,1024]{2,1,0:T(8,128)(2,1)}, u32[]{:S(2)}, u32[]{:S(2)}) async-start(bf16[16,16,1024]{2,1,0:T(8,128)(2,1)} %bitcast.57), calls=%async_computation.5 | async-start | bytes 1048576 | tf_op jit(solution)/shard_map/all_to_all | solution.py:26
  68.9 0.0 collective-permute-done.11.received_hbm
  68.9 3.1 %shard_map.106 = (bf16[384,384]{1,0:T(8,128)(2,1)}, bf16[384,1024]{1,0:T(8,128)(2,1)}, bf16[128,1024]{1,0:T(8,128)(2,1)}) custom-call(bf16[8,32,1152]{2,1,0:T(8,128)(2,1)} %bitcast.55, bf16[8,32,1152]{2,1,0:T(8,128)(2,1)} %collective-permute-done.11.received_hbm, f32[8,128]{1,0:T(8,128)} %get-tuple-element.109.marks_hbm, ...), custom_call_target="tpu_custom_call" | custom-call | flops 301989888 | bytes 4231168 | tf_op jit(solution)/shard_map/pallas_call | solution.py:85
  72.0 1.3 collective-permute-start.14
  73.3 0.0 collective-permute-done.12._rows_hbm.other_rows_hbm
  73.3 4.1 %shard_map.107 = (f32[128,768]{1,0:T(8,128)}, bf16[400,768]{1,0:T(8,128)(2,1)}, bf16[128,1024]{1,0:T(8,128)(2,1)}, bf16[128,1024]{1,0:T(8,128)(2,1)}) custom-call(bf16[8,32,1152]{2,1,0:T(8,128)(2,1)} %bitcast.56, bf16[8,32,1152]{2,1,0:T(8,128)(2,1)} %collective-permute-done.11.received_hbm, f32[8,128]{1,0:T(8,128)} %get-tuple-element.109.marks_hbm, ...), custom_call_target="tpu_custom_call" | custom-call | flops 6000000000 | bytes 7073792 | tf_op jit(solution)/shard_map/pallas_call | solution.py:85
  77.4 0.3 collective-permute-start.13
  77.8 2.9 %collective-permute-done.14.remote_hbm = bf16[384,384]{1,0:T(8,128)(2,1)} collective-permute-done((bf16[384,384]{1,0:T(8,128)(2,1)}, bf16[384,384]{1,0:T(8,128)(2,1)}, u32[]{:S(2)}, u32[]{:S(2)}) %collective-permute-start.14) | collective-permute-done | bytes 294944 | tf_op jit(solution)/shard_map/ppermute | solution.py:22
  80.6 2.3 %all-to-all-done.5 = bf16[16,16,1024]{2,1,0:T(8,128)(2,1)} async-done(((bf16[16,16,1024]{2,1,0:T(8,128)(2,1)}), bf16[16,16,1024]{2,1,0:T(8,128)(2,1)}, u32[]{:S(2)}, u32[]{:S(2)}) %all-to-all-start.5) | async-done | bytes 524320 | tf_op jit(solution)/shard_map/all_to_all | solution.py:26
  82.9 5.7 %shard_map.108 = (bf16[384,2048]{1,0:T(8,128)(2,1)}, bf16[384,384]{1,0:T(8,128)(2,1)}, bf16[384,768]{1,0:T(8,128)(2,1)}, bf16[384,384]{1,0:T(8,128)(2,1)}, bf16[384,1024]{1,0:T(8,128)(2,1)}) custom-call(bf16[256,1024]{1,0:T(8,128)(2,1)} %bitcast.29.recv_hbm, bf16[128,1024]{1,0:T(8,128)(2,1)} %get-tuple-element.120.late_hbm, ...), custom_call_target="tpu_custom_call" | custom-call | flops 1207959552 | bytes 9732096 | tf_op jit(solution)/shard_map/pallas_call | solution.py:85
  88.6 1.3 collective-permute-start.15
  89.9 0.3 collective-permute-start.16
  90.1 6.0 %all-to-all-start.6 = ((bf16[16,24,2048]{2,1,0:T(8,128)(2,1)}), bf16[16,24,2048]{2,1,0:T(8,128)(2,1)}, u32[]{:S(2)}, u32[]{:S(2)}) async-start(bf16[16,24,2048]{2,1,0:T(8,128)(2,1)} %bitcast.52), calls=%async_computation.6 | async-start | bytes 3145728 | tf_op jit(solution)/shard_map/all_to_all | solution.py:26
  96.1 0.0 collective-permute-done.13.pre_hbm
  96.1 4.0 %collective-permute-done.15.hidden_hbm = bf16[384,384]{1,0:T(8,128)(2,1)} collective-permute-done((bf16[384,384]{1,0:T(8,128)(2,1)}, bf16[384,384]{1,0:T(8,128)(2,1)}, u32[]{:S(2)}, u32[]{:S(2)}) %collective-permute-start.15) | collective-permute-done | bytes 294944 | tf_op jit(solution)/shard_map/ppermute | solution.py:22
  100.1 3.7 %shard_map.109 = (bf16[384,1024]{1,0:T(8,128)(2,1)}, bf16[384,768]{1,0:T(8,128)(2,1)}) custom-call(bf16[400,768]{1,0:T(8,128)(2,1)} %collective-permute-done.13.pre_hbm, bf16[384,384]{1,0:T(8,128)(2,1)} %collective-permute-done.15.hidden_hbm, bf16[384,384]{1,0:T(8,128)(2,1)} %get-tuple-element.125.act_hbm, bf16[384,1024]{1,0:T(8,128)(2,1)} %get-tuple-element.126.grads_hbm, ...), custom_call_target="tpu_custom_call" | custom-call | flops 99999997952 | bytes 4153344 | tf_op jit(solution)/shard_map/pallas_call | solution.py:85
  103.8 1.9 %collective-permute-done.16.other_late_hbm = bf16[128,1024]{1,0:T(8,128)(2,1)} collective-permute-done((bf16[128,1024]{1,0:T(8,128)(2,1)}, bf16[128,1024]{1,0:T(8,128)(2,1)}, u32[]{:S(2)}, u32[]{:S(2)}) %collective-permute-start.16) | collective-permute-done | bytes 262176 | tf_op jit(solution)/shard_map/ppermute | solution.py:22
  105.7 1.2 collective-permute-start.17
  106.9 1.4 slice_reduce_fusion.1
  108.3 1.4 slice_reduce_fusion
  110.9 4.8 %shard_map.111 = (bf16[1024,384]{1,0:T(8,128)(2,1)}, bf16[1024,384]{1,0:T(8,128)(2,1)}) custom-call(bf16[256,2048]{1,0:T(8,128)(2,1)} %bitcast.17.rows_hbm, bf16[128,1024]{1,0:T(8,128)(2,1)} %get-tuple-element.133.late_rows_hbm, bf16[256,1024]{1,0:T(8,128)(2,1)} %collective-permute-done.12._rows_hbm.other_rows_hbm, ...), custom_call_target="tpu_custom_call" | custom-call | flops 1207959552 | bytes 4849664 | tf_op jit(solution)/shard_map/pallas_call | solution.py:85
  115.8 8.1 %collective-permute-done.17.other_hbm = bf16[384,1024]{1,0:T(8,128)(2,1)} collective-permute-done((bf16[384,1024]{1,0:T(8,128)(2,1)}, bf16[384,1024]{1,0:T(8,128)(2,1)}, u32[]{:S(2)}, u32[]{:S(2)}) %collective-permute-start.17) | collective-permute-done | bytes 786464 | tf_op jit(solution)/shard_map/ppermute | solution.py:22
  123.9 8.5 %all-to-all-done.6 = bf16[16,24,2048]{2,1,0:T(8,128)(2,1)} async-done(((bf16[16,24,2048]{2,1,0:T(8,128)(2,1)}), bf16[16,24,2048]{2,1,0:T(8,128)(2,1)}, u32[]{:S(2)}, u32[]{:S(2)}) %all-to-all-start.6) | async-done | bytes 1572896 | tf_op jit(solution)/shard_map/all_to_all | solution.py:26
  132.4 3.0 %shard_map.110 = (bf16[128,2048]{1,0:T(8,128)(2,1)}, bf16[384,2048]{1,0:T(8,128)(2,1)}) custom-call(bf16[384,128]{1,0:T(8,128)(2,1)} %get-tuple-element.118.place_hbm, bf16[384,2048]{1,0:T(8,128)(2,1)} %bitcast.31.returned_hbm, bf16[384,1024]{1,0:T(8,128)(2,1)} %get-tuple-element.131.own_hbm, bf16[384,1024]{1,0:T(8,128)(2,1)} %collective-permute-done.17.other_hbm), custom_call_target="tpu_custom_call" | custom-call | flops 201326592 | bytes 5341184 | tf_op jit(solution)/shard_map/pallas_call | solution.py:85
  (1 shorter events, 0.0 us)
Async XLA Ops:
  3.3 6.7 %copy-start.12 = (bf16[144,1024]{1,0:T(8,128)(2,1)S(1)}, bf16[144,1024]{1,0:T(8,128)(2,1)}, u32[]{:S(2)}) copy-start(bf16[144,1024]{1,0:T(8,128)(2,1)} %get-tuple-element.103) | copy-start | bytes 884740
  3.3 9.5 %copy-start.10 = (bf16[16,1152]{1,0:T(8,128)(2,1)S(1)}, bf16[16,1152]{1,0:T(8,128)(2,1)}, u32[]{:S(2)}) copy-start(bf16[16,1152]{1,0:T(8,128)(2,1)} %get-tuple-element.105) | copy-start | bytes 110596
  3.3 37.2 %all-to-all-start.3 = ((bf16[16,16,2048]{2,1,0:T(8,128)(2,1)}), bf16[16,16,2048]{2,1,0:T(8,128)(2,1)}, u32[]{:S(2)}, u32[]{:S(2)}) async-start(bf16[16,16,2048]{2,1,0:T(8,128)(2,1)} %bitcast.53), calls=%async_computation.3 | async-start | bytes 2097152 | tf_op jit(solution)/shard_map/all_to_all | solution.py:26
  10.0 8.4 %collective-permute-start.5 = (bf16[144,1024]{1,0:T(8,128)(2,1)S(1)}, bf16[144,1024]{1,0:T(8,128)(2,1)}, u32[]{:S(2)}, u32[]{:S(2)}) collective-permute-start(bf16[144,1024]{1,0:T(8,128)(2,1)S(1)} %copy-done.12), channel_id=1, source_target_pairs={{0,16},{16,0},{1,17},{17,1},{2,18},{18,2},{3,19},{19,3},{4,20},{20... | collective-permute-start | bytes 884744 | tf_op jit(solution)/shard_map/ppermute | solution.py:22
  11.3 29.3 %collective-permute-start.4 = (bf16[1024,384]{1,0:T(8,128)(2,1)}, bf16[1024,384]{1,0:T(8,128)(2,1)}, u32[]{:S(2)}, u32[]{:S(2)}) collective-permute-start(bf16[1024,384]{1,0:T(8,128)(2,1)} %bitcast.18.gate_hbm), channel_id=1, source_target_pairs={{0,16},{16,0},{1,17},{17,1},{2,18},{18,2},{3,19},{19,3},{4,20},{20... | collective-permute-start | bytes 2359304 | tf_op jit(solution)/shard_map/ppermute | solution.py:22
  11.6 40.6 %collective-permute-start.10 = (bf16[1024,384]{1,0:T(8,128)(2,1)}, bf16[1024,384]{1,0:T(8,128)(2,1)}, u32[]{:S(2)}, u32[]{:S(2)}) collective-permute-start(bf16[1024,384]{1,0:T(8,128)(2,1)} %bitcast.23.up_hbm), channel_id=1, source_target_pairs={{0,16},{16,0},{1,17},{17,1},{2,18},{18,2},{3,19},{19,3},{4,20},{20... | collective-permute-start | bytes 2359304 | tf_op jit(solution)/shard_map/ppermute | solution.py:22
  22.4 17.2 %collective-permute-start.8 = (bf16[32,1152]{1,0:T(8,128)(2,1)}, bf16[32,1152]{1,0:T(8,128)(2,1)S(1)}, u32[]{:S(2)}, u32[]{:S(2)}) collective-permute-start(bf16[32,1152]{1,0:T(8,128)(2,1)} %constant_dynamic-update-slice_fusion), channel_id=1, source_target_pairs={{0,12},{1,13},{2,14},{3,15},{4,8},{5,9},{6,10},{7,11},{8,4},{9,5},... | collective-permute-start | bytes 221192 | tf_op jit(solution)/shard_map/ppermute | solution.py:604
  23.6 16.0 %collective-permute-start.7 = (bf16[32,1152]{1,0:T(8,128)(2,1)}, bf16[32,1152]{1,0:T(8,128)(2,1)S(1)}, u32[]{:S(2)}, u32[]{:S(2)}) collective-permute-start(bf16[32,1152]{1,0:T(8,128)(2,1)} %constant_dynamic-update-slice_fusion), channel_id=1, source_target_pairs={{0,8},{1,9},{2,10},{3,11},{4,12},{5,13},{6,14},{7,15},{8,0},{9,1},... | collective-permute-start | bytes 221192 | tf_op jit(solution)/shard_map/ppermute | solution.py:604
  24.8 14.8 %collective-permute-start.6 = (bf16[32,1152]{1,0:T(8,128)(2,1)}, bf16[32,1152]{1,0:T(8,128)(2,1)S(1)}, u32[]{:S(2)}, u32[]{:S(2)}) collective-permute-start(bf16[32,1152]{1,0:T(8,128)(2,1)} %constant_dynamic-update-slice_fusion), channel_id=1, source_target_pairs={{0,4},{1,5},{2,6},{3,7},{4,0},{5,1},{6,2},{7,3},{8,12},{9,13},{10,... | collective-permute-start | bytes 221192 | tf_op jit(solution)/shard_map/ppermute | solution.py:604
  40.5 0.7 copy-start.9
  41.3 10.9 %collective-permute-start.9 = (bf16[4,32,1152]{2,1,0:T(8,128)(2,1)S(1)}, bf16[4,32,1152]{2,1,0:T(8,128)(2,1)}, u32[]{:S(2)}, u32[]{:S(2)}) collective-permute-start(bf16[4,32,1152]{2,1,0:T(8,128)(2,1)S(1)} %pad_maximum_fusion.7.pool_hbm), channel_id=1, source_target_pairs={{0,2},{1,3},{2,0},{3,1},{4,6},{5,7},{6,4},{7,5},{8,10},{9,11},{10,... | collective-permute-start | bytes 884744 | tf_op jit(solution)/shard_map/ppermute | solution.py:604
  41.5 22.7 %all-to-all-start.4 = ((bf16[16,16,1024]{2,1,0:T(8,128)(2,1)}), bf16[16,16,1024]{2,1,0:T(8,128)(2,1)}, u32[]{:S(2)}, u32[]{:S(2)}) async-start(bf16[16,16,1024]{2,1,0:T(8,128)(2,1)} %bitcast.58), calls=%async_computation.4 | async-start | bytes 1048576 | tf_op jit(solution)/shard_map/all_to_all | solution.py:26
  54.0 14.8 %collective-permute-start.11 = (bf16[8,32,1152]{2,1,0:T(8,128)(2,1)}, bf16[8,32,1152]{2,1,0:T(8,128)(2,1)}, u32[]{:S(2)}, u32[]{:S(2)}) collective-permute-start(bf16[8,32,1152]{2,1,0:T(8,128)(2,1)} %bitcast.54), channel_id=1, source_target_pairs={{0,1},{1,0},{2,3},{3,2},{4,5},{5,4},{6,7},{7,6},{8,9},{9,8},{10,11... | collective-permute-start | bytes 1769480 | tf_op jit(solution)/shard_map/ppermute | solution.py:604
  57.1 16.1 %collective-permute-start.12 = (bf16[256,1024]{1,0:T(8,128)(2,1)}, bf16[256,1024]{1,0:T(8,128)(2,1)}, u32[]{:S(2)}, u32[]{:S(2)}) collective-permute-start(bf16[256,1024]{1,0:T(8,128)(2,1)} %slice.21), channel_id=1, source_target_pairs={{0,16},{16,0},{1,17},{17,1},{2,18},{18,2},{3,19},{19,3},{4,20},{20... | collective-permute-start | bytes 1572872 | tf_op jit(solution)/shard_map/ppermute | solution.py:22
  64.2 18.7 %all-to-all-start.5 = ((bf16[16,16,1024]{2,1,0:T(8,128)(2,1)}), bf16[16,16,1024]{2,1,0:T(8,128)(2,1)}, u32[]{:S(2)}, u32[]{:S(2)}) async-start(bf16[16,16,1024]{2,1,0:T(8,128)(2,1)} %bitcast.57), calls=%async_computation.5 | async-start | bytes 1048576 | tf_op jit(solution)/shard_map/all_to_all | solution.py:26
  72.0 8.6 %collective-permute-start.14 = (bf16[384,384]{1,0:T(8,128)(2,1)}, bf16[384,384]{1,0:T(8,128)(2,1)}, u32[]{:S(2)}, u32[]{:S(2)}) collective-permute-start(bf16[384,384]{1,0:T(8,128)(2,1)} %get-tuple-element.116._hidden_hbm), channel_id=1, source_target_pairs={{0,16},{16,0},{1,17},{17,1},{2,18},{18,2},{3,19},{19,3},{4,20},{20... | collective-permute-start | bytes 884744 | tf_op jit(solution)/shard_map/ppermute | solution.py:22
  77.4 18.7 %collective-permute-start.13 = (bf16[400,768]{1,0:T(8,128)(2,1)}, bf16[400,768]{1,0:T(8,128)(2,1)}, u32[]{:S(2)}, u32[]{:S(2)}) collective-permute-start(bf16[400,768]{1,0:T(8,128)(2,1)} %get-tuple-element.117), channel_id=1, source_target_pairs={{0,16},{16,0},{1,17},{17,1},{2,18},{18,2},{3,19},{19,3},{4,20},{20... | collective-permute-start | bytes 1843208 | tf_op jit(solution)/shard_map/ppermute | solution.py:22
  88.6 11.5 %collective-permute-start.15 = (bf16[384,384]{1,0:T(8,128)(2,1)}, bf16[384,384]{1,0:T(8,128)(2,1)}, u32[]{:S(2)}, u32[]{:S(2)}) collective-permute-start(bf16[384,384]{1,0:T(8,128)(2,1)} %get-tuple-element.124), channel_id=1, source_target_pairs={{0,16},{16,0},{1,17},{17,1},{2,18},{18,2},{3,19},{19,3},{4,20},{20... | collective-permute-start | bytes 884744 | tf_op jit(solution)/shard_map/ppermute | solution.py:22
  89.9 15.9 %collective-permute-start.16 = (bf16[128,1024]{1,0:T(8,128)(2,1)}, bf16[128,1024]{1,0:T(8,128)(2,1)}, u32[]{:S(2)}, u32[]{:S(2)}) collective-permute-start(bf16[128,1024]{1,0:T(8,128)(2,1)} %get-tuple-element.130), channel_id=1, source_target_pairs={{0,16},{16,0},{1,17},{17,1},{2,18},{18,2},{3,19},{19,3},{4,20},{20... | collective-permute-start | bytes 786440 | tf_op jit(solution)/shard_map/ppermute | solution.py:22
  90.1 42.3 %all-to-all-start.6 = ((bf16[16,24,2048]{2,1,0:T(8,128)(2,1)}), bf16[16,24,2048]{2,1,0:T(8,128)(2,1)}, u32[]{:S(2)}, u32[]{:S(2)}) async-start(bf16[16,24,2048]{2,1,0:T(8,128)(2,1)} %bitcast.52), calls=%async_computation.6 | async-start | bytes 3145728 | tf_op jit(solution)/shard_map/all_to_all | solution.py:26
  105.7 18.2 %collective-permute-start.17 = (bf16[384,1024]{1,0:T(8,128)(2,1)}, bf16[384,1024]{1,0:T(8,128)(2,1)}, u32[]{:S(2)}, u32[]{:S(2)}) collective-permute-start(bf16[384,1024]{1,0:T(8,128)(2,1)} %get-tuple-element.131.own_hbm), channel_id=1, source_target_pairs={{0,16},{16,0},{1,17},{17,1},{2,18},{18,2},{3,19},{19,3},{4,20},{20... | collective-permute-start | bytes 2359304 | tf_op jit(solution)/shard_map/ppermute | solution.py:22

commit v7 on v6

--- a/solution.py
+++ b/solution.py
@@ -399,6 +399,16 @@
         )
     ]
     weights = weight_copies(move, joined, (gate_hbm, up_hbm), (other_gate_hbm, other_up_hbm))
+    at = lane_row(slots)
+    late = at - kept
+    target = jnp.where(
+        at < kept,
+        lax.shift_right_logical(at, base.bit_length() - 1) * depth + (at & (base - 1)),
+        lax.shift_right_arithmetic(late, extra.bit_length() - 1) * depth
+        + base
+        + (late & (extra - 1)),
+    )
+    order = zero_one(row_index(slots, slots) == target)
     wait(*first)
     stores = [move.start(grads, grads_hbm)]
     hidden_grad = dot(grads[...], down[...], (1, 1))
@@ -412,16 +422,6 @@
         move.start(source, target)
         for source, target in ((hidden_at, hidden_hbm), (act, act_hbm), (sides, sides_hbm))
     ]
-    at = lane_row(slots)
-    late = at - kept
-    target = jnp.where(
-        at < kept,
-        lax.shift_right_logical(at, base.bit_length() - 1) * depth + (at & (base - 1)),
-        lax.shift_right_arithmetic(late, extra.bit_length() - 1) * depth
-        + base
-        + (late & (extra - 1)),
-    )
-    order = zero_one(row_index(slots, slots) == target)
     both = dot(order, both, (1, 0)).astype(BF16)
     for part in range(2):
         wait(*weights[part])

time: 137 us -> 137 us (level)
  no operation moved by 1% of the time
where the time goes in v7:
time: 137 us; the launch traced here: 136 us
  waiting for transfers between devices  50.2 us (37%)
  starting transfers between devices  39.1 us (29%)
  Pallas kernels  35.9 us (26%)
  local copies, waits for them, and re-layouts  4.57 us (3%)
  other arithmetic  3.64 us (3%)
  between operations  2.25 us (2%)
    pallas_call x10, Pallas kernels, call(): pl.pallas_call(kernel, out_shape=list(out_shapes), in_specs=[IN_HBM] * le...  35.9 us
    all_to_all x4, starting transfers between devices, exchange(): return lax.all_to_all(x, axes, split_axis=0, concat_axis=0, tiled=True)  26.1 us
    ppermute x9, waiting for transfers between devices, swap(): return lax.ppermute(x, 'dp', [(0, 1), (1, 0)])  23.9 us
    ppermute x5, waiting for transfers between devices, from_distance(): lax.ppermute(x, 'expert', [(at, at ^ distance) for at in range(experts)])  13.9 us
    all_to_all x4, waiting for transfers between devices, exchange(): return lax.all_to_all(x, axes, split_axis=0, concat_axis=0, tiled=True)  12.4 us
    ppermute x9, starting transfers between devices, swap(): return lax.ppermute(x, 'dp', [(0, 1), (1, 0)])  8.27 us
    ppermute x5, starting transfers between devices, from_distance(): lax.ppermute(x, 'expert', [(at, at ^ distance) for at in range(experts)])  4.75 us
  transfers between devices with their start and end apart: 18, of which 10 were waited for; matrix products, arithmetic and copies ran while one was open for 6% of the time, Pallas kernels for 22%

profile of v7, /device:TPU:13, one launch (start us, length us, event | category | flops | bytes accessed | tf_op | source)
XLA Modules:
  0.0 135.6 jit_solution(17871282584955883469)
XLA Ops:
  0.6 2.7 %shard_map.102 = (bf16[256,2048]{1,0:T(8,128)(2,1)}, bf16[16,1152]{1,0:T(8,128)(2,1)}, bf16[384,128]{1,0:T(8,128)(2,1)}, f32[8,128]{1,0:T(8,128)}, bf16[144,1024]{1,0:T(8,128)(2,1)}) custom-call(s32[1,128]{1,0:T(1,128)} %bitcast.66, f32[1,128]{1,0:T(1,128)} %bitcast.63, bf16[128,2048]{1,0:T(8,128)(2,1)} %tokens_hbm.1, bf16[128,2048]{1,0:T(8,128)(2,1)} %grad_hbm.3), custom_call_target="tpu_custom_call" | custom-call | flops 134217728 | bytes 2532352 | tf_op jit(solution)/shard_map/pallas_call | solution.py:85
  3.3 0.0 copy-start.12
  3.3 0.0 copy-start.10
  3.3 6.7 %all-to-all-start.3 = ((bf16[16,16,2048]{2,1,0:T(8,128)(2,1)}), bf16[16,16,2048]{2,1,0:T(8,128)(2,1)}, u32[]{:S(2)}, u32[]{:S(2)}) async-start(bf16[16,16,2048]{2,1,0:T(8,128)(2,1)} %bitcast.53), calls=%async_computation.3 | async-start | bytes 2097152 | tf_op jit(solution)/shard_map/all_to_all | solution.py:26
  10.0 0.0 copy-done.12
  10.0 1.3 collective-permute-start.5
  11.3 0.3 collective-permute-start.4
  11.6 1.2 collective-permute-start.10
  12.8 0.0 copy-done.10
  12.8 0.6 constant_dynamic-update-slice_fusion.1
  13.4 5.0 %collective-permute-done.5.other_hbm = bf16[144,1024]{1,0:T(8,128)(2,1)} collective-permute-done((bf16[144,1024]{1,0:T(8,128)(2,1)S(1)}, bf16[144,1024]{1,0:T(8,128)(2,1)}, u32[]{:S(2)}, u32[]{:S(2)}) %collective-permute-start.5) | collective-permute-done | bytes 294944 | tf_op jit(solution)/shard_map/ppermute | solution.py:22
  18.4 2.6 %shard_map.103 = (bf16[256,1024]{1,0:T(8,128)(2,1)}, bf16[256,1024]{1,0:T(8,128)(2,1)}, bf16[16,1152]{1,0:T(8,128)(2,1)}) custom-call(s32[1,128]{1,0:T(1,128)} %bitcast.67, f32[1,128]{1,0:T(1,128)} %bitcast.64, bf16[128,2048]{1,0:T(8,128)(2,1)} %grad_hbm.3, bf16[144,1024]{1,0:T(8,128)(2,1)} %collective-permute-done.5.other_hbm), custom_call_target="tpu_custom_call" | custom-call | flops 268435456 | bytes 1905664 | tf_op jit(solution)/shard_map/pallas_call | solution.py:85
  21.0 1.4 %constant_dynamic-update-slice_fusion = bf16[32,1152]{1,0:T(8,128)(2,1)} fusion(bf16[32,1152]{1,0:T(8,128)(2,1)} %constant_dynamic-update-slice_fusion.1, bf16[16,1152]{1,0:T(8,128)(2,1)} %get-tuple-element.106), kind=kLoop, calls=%fused_computation.50 | loop fusion | bytes 73728 | tf_op jit(solution)/shard_map/concatenate | solution.py:607
  22.4 1.2 collective-permute-start.8
  23.6 1.2 collective-permute-start.7
  24.8 0.9 collective-permute-start.6
  25.7 13.9 %collective-permute-done.8 = bf16[32,1152]{1,0:T(8,128)(2,1)S(1)} collective-permute-done((bf16[32,1152]{1,0:T(8,128)(2,1)}, bf16[32,1152]{1,0:T(8,128)(2,1)S(1)}, u32[]{:S(2)}, u32[]{:S(2)}) %collective-permute-start.8) | collective-permute-done | bytes 73760 | tf_op jit(solution)/shard_map/ppermute | solution.py:604
  39.6 0.0 collective-permute-done.7
  39.6 0.0 collective-permute-done.6
  39.6 0.9 pad_maximum_fusion.7.pool_hbm
  40.5 0.0 copy-start.9
  40.6 0.0 collective-permute-done.4._other_hbm.other_gate_hbm
  40.6 0.0 all-to-all-done.3
  40.6 0.7 copy-done.9
  41.3 0.2 collective-permute-start.9
  41.5 8.7 %all-to-all-start.4 = ((bf16[16,16,1024]{2,1,0:T(8,128)(2,1)}), bf16[16,16,1024]{2,1,0:T(8,128)(2,1)}, u32[]{:S(2)}, u32[]{:S(2)}) async-start(bf16[16,16,1024]{2,1,0:T(8,128)(2,1)} %bitcast.58), calls=%async_computation.4 | async-start | bytes 1048576 | tf_op jit(solution)/shard_map/all_to_all | solution.py:26
  50.2 2.0 %collective-permute-done.10._one_hbm.other_up_hbm = bf16[1024,384]{1,0:T(8,128)(2,1)} collective-permute-done((bf16[1024,384]{1,0:T(8,128)(2,1)}, bf16[1024,384]{1,0:T(8,128)(2,1)}, u32[]{:S(2)}, u32[]{:S(2)}) %collective-permute-start.10) | collective-permute-done | bytes 786464 | tf_op jit(solution)/shard_map/ppermute | solution.py:22
  52.1 0.0 collective-permute-done.9.received_hbm
  52.1 1.9 %shard_map.104 = bf16[4,2,32,1152]{3,2,1,0:T(8,128)(2,1)} custom-call(bf16[4,32,1152]{2,1,0:T(8,128)(2,1)} %copy-done.9, bf16[4,32,1152]{2,1,0:T(8,128)(2,1)} %collective-permute-done.9.received_hbm, bf16[1024,384]{1,0:T(8,128)(2,1)} %collective-permute-done.10._one_hbm.other_up_hbm, bf16[1024,384]{1,0:T(8,128)(2,1)} %collective-permute-done.4._other_hbm.other_gate_hbm), custom_call_target="tpu_custom_call" | custom-call | flops 99999997952 | bytes 2752512 | tf_op jit(solution)/shard_map/pallas_call | solution.py:85
  54.0 1.3 collective-permute-start.11
  55.3 1.9 %slice.21 = bf16[256,1024]{1,0:T(8,128)(2,1)} slice(bf16[256,2048]{1,0:T(8,128)(2,1)} %bitcast.17.rows_hbm), slice={[0:256], [1024:2048]} | slice | bytes 1048576 | tf_op jit(solution)/shard_map/slice | solution.py:614
  57.1 1.2 collective-permute-start.12
  58.4 4.2 %shard_map.105 = (f32[256,768]{1,0:T(8,128)}, bf16[256,768]{1,0:T(8,128)(2,1)}) custom-call(bf16[256,2048]{1,0:T(8,128)(2,1)} %bitcast.17.rows_hbm, bf16[1024,384]{1,0:T(8,128)(2,1)} %bitcast.18.gate_hbm, bf16[1024,384]{1,0:T(8,128)(2,1)} %bitcast.23.up_hbm, bf16[1024,384]{1,0:T(8,128)(2,1)} %collective-permute-done.4._other_hbm.other_gate_hbm, ...), custom_call_target="tpu_custom_call" | custom-call | bytes 5373952 | tf_op jit(solution)/shard_map/pallas_call | solution.py:85
  62.6 1.6 %all-to-all-done.4 = bf16[16,16,1024]{2,1,0:T(8,128)(2,1)} async-done(((bf16[16,16,1024]{2,1,0:T(8,128)(2,1)}), bf16[16,16,1024]{2,1,0:T(8,128)(2,1)}, u32[]{:S(2)}, u32[]{:S(2)}) %all-to-all-start.4) | async-done | bytes 524320 | tf_op jit(solution)/shard_map/all_to_all | solution.py:26
  64.2 4.7 %all-to-all-start.5 = ((bf16[16,16,1024]{2,1,0:T(8,128)(2,1)}), bf16[16,16,1024]{2,1,0:T(8,128)(2,1)}, u32[]{:S(2)}, u32[]{:S(2)}) async-start(bf16[16,16,1024]{2,1,0:T(8,128)(2,1)} %bitcast.57), calls=%async_computation.5 | async-start | bytes 1048576 | tf_op jit(solution)/shard_map/all_to_all | solution.py:26
  68.9 0.0 collective-permute-done.11.received_hbm
  68.9 3.1 %shard_map.106 = (bf16[384,384]{1,0:T(8,128)(2,1)}, bf16[384,1024]{1,0:T(8,128)(2,1)}, bf16[128,1024]{1,0:T(8,128)(2,1)}) custom-call(bf16[8,32,1152]{2,1,0:T(8,128)(2,1)} %bitcast.55, bf16[8,32,1152]{2,1,0:T(8,128)(2,1)} %collective-permute-done.11.received_hbm, f32[8,128]{1,0:T(8,128)} %get-tuple-element.109.marks_hbm, ...), custom_call_target="tpu_custom_call" | custom-call | flops 301989888 | bytes 4231168 | tf_op jit(solution)/shard_map/pallas_call | solution.py:85
  72.0 1.3 collective-permute-start.14
  73.3 0.0 collective-permute-done.12._rows_hbm.other_rows_hbm
  73.3 4.1 %shard_map.107 = (f32[128,768]{1,0:T(8,128)}, bf16[400,768]{1,0:T(8,128)(2,1)}, bf16[128,1024]{1,0:T(8,128)(2,1)}, bf16[128,1024]{1,0:T(8,128)(2,1)}) custom-call(bf16[8,32,1152]{2,1,0:T(8,128)(2,1)} %bitcast.56, bf16[8,32,1152]{2,1,0:T(8,128)(2,1)} %collective-permute-done.11.received_hbm, f32[8,128]{1,0:T(8,128)} %get-tuple-element.109.marks_hbm, ...), custom_call_target="tpu_custom_call" | custom-call | flops 6000000000 | bytes 7073792 | tf_op jit(solution)/shard_map/pallas_call | solution.py:85
  77.4 0.3 collective-permute-start.13
  77.8 2.9 %collective-permute-done.14.remote_hbm = bf16[384,384]{1,0:T(8,128)(2,1)} collective-permute-done((bf16[384,384]{1,0:T(8,128)(2,1)}, bf16[384,384]{1,0:T(8,128)(2,1)}, u32[]{:S(2)}, u32[]{:S(2)}) %collective-permute-start.14) | collective-permute-done | bytes 294944 | tf_op jit(solution)/shard_map/ppermute | solution.py:22
  80.6 2.3 %all-to-all-done.5 = bf16[16,16,1024]{2,1,0:T(8,128)(2,1)} async-done(((bf16[16,16,1024]{2,1,0:T(8,128)(2,1)}), bf16[16,16,1024]{2,1,0:T(8,128)(2,1)}, u32[]{:S(2)}, u32[]{:S(2)}) %all-to-all-start.5) | async-done | bytes 524320 | tf_op jit(solution)/shard_map/all_to_all | solution.py:26
  82.9 5.7 %shard_map.108 = (bf16[384,2048]{1,0:T(8,128)(2,1)}, bf16[384,384]{1,0:T(8,128)(2,1)}, bf16[384,768]{1,0:T(8,128)(2,1)}, bf16[384,384]{1,0:T(8,128)(2,1)}, bf16[384,1024]{1,0:T(8,128)(2,1)}) custom-call(bf16[256,1024]{1,0:T(8,128)(2,1)} %bitcast.29.recv_hbm, bf16[128,1024]{1,0:T(8,128)(2,1)} %get-tuple-element.120.late_hbm, ...), custom_call_target="tpu_custom_call" | custom-call | flops 1207959552 | bytes 9732096 | tf_op jit(solution)/shard_map/pallas_call | solution.py:85
  88.6 1.3 collective-permute-start.15
  89.9 0.2 collective-permute-start.16
  90.1 6.0 %all-to-all-start.6 = ((bf16[16,24,2048]{2,1,0:T(8,128)(2,1)}), bf16[16,24,2048]{2,1,0:T(8,128)(2,1)}, u32[]{:S(2)}, u32[]{:S(2)}) async-start(bf16[16,24,2048]{2,1,0:T(8,128)(2,1)} %bitcast.52), calls=%async_computation.6 | async-start | bytes 3145728 | tf_op jit(solution)/shard_map/all_to_all | solution.py:26
  96.1 0.0 collective-permute-done.13.pre_hbm
  96.1 4.0 %collective-permute-done.15.hidden_hbm = bf16[384,384]{1,0:T(8,128)(2,1)} collective-permute-done((bf16[384,384]{1,0:T(8,128)(2,1)}, bf16[384,384]{1,0:T(8,128)(2,1)}, u32[]{:S(2)}, u32[]{:S(2)}) %collective-permute-start.15) | collective-permute-done | bytes 294944 | tf_op jit(solution)/shard_map/ppermute | solution.py:22
  100.1 3.7 %shard_map.109 = (bf16[384,1024]{1,0:T(8,128)(2,1)}, bf16[384,768]{1,0:T(8,128)(2,1)}) custom-call(bf16[400,768]{1,0:T(8,128)(2,1)} %collective-permute-done.13.pre_hbm, bf16[384,384]{1,0:T(8,128)(2,1)} %collective-permute-done.15.hidden_hbm, bf16[384,384]{1,0:T(8,128)(2,1)} %get-tuple-element.125.act_hbm, bf16[384,1024]{1,0:T(8,128)(2,1)} %get-tuple-element.126.grads_hbm, ...), custom_call_target="tpu_custom_call" | custom-call | flops 99999997952 | bytes 4153344 | tf_op jit(solution)/shard_map/pallas_call | solution.py:85
  103.8 1.9 %collective-permute-done.16.other_late_hbm = bf16[128,1024]{1,0:T(8,128)(2,1)} collective-permute-done((bf16[128,1024]{1,0:T(8,128)(2,1)}, bf16[128,1024]{1,0:T(8,128)(2,1)}, u32[]{:S(2)}, u32[]{:S(2)}) %collective-permute-start.16) | collective-permute-done | bytes 262176 | tf_op jit(solution)/shard_map/ppermute | solution.py:22
  105.7 1.2 collective-permute-start.17
  106.9 1.4 slice_reduce_fusion.1
  108.3 1.4 slice_reduce_fusion
  110.9 4.8 %shard_map.111 = (bf16[1024,384]{1,0:T(8,128)(2,1)}, bf16[1024,384]{1,0:T(8,128)(2,1)}) custom-call(bf16[256,2048]{1,0:T(8,128)(2,1)} %bitcast.17.rows_hbm, bf16[128,1024]{1,0:T(8,128)(2,1)} %get-tuple-element.133.late_rows_hbm, bf16[256,1024]{1,0:T(8,128)(2,1)} %collective-permute-done.12._rows_hbm.other_rows_hbm, ...), custom_call_target="tpu_custom_call" | custom-call | flops 1207959552 | bytes 4849664 | tf_op jit(solution)/shard_map/pallas_call | solution.py:85
  115.8 8.1 %collective-permute-done.17.other_hbm = bf16[384,1024]{1,0:T(8,128)(2,1)} collective-permute-done((bf16[384,1024]{1,0:T(8,128)(2,1)}, bf16[384,1024]{1,0:T(8,128)(2,1)}, u32[]{:S(2)}, u32[]{:S(2)}) %collective-permute-start.17) | collective-permute-done | bytes 786464 | tf_op jit(solution)/shard_map/ppermute | solution.py:22
  123.9 8.5 %all-to-all-done.6 = bf16[16,24,2048]{2,1,0:T(8,128)(2,1)} async-done(((bf16[16,24,2048]{2,1,0:T(8,128)(2,1)}), bf16[16,24,2048]{2,1,0:T(8,128)(2,1)}, u32[]{:S(2)}, u32[]{:S(2)}) %all-to-all-start.6) | async-done | bytes 1572896 | tf_op jit(solution)/shard_map/all_to_all | solution.py:26
  132.4 3.0 %shard_map.110 = (bf16[128,2048]{1,0:T(8,128)(2,1)}, bf16[384,2048]{1,0:T(8,128)(2,1)}) custom-call(bf16[384,128]{1,0:T(8,128)(2,1)} %get-tuple-element.118.place_hbm, bf16[384,2048]{1,0:T(8,128)(2,1)} %bitcast.31.returned_hbm, bf16[384,1024]{1,0:T(8,128)(2,1)} %get-tuple-element.131.own_hbm, bf16[384,1024]{1,0:T(8,128)(2,1)} %collective-permute-done.17.other_hbm), custom_call_target="tpu_custom_call" | custom-call | flops 201326592 | bytes 5341184 | tf_op jit(solution)/shard_map/pallas_call | solution.py:85
  (1 shorter events, 0.0 us)
Async XLA Ops:
  3.3 6.7 %copy-start.12 = (bf16[144,1024]{1,0:T(8,128)(2,1)S(1)}, bf16[144,1024]{1,0:T(8,128)(2,1)}, u32[]{:S(2)}) copy-start(bf16[144,1024]{1,0:T(8,128)(2,1)} %get-tuple-element.103) | copy-start | bytes 884740
  3.3 9.5 %copy-start.10 = (bf16[16,1152]{1,0:T(8,128)(2,1)S(1)}, bf16[16,1152]{1,0:T(8,128)(2,1)}, u32[]{:S(2)}) copy-start(bf16[16,1152]{1,0:T(8,128)(2,1)} %get-tuple-element.105) | copy-start | bytes 110596
  3.3 37.2 %all-to-all-start.3 = ((bf16[16,16,2048]{2,1,0:T(8,128)(2,1)}), bf16[16,16,2048]{2,1,0:T(8,128)(2,1)}, u32[]{:S(2)}, u32[]{:S(2)}) async-start(bf16[16,16,2048]{2,1,0:T(8,128)(2,1)} %bitcast.53), calls=%async_computation.3 | async-start | bytes 2097152 | tf_op jit(solution)/shard_map/all_to_all | solution.py:26
  10.0 8.4 %collective-permute-start.5 = (bf16[144,1024]{1,0:T(8,128)(2,1)S(1)}, bf16[144,1024]{1,0:T(8,128)(2,1)}, u32[]{:S(2)}, u32[]{:S(2)}) collective-permute-start(bf16[144,1024]{1,0:T(8,128)(2,1)S(1)} %copy-done.12), channel_id=1, source_target_pairs={{0,16},{16,0},{1,17},{17,1},{2,18},{18,2},{3,19},{19,3},{4,20},{20... | collective-permute-start | bytes 884744 | tf_op jit(solution)/shard_map/ppermute | solution.py:22
  11.3 29.3 %collective-permute-start.4 = (bf16[1024,384]{1,0:T(8,128)(2,1)}, bf16[1024,384]{1,0:T(8,128)(2,1)}, u32[]{:S(2)}, u32[]{:S(2)}) collective-permute-start(bf16[1024,384]{1,0:T(8,128)(2,1)} %bitcast.18.gate_hbm), channel_id=1, source_target_pairs={{0,16},{16,0},{1,17},{17,1},{2,18},{18,2},{3,19},{19,3},{4,20},{20... | collective-permute-start | bytes 2359304 | tf_op jit(solution)/shard_map/ppermute | solution.py:22
  11.6 40.6 %collective-permute-start.10 = (bf16[1024,384]{1,0:T(8,128)(2,1)}, bf16[1024,384]{1,0:T(8,128)(2,1)}, u32[]{:S(2)}, u32[]{:S(2)}) collective-permute-start(bf16[1024,384]{1,0:T(8,128)(2,1)} %bitcast.23.up_hbm), channel_id=1, source_target_pairs={{0,16},{16,0},{1,17},{17,1},{2,18},{18,2},{3,19},{19,3},{4,20},{20... | collective-permute-start | bytes 2359304 | tf_op jit(solution)/shard_map/ppermute | solution.py:22
  22.4 17.2 %collective-permute-start.8 = (bf16[32,1152]{1,0:T(8,128)(2,1)}, bf16[32,1152]{1,0:T(8,128)(2,1)S(1)}, u32[]{:S(2)}, u32[]{:S(2)}) collective-permute-start(bf16[32,1152]{1,0:T(8,128)(2,1)} %constant_dynamic-update-slice_fusion), channel_id=1, source_target_pairs={{0,12},{1,13},{2,14},{3,15},{4,8},{5,9},{6,10},{7,11},{8,4},{9,5},... | collective-permute-start | bytes 221192 | tf_op jit(solution)/shard_map/ppermute | solution.py:604
  23.6 16.0 %collective-permute-start.7 = (bf16[32,1152]{1,0:T(8,128)(2,1)}, bf16[32,1152]{1,0:T(8,128)(2,1)S(1)}, u32[]{:S(2)}, u32[]{:S(2)}) collective-permute-start(bf16[32,1152]{1,0:T(8,128)(2,1)} %constant_dynamic-update-slice_fusion), channel_id=1, source_target_pairs={{0,8},{1,9},{2,10},{3,11},{4,12},{5,13},{6,14},{7,15},{8,0},{9,1},... | collective-permute-start | bytes 221192 | tf_op jit(solution)/shard_map/ppermute | solution.py:604
  24.8 14.8 %collective-permute-start.6 = (bf16[32,1152]{1,0:T(8,128)(2,1)}, bf16[32,1152]{1,0:T(8,128)(2,1)S(1)}, u32[]{:S(2)}, u32[]{:S(2)}) collective-permute-start(bf16[32,1152]{1,0:T(8,128)(2,1)} %constant_dynamic-update-slice_fusion), channel_id=1, source_target_pairs={{0,4},{1,5},{2,6},{3,7},{4,0},{5,1},{6,2},{7,3},{8,12},{9,13},{10,... | collective-permute-start | bytes 221192 | tf_op jit(solution)/shard_map/ppermute | solution.py:604
  40.5 0.7 copy-start.9
  41.3 10.9 %collective-permute-start.9 = (bf16[4,32,1152]{2,1,0:T(8,128)(2,1)S(1)}, bf16[4,32,1152]{2,1,0:T(8,128)(2,1)}, u32[]{:S(2)}, u32[]{:S(2)}) collective-permute-start(bf16[4,32,1152]{2,1,0:T(8,128)(2,1)S(1)} %pad_maximum_fusion.7.pool_hbm), channel_id=1, source_target_pairs={{0,2},{1,3},{2,0},{3,1},{4,6},{5,7},{6,4},{7,5},{8,10},{9,11},{10,... | collective-permute-start | bytes 884744 | tf_op jit(solution)/shard_map/ppermute | solution.py:604
  41.5 22.7 %all-to-all-start.4 = ((bf16[16,16,1024]{2,1,0:T(8,128)(2,1)}), bf16[16,16,1024]{2,1,0:T(8,128)(2,1)}, u32[]{:S(2)}, u32[]{:S(2)}) async-start(bf16[16,16,1024]{2,1,0:T(8,128)(2,1)} %bitcast.58), calls=%async_computation.4 | async-start | bytes 1048576 | tf_op jit(solution)/shard_map/all_to_all | solution.py:26
  54.0 14.8 %collective-permute-start.11 = (bf16[8,32,1152]{2,1,0:T(8,128)(2,1)}, bf16[8,32,1152]{2,1,0:T(8,128)(2,1)}, u32[]{:S(2)}, u32[]{:S(2)}) collective-permute-start(bf16[8,32,1152]{2,1,0:T(8,128)(2,1)} %bitcast.54), channel_id=1, source_target_pairs={{0,1},{1,0},{2,3},{3,2},{4,5},{5,4},{6,7},{7,6},{8,9},{9,8},{10,11... | collective-permute-start | bytes 1769480 | tf_op jit(solution)/shard_map/ppermute | solution.py:604
  57.1 16.1 %collective-permute-start.12 = (bf16[256,1024]{1,0:T(8,128)(2,1)}, bf16[256,1024]{1,0:T(8,128)(2,1)}, u32[]{:S(2)}, u32[]{:S(2)}) collective-permute-start(bf16[256,1024]{1,0:T(8,128)(2,1)} %slice.21), channel_id=1, source_target_pairs={{0,16},{16,0},{1,17},{17,1},{2,18},{18,2},{3,19},{19,3},{4,20},{20... | collective-permute-start | bytes 1572872 | tf_op jit(solution)/shard_map/ppermute | solution.py:22
  64.2 18.7 %all-to-all-start.5 = ((bf16[16,16,1024]{2,1,0:T(8,128)(2,1)}), bf16[16,16,1024]{2,1,0:T(8,128)(2,1)}, u32[]{:S(2)}, u32[]{:S(2)}) async-start(bf16[16,16,1024]{2,1,0:T(8,128)(2,1)} %bitcast.57), calls=%async_computation.5 | async-start | bytes 1048576 | tf_op jit(solution)/shard_map/all_to_all | solution.py:26
  72.0 8.6 %collective-permute-start.14 = (bf16[384,384]{1,0:T(8,128)(2,1)}, bf16[384,384]{1,0:T(8,128)(2,1)}, u32[]{:S(2)}, u32[]{:S(2)}) collective-permute-start(bf16[384,384]{1,0:T(8,128)(2,1)} %get-tuple-element.116._hidden_hbm), channel_id=1, source_target_pairs={{0,16},{16,0},{1,17},{17,1},{2,18},{18,2},{3,19},{19,3},{4,20},{20... | collective-permute-start | bytes 884744 | tf_op jit(solution)/shard_map/ppermute | solution.py:22
  77.4 18.7 %collective-permute-start.13 = (bf16[400,768]{1,0:T(8,128)(2,1)}, bf16[400,768]{1,0:T(8,128)(2,1)}, u32[]{:S(2)}, u32[]{:S(2)}) collective-permute-start(bf16[400,768]{1,0:T(8,128)(2,1)} %get-tuple-element.117), channel_id=1, source_target_pairs={{0,16},{16,0},{1,17},{17,1},{2,18},{18,2},{3,19},{19,3},{4,20},{20... | collective-permute-start | bytes 1843208 | tf_op jit(solution)/shard_map/ppermute | solution.py:22
  88.6 11.5 %collective-permute-start.15 = (bf16[384,384]{1,0:T(8,128)(2,1)}, bf16[384,384]{1,0:T(8,128)(2,1)}, u32[]{:S(2)}, u32[]{:S(2)}) collective-permute-start(bf16[384,384]{1,0:T(8,128)(2,1)} %get-tuple-element.124), channel_id=1, source_target_pairs={{0,16},{16,0},{1,17},{17,1},{2,18},{18,2},{3,19},{19,3},{4,20},{20... | collective-permute-start | bytes 884744 | tf_op jit(solution)/shard_map/ppermute | solution.py:22
  89.9 15.9 %collective-permute-start.16 = (bf16[128,1024]{1,0:T(8,128)(2,1)}, bf16[128,1024]{1,0:T(8,128)(2,1)}, u32[]{:S(2)}, u32[]{:S(2)}) collective-permute-start(bf16[128,1024]{1,0:T(8,128)(2,1)} %get-tuple-element.130), channel_id=1, source_target_pairs={{0,16},{16,0},{1,17},{17,1},{2,18},{18,2},{3,19},{19,3},{4,20},{20... | collective-permute-start | bytes 786440 | tf_op jit(solution)/shard_map/ppermute | solution.py:22
  90.1 42.3 %all-to-all-start.6 = ((bf16[16,24,2048]{2,1,0:T(8,128)(2,1)}), bf16[16,24,2048]{2,1,0:T(8,128)(2,1)}, u32[]{:S(2)}, u32[]{:S(2)}) async-start(bf16[16,24,2048]{2,1,0:T(8,128)(2,1)} %bitcast.52), calls=%async_computation.6 | async-start | bytes 3145728 | tf_op jit(solution)/shard_map/all_to_all | solution.py:26
  105.7 18.2 %collective-permute-start.17 = (bf16[384,1024]{1,0:T(8,128)(2,1)}, bf16[384,1024]{1,0:T(8,128)(2,1)}, u32[]{:S(2)}, u32[]{:S(2)}) collective-permute-start(bf16[384,1024]{1,0:T(8,128)(2,1)} %get-tuple-element.131.own_hbm), channel_id=1, source_target_pairs={{0,16},{16,0},{1,17},{17,1},{2,18},{18,2},{3,19},{19,3},{4,20},{20... | collective-permute-start | bytes 2359304 | tf_op jit(solution)/shard_map/ppermute | solution.py:22
